TPU v7x, 32 devices: a whole 2x2x4 slice. The times are simulated.
32 devices in a mesh: batch: 2 (over x), seq: 4 (over y, core), head: 4 (over z).
Axes of the slice: x: 2, y: 2, z: 4, core: 2. Of those that a mesh axis runs over, the one named last changes fastest.
Arguments:
- inputs: bfloat16 [16, 1024, 1024], P('batch', ('seq', 'head')), may hold values from -6 to 6
- memory: bfloat16 [16, 1024, 1024], P('batch', ('seq', 'head')), may hold values from -6 to 6
- cotangent: bfloat16 [16, 1024, 1024], P('batch', ('seq', 'head')), may hold values from -6 to 6
- tgt_lengths: int32 [16, 16], P('batch'), may hold values from 1 to 1009, as said below
- src_ids: int32 [16, 1024], P('batch'), may hold values from 0 to 15, as said below
- gain_one: float32 [1024], replicated, may hold values from 0.5 to 1.5
- w_query: bfloat16 [1024, 1024], P(None, 'head'), may hold values from -0.1875 to 0.1875
- w_key: bfloat16 [1024, 1024], P(None, 'head'), may hold values from -0.1875 to 0.1875
- w_value: bfloat16 [1024, 1024], P(None, 'head'), may hold values from -0.1875 to 0.1875
- w_out: bfloat16 [1024, 1024], P('head'), may hold values from -0.75 to 0.75
- gain_two: float32 [1024], replicated, may hold values from 0.5 to 1.5
- w_cross_query: bfloat16 [1024, 1024], P(None, 'head'), may hold values from -0.1875 to 0.1875
- w_mem_key: bfloat16 [1024, 1024], P(None, 'head'), may hold values from -0.1875 to 0.1875
- w_mem_value: bfloat16 [1024, 1024], P(None, 'head'), may hold values from -0.1875 to 0.1875
- w_cross_out: bfloat16 [1024, 1024], P('head'), may hold values from -0.75 to 0.75
- gain_three: float32 [1024], replicated, may hold values from 0.5 to 1.5
- w_up: bfloat16 [1024, 4096], P(None, 'head'), may hold values from -0.1875 to 0.1875
- w_down: bfloat16 [4096, 1024], P('head'), may hold values from -0.09375 to 0.09375
Outputs:
- output: bfloat16 [16, 1024, 1024], P('batch', ('seq', 'head'))
- grad_inputs: float32 [16, 1024, 1024], P('batch', ('seq', 'head'))
- grad_memory: float32 [16, 1024, 1024], P('batch', ('seq', 'head'))
- grad_gain_one: float32 [1024], replicated
- grad_w_query: float32 [1024, 1024], P(None, 'head')
- grad_w_key: float32 [1024, 1024], P(None, 'head')
- grad_w_value: float32 [1024, 1024], P(None, 'head')
- grad_w_out: float32 [1024, 1024], P('head')
- grad_gain_two: float32 [1024], replicated
- grad_w_cross_query: float32 [1024, 1024], P(None, 'head')
- grad_w_mem_key: float32 [1024, 1024], P(None, 'head')
- grad_w_mem_value: float32 [1024, 1024], P(None, 'head')
- grad_w_cross_out: float32 [1024, 1024], P('head')
- grad_gain_three: float32 [1024], replicated
- grad_w_up: float32 [1024, 4096], P(None, 'head')
- grad_w_down: float32 [4096, 1024], P('head')
Inputs may be any that keep to these rules, and one draw needn't show every extreme that they name: `tgt_lengths`: each row's lengths are positive and add up to 1024. `src_ids`: non-decreasing along each row; every value from 0 to 15 occurs in every row.
All inputs are finite; a program needn't handle non-finite values.
Results may differ from a plain program's by a relative error of at most 0.02.
Values may be sent and summed in bfloat16 or wider, within the bound.
No kernel may reach another device: no remote copies, remote signals or barrier semaphores. Data moves between devices by JAX's collectives and lax.ppermute only.
A program may use at most 512 MiB of HBM per device.

v0:
```python
import jax
import jax.numpy as jnp
from jax import lax
from jax.sharding import PartitionSpec as P

HEAD_DIM = 64
LEN = 1024


EPSILON = 1e-05
MASKED = -1000000000.0


def normalize(activity, gain_vector):
    centre = jnp.mean(activity, -1, keepdims=True)
    shifted = activity - centre
    variance = jnp.mean(shifted * shifted, -1, keepdims=True)
    return shifted * lax.rsqrt(variance + EPSILON) * gain_vector


def smooth_gate(pre_act):
    return jax.nn.gelu(pre_act, approximate=True)


def segment_ids(lengths, total_len):
    segment_ends = jnp.cumsum(lengths, -1)[:, :-1]
    positions = jnp.arange(total_len, dtype=jnp.int32)
    return jnp.sum((positions[None, :, None] >= segment_ends[:, None, :]).astype(jnp.int32), -1)


def project(token_rows, matrix):
    return jnp.einsum("rtd,de->rte", token_rows, matrix, preferred_element_type=jnp.float32)


def project_back(grad_rows, matrix):
    return jnp.einsum("rte,de->rtd", grad_rows, matrix, preferred_element_type=jnp.float32)


def weight_grad(token_rows, grad_rows):
    return jnp.einsum("rtd,rte->de", token_rows, grad_rows, preferred_element_type=jnp.float32)


def spread(token_rows):
    return lax.all_gather(token_rows, "head", axis=1, tiled=True)


def collect(partial_rows):
    return lax.psum_scatter(partial_rows, "head", scatter_dimension=1, tiled=True)


def split_heads(matrix, head_count):
    return matrix.reshape(matrix.shape[:2] + (head_count, matrix.shape[2] // head_count))


def permitted(query_ids, key_ids, first_pos, causal):
    allowed = query_ids[:, :, None] == key_ids[:, None, :]
    if causal:
        query_pos = first_pos + jnp.arange(query_ids.shape[1], dtype=jnp.int32)
        key_pos = jnp.arange(key_ids.shape[1], dtype=jnp.int32)
        allowed = allowed & (key_pos[None, None, :] <= query_pos[None, :, None])
    return allowed


def softmax_of(queries, key_rows, allowed, head_count):
    query_four = split_heads(queries, head_count)
    key_four = split_heads(key_rows, head_count)
    scaling = query_four.shape[3] ** (-0.5)
    scores = (
        jnp.einsum("gqhe,gkhe->ghqk", query_four, key_four, preferred_element_type=jnp.float32)
        * scaling
    )
    scores = jnp.where(allowed[:, None], scores, MASKED)
    highest = jnp.max(scores, -1, keepdims=True)
    weights = jnp.exp(scores - highest)
    return weights / jnp.sum(weights, -1, keepdims=True)


def attend_block(queries, key_rows, value_rows, allowed, head_count):
    chances = softmax_of(queries, key_rows, allowed, head_count)
    mixed = jnp.einsum(
        "ghqk,gkhe->gqhe",
        chances.astype(jnp.bfloat16),
        split_heads(value_rows, head_count),
        preferred_element_type=jnp.float32,
    )
    return mixed.reshape(queries.shape).astype(jnp.bfloat16)


def attend_back(queries, key_rows, value_rows, allowed, head_count, grad_mixed):
    chances = softmax_of(queries, key_rows, allowed, head_count)
    query_four = split_heads(queries, head_count)
    key_four = split_heads(key_rows, head_count)
    value_four = split_heads(value_rows, head_count)
    grad_four = split_heads(grad_mixed, head_count)
    grad_chances = jnp.einsum(
        "gqhe,gkhe->ghqk", grad_four, value_four, preferred_element_type=jnp.float32
    )
    inner = jnp.sum(chances * grad_chances, -1, keepdims=True)
    grad_scores = (chances * (grad_chances - inner)).astype(jnp.bfloat16)
    scaling = query_four.shape[3] ** (-0.5)
    grad_query = (
        jnp.einsum("ghqk,gkhe->gqhe", grad_scores, key_four, preferred_element_type=jnp.float32)
        * scaling
    )
    grad_key = (
        jnp.einsum("ghqk,gqhe->gkhe", grad_scores, query_four, preferred_element_type=jnp.float32)
        * scaling
    )
    grad_value = jnp.einsum(
        "ghqk,gqhe->gkhe",
        chances.astype(jnp.bfloat16),
        grad_four,
        preferred_element_type=jnp.float32,
    )
    return (
        grad_query.reshape(queries.shape),
        grad_key.reshape(key_rows.shape),
        grad_value.reshape(value_rows.shape),
    )


def group_size(row_count, length):
    group_rows = max(1, min(row_count, 512 // length))
    while row_count % group_rows:
        group_rows -= 1
    return group_rows


def grouped(function, members, group_rows):
    stacked = tuple(
        (
            member.reshape((member.shape[0] // group_rows, group_rows) + member.shape[1:])
            for member in members
        )
    )
    result = lax.map(lambda block_items: function(*block_items), stacked)
    return jax.tree.map(lambda blocked: blocked.reshape((-1,) + blocked.shape[2:]), result)


def keyed_attend(queries, key_all, value_all, query_ids, key_ids, first_pos, causal, head_count):
    group_rows = group_size(queries.shape[0], queries.shape[1])

    def one_block(query_part, key_part, value_part, qid_part, kid_part):
        allowed = permitted(qid_part, kid_part, first_pos, causal)
        return attend_block(query_part, key_part, value_part, allowed, head_count)

    return grouped(one_block, (queries, key_all, value_all, query_ids, key_ids), group_rows)


def keyed_back(
    queries, key_all, value_all, query_ids, key_ids, first_pos, causal, head_count, grad_mixed
):
    group_rows = group_size(queries.shape[0], queries.shape[1])

    def one_block(query_part, key_part, value_part, qid_part, kid_part, grad_part):
        allowed = permitted(qid_part, kid_part, first_pos, causal)
        return attend_back(query_part, key_part, value_part, allowed, head_count, grad_part)

    return grouped(
        one_block, (queries, key_all, value_all, query_ids, key_ids, grad_mixed), group_rows
    )


def body(
    inputs,
    memory,
    cotangent,
    tgt_lengths,
    src_ids,
    gain_one,
    w_query,
    w_key,
    w_value,
    w_out,
    gain_two,
    w_cross_query,
    w_mem_key,
    w_mem_value,
    w_cross_out,
    gain_three,
    w_up,
    w_down,
):
    bf_type = jnp.bfloat16
    head_count = w_query.shape[1] // HEAD_DIM
    seq_count = lax.axis_size("seq")
    seq_index = lax.axis_index("seq")
    row_span = LEN // seq_count
    first_pos = seq_index * row_span
    target_ids = segment_ids(tgt_lengths, LEN)
    query_ids = lax.dynamic_slice_in_dim(target_ids, first_pos, row_span, 1)
    residual = inputs.astype(jnp.float32)
    first_spread = spread(normalize(residual, gain_one).astype(bf_type))
    memory_spread = spread(memory)
    queries = project(first_spread, w_query).astype(bf_type)
    key_rows = project(first_spread, w_key).astype(bf_type)
    value_rows = project(first_spread, w_value).astype(bf_type)
    mem_keys = project(memory_spread, w_mem_key).astype(bf_type)
    mem_values = project(memory_spread, w_mem_value).astype(bf_type)
    key_all, value_all, mem_key_all, mem_value_all = (
        lax.all_gather(key_rows, "seq", axis=1, tiled=True),
        lax.all_gather(value_rows, "seq", axis=1, tiled=True),
        lax.all_gather(mem_keys, "seq", axis=1, tiled=True),
        lax.all_gather(mem_values, "seq", axis=1, tiled=True),
    )
    self_mixed = keyed_attend(
        queries, key_all, value_all, query_ids, target_ids, first_pos, True, head_count
    )
    after_self = residual + collect(project(self_mixed, w_out))
    second_spread = spread(normalize(after_self, gain_two).astype(bf_type))
    cross_queries = project(second_spread, w_cross_query).astype(bf_type)
    cross_mixed = keyed_attend(
        cross_queries, mem_key_all, mem_value_all, query_ids, src_ids, first_pos, False, head_count
    )
    after_cross = after_self + collect(project(cross_mixed, w_cross_out))
    third_spread = spread(normalize(after_cross, gain_three).astype(bf_type))
    hidden_pre = project(third_spread, w_up)
    hidden_act = smooth_gate(hidden_pre).astype(bf_type)
    output = (after_cross + collect(project(hidden_act, w_down))).astype(bf_type)
    ffn_grad_spread = spread(cotangent)
    grad_w_down = weight_grad(hidden_act, ffn_grad_spread)
    grad_act = project_back(ffn_grad_spread, w_down)
    gate_value, gate_pull = jax.vjp(smooth_gate, hidden_pre)
    grad_pre = gate_pull(grad_act)[0].astype(bf_type)
    grad_w_up = weight_grad(third_spread, grad_pre)
    third_back = collect(project_back(grad_pre, w_up))
    norm_value, norm_pull = jax.vjp(normalize, after_cross, gain_three)
    grad_cross_in, grad_gain_three = norm_pull(third_back)
    grad_after_cross = cotangent.astype(jnp.float32) + grad_cross_in
    cross_grad_spread = spread(grad_after_cross.astype(bf_type))
    grad_w_cross_out = weight_grad(cross_mixed, cross_grad_spread)
    grad_cross_mixed = project_back(cross_grad_spread, w_cross_out).astype(bf_type)
    part_query, part_mem_key, part_mem_value = keyed_back(
        cross_queries,
        mem_key_all,
        mem_value_all,
        query_ids,
        src_ids,
        first_pos,
        False,
        head_count,
        grad_cross_mixed,
    )
    summed_key, summed_value = (
        lax.psum_scatter(
            part_mem_key.astype(jnp.bfloat16), "seq", scatter_dimension=1, tiled=True
        ).astype(jnp.float32),
        lax.psum_scatter(
            part_mem_value.astype(jnp.bfloat16), "seq", scatter_dimension=1, tiled=True
        ).astype(jnp.float32),
    )
    grad_cross_queries = part_query.astype(bf_type)
    grad_mem_keys = summed_key.astype(bf_type)
    grad_mem_values = summed_value.astype(bf_type)
    grad_w_cross_query = weight_grad(second_spread, grad_cross_queries)
    grad_w_mem_key = weight_grad(memory_spread, grad_mem_keys)
    grad_w_mem_value = weight_grad(memory_spread, grad_mem_values)
    second_back = collect(project_back(grad_cross_queries, w_cross_query))
    grad_memory = collect(
        project_back(grad_mem_keys, w_mem_key) + project_back(grad_mem_values, w_mem_value)
    )
    norm_value, norm_pull = jax.vjp(normalize, after_self, gain_two)
    grad_self_in, grad_gain_two = norm_pull(second_back)
    grad_after_self = grad_after_cross + grad_self_in
    self_grad_spread = spread(grad_after_self.astype(bf_type))
    grad_w_out = weight_grad(self_mixed, self_grad_spread)
    grad_self_mixed = project_back(self_grad_spread, w_out).astype(bf_type)
    part_query, part_key, part_value = keyed_back(
        queries,
        key_all,
        value_all,
        query_ids,
        target_ids,
        first_pos,
        True,
        head_count,
        grad_self_mixed,
    )
    summed_key, summed_value = (
        lax.psum_scatter(
            part_key.astype(jnp.bfloat16), "seq", scatter_dimension=1, tiled=True
        ).astype(jnp.float32),
        lax.psum_scatter(
            part_value.astype(jnp.bfloat16), "seq", scatter_dimension=1, tiled=True
        ).astype(jnp.float32),
    )
    grad_queries = part_query.astype(bf_type)
    grad_keys = summed_key.astype(bf_type)
    grad_values = summed_value.astype(bf_type)
    grad_w_query = weight_grad(first_spread, grad_queries)
    grad_w_key = weight_grad(first_spread, grad_keys)
    grad_w_value = weight_grad(first_spread, grad_values)
    first_back = collect(
        project_back(grad_queries, w_query)
        + project_back(grad_keys, w_key)
        + project_back(grad_values, w_value)
    )
    norm_value, norm_pull = jax.vjp(normalize, residual, gain_one)
    grad_input_in, grad_gain_one = norm_pull(first_back)
    grad_inputs = grad_after_self + grad_input_in
    summed = (
        lax.psum(grad_w_query.astype(jnp.bfloat16), ("batch", "seq")).astype(jnp.float32),
        lax.psum(grad_w_key.astype(jnp.bfloat16), ("batch", "seq")).astype(jnp.float32),
        lax.psum(grad_w_value.astype(jnp.bfloat16), ("batch", "seq")).astype(jnp.float32),
        lax.psum(grad_w_out.astype(jnp.bfloat16), ("batch", "seq")).astype(jnp.float32),
        lax.psum(grad_w_cross_query.astype(jnp.bfloat16), ("batch", "seq")).astype(jnp.float32),
        lax.psum(grad_w_mem_key.astype(jnp.bfloat16), ("batch", "seq")).astype(jnp.float32),
        lax.psum(grad_w_mem_value.astype(jnp.bfloat16), ("batch", "seq")).astype(jnp.float32),
        lax.psum(grad_w_cross_out.astype(jnp.bfloat16), ("batch", "seq")).astype(jnp.float32),
        lax.psum(grad_w_up.astype(jnp.bfloat16), ("batch", "seq")).astype(jnp.float32),
        lax.psum(grad_w_down.astype(jnp.bfloat16), ("batch", "seq")).astype(jnp.float32),
    )
    gains = lax.psum((grad_gain_one, grad_gain_two, grad_gain_three), ("batch", "seq", "head"))
    return (
        output,
        grad_inputs,
        grad_memory,
        gains[0],
        summed[0],
        summed[1],
        summed[2],
        summed[3],
        gains[1],
        summed[4],
        summed[5],
        summed[6],
        summed[7],
        gains[2],
        summed[8],
        summed[9],
    )


def solution(mesh):
    placed = (
        P("batch", ("seq", "head"), None),
        P("batch", ("seq", "head"), None),
        P("batch", ("seq", "head"), None),
        P("batch", None),
        P("batch", None),
        P(),
        P(None, "head"),
        P(None, "head"),
        P(None, "head"),
        P("head", None),
        P(),
        P(None, "head"),
        P(None, "head"),
        P(None, "head"),
        P("head", None),
        P(),
        P(None, "head"),
        P("head", None),
    )
    return jax.shard_map(
        body,
        mesh=mesh,
        in_specs=placed,
        out_specs=(
            P("batch", ("seq", "head"), None),
            P("batch", ("seq", "head"), None),
            P("batch", ("seq", "head"), None),
            P(),
            P(None, "head"),
            P(None, "head"),
            P(None, "head"),
            P("head", None),
            P(),
            P(None, "head"),
            P(None, "head"),
            P(None, "head"),
            P("head", None),
            P(),
            P(None, "head"),
            P("head", None),
        ),
        check_vma=False,
    )
```

profile of v0, /device:TPU:1, one launch (start us, length us, event | category | flops | bytes accessed | tf_op | source)
XLA Modules:
  0.0 2353.3 jit_solution(7405527113216655735)
XLA Ops:
  14.4 82.9 %all-gather.12.cloned.1.call-done = bf16[8,256,1024]{2,1,0:T(8,128)(2,1)} async-done(((bf16[8,64,1024]{2,1,0:T(8,128)(2,1)}), bf16[8,256,1024]{2,1,0:T(8,128)(2,1)}) %all-gather.12.cloned.1.call-update) | async-done | bytes 4194320 | tf_op jit(solution)/shard_map/all_gather | solution.py:44
  113.0 22.4 all-gather.16.cloned.1.call-done
  141.5 30.5 %all-gather.14.cloned.1.call-done = bf16[8,1024,256]{2,1,0:T(8,128)(2,1)} async-done(((bf16[8,256,256]{2,1,0:T(8,128)(2,1)}), bf16[8,1024,256]{2,1,0:T(8,128)(2,1)}) %all-gather.14.cloned.1.call-update) | async-done | bytes 4194320 | tf_op jit(solution)/shard_map/all_gather | solution.py:202
  179.2 74.4 %while.48 = (s32[]{:T(128)}, bf16[4,2,256,256]{2,3,1,0:T(8,128)(2,1)}, bf16[4,2,1024,256]{2,3,1,0:T(8,128)(2,1)}, s32[4,2,256]{2,1,0:T(2,128)S(1)}, s32[4,2,1024...) while((s32[]{:T(128)}, ...), condition=%wide.region_7.8_spmd, body=%wide.region_4.7_spmd.sunk | while | flops 550896896 | bytes 26263676 | solution.py:136
  203.2 7.8 fusion.225
  221.8 7.8 fusion.225
  270.5 133.3 %reduce-scatter.12.cloned.1.call-done = f32[8,64,1024]{2,1,0:T(8,128)} async-done(((f32[8,256,1024]{2,1,0:T(8,128)}), f32[8,64,1024]{2,1,0:T(8,128)}) %reduce-scatter.12.cloned.1.call-update) | async-done | bytes 2097168 | tf_op jit(solution)/shard_map/reduce_scatter | solution.py:48
  408.7 33.0 %all-gather.24.cloned.1.call-done = bf16[8,1024,256]{2,1,0:T(8,128)(2,1)} async-done(((bf16[8,256,256]{2,1,0:T(8,128)(2,1)}), bf16[8,1024,256]{2,1,0:T(8,128)(2,1)}) %all-gather.24.cloned.1.call-update) | async-done | bytes 4194320 | tf_op jit(solution)/shard_map/all_gather | solution.py:203
  448.0 30.4 %all-gather.20.cloned.1.call-done = bf16[8,1024,256]{2,1,0:T(8,128)(2,1)} async-done(((bf16[8,256,256]{2,1,0:T(8,128)(2,1)}), bf16[8,1024,256]{2,1,0:T(8,128)(2,1)}) %all-gather.20.cloned.1.call-update) | async-done | bytes 4194320 | tf_op jit(solution)/shard_map/all_gather | solution.py:204
  484.6 76.2 %all-gather.22.cloned.1.call-done = bf16[8,256,1024]{2,1,0:T(8,128)(2,1)} async-done(((bf16[8,64,1024]{2,1,0:T(8,128)(2,1)}), bf16[8,256,1024]{2,1,0:T(8,128)(2,1)}) %all-gather.22.cloned.1.call-update) | async-done | bytes 4194320 | tf_op jit(solution)/shard_map/all_gather | solution.py:44
  566.8 72.9 %while.49 = (s32[]{:T(128)}, bf16[4,2,256,256]{2,3,1,0:T(8,128)(2,1)}, bf16[4,2,1024,256]{2,3,1,0:T(8,128)(2,1)}, s32[4,2,256]{2,1,0:T(2,128)S(1)}, s32[4,2,1024...) while((s32[]{:T(128)}, ...), condition=%wide.region_14.15_spmd, body=%wide.region_11.14_spmd.sunk | while | flops 550110208 | bytes 25737328 | solution.py:136
  589.9 7.8 fusion.230
  645.7 142.9 %reduce-scatter.14.cloned.1.call-done = f32[8,64,1024]{2,1,0:T(8,128)} async-done(((f32[8,256,1024]{2,1,0:T(8,128)}), f32[8,64,1024]{2,1,0:T(8,128)}) %reduce-scatter.14.cloned.1.call-update) | async-done | bytes 2097168 | tf_op jit(solution)/shard_map/reduce_scatter | solution.py:48
  795.0 80.6 %all-gather.26.cloned.1.call-done = bf16[8,256,1024]{2,1,0:T(8,128)(2,1)} async-done(((bf16[8,64,1024]{2,1,0:T(8,128)(2,1)}), bf16[8,256,1024]{2,1,0:T(8,128)(2,1)}) %all-gather.26.cloned.1.call-update) | async-done | bytes 4194320 | tf_op jit(solution)/shard_map/all_gather | solution.py:44
  875.6 9.0 fusion.68
  884.6 71.9 %all-gather.28.cloned.1.call-done = bf16[8,256,1024]{2,1,0:T(8,128)(2,1)} async-done(((bf16[8,64,1024]{2,1,0:T(8,128)(2,1)}), bf16[8,256,1024]{2,1,0:T(8,128)(2,1)}) %all-gather.28.cloned.1.call-update) | async-done | bytes 4194320 | tf_op jit(solution)/shard_map/all_gather | solution.py:44
  956.5 12.5 fusion.52
  979.6 12.0 fusion.64
  991.6 129.3 %reduce-scatter.18.cloned.1.call-done = f32[8,64,1024]{2,1,0:T(8,128)} async-done(((f32[8,256,1024]{2,1,0:T(8,128)}), f32[8,64,1024]{2,1,0:T(8,128)}) %reduce-scatter.18.cloned.1.call-update) | async-done | bytes 2097168 | tf_op jit(solution)/shard_map/reduce_scatter | solution.py:48
  1123.9 144.7 %reduce-scatter.16.cloned.1.call-done = f32[8,64,1024]{2,1,0:T(8,128)} async-done(((f32[8,256,1024]{2,1,0:T(8,128)}), f32[8,64,1024]{2,1,0:T(8,128)}) %reduce-scatter.16.cloned.1.call-update) | async-done | bytes 2097168 | tf_op jit(solution)/shard_map/reduce_scatter | solution.py:48
  1275.4 81.6 %all-gather.30.cloned.1.call-done = bf16[8,256,1024]{2,1,0:T(8,128)(2,1)} async-done(((bf16[8,64,1024]{2,1,0:T(8,128)(2,1)}), bf16[8,256,1024]{2,1,0:T(8,128)(2,1)}) %all-gather.30.cloned.1.call-update) | async-done | bytes 4194320 | tf_op jit(solution)/shard_map/all_gather | solution.py:44
  1367.5 100.3 %while.50 = (s32[]{:T(128)}, bf16[4,2,256,256]{2,3,1,0:T(8,128)(2,1)}, bf16[4,2,1024,256]{2,3,1,0:T(8,128)(2,1)}, bf16[4,2,1024,256]{2,3,1,0:T(8,128)(2,1)}, bf1...) while((s32[]{:T(128)}, ...), condition=%wide.region_26.27_spmd, body=%wide.region_22.26_spmd.sunk | while | flops 1371274240 | bytes 115685568 | solution.py:136
  1473.8 142.9 %reduce-scatter.20.cloned.1.call-done = f32[8,64,1024]{2,1,0:T(8,128)} async-done(((f32[8,256,1024]{2,1,0:T(8,128)}), f32[8,64,1024]{2,1,0:T(8,128)}) %reduce-scatter.20.cloned.1.call-update) | async-done | bytes 2097168 | tf_op jit(solution)/shard_map/reduce_scatter | solution.py:48
  1624.4 80.2 %all-gather.32.cloned.1.call-done = bf16[8,256,1024]{2,1,0:T(8,128)(2,1)} async-done(((bf16[8,64,1024]{2,1,0:T(8,128)(2,1)}), bf16[8,256,1024]{2,1,0:T(8,128)(2,1)}) %all-gather.32.cloned.1.call-update) | async-done | bytes 4194320 | tf_op jit(solution)/shard_map/all_gather | solution.py:44
  1714.5 100.9 %while.51 = (s32[]{:T(128)}, bf16[4,2,256,256]{2,3,1,0:T(8,128)(2,1)}, bf16[4,2,1024,256]{2,3,1,0:T(8,128)(2,1)}, bf16[4,2,1024,256]{2,3,1,0:T(8,128)(2,1)}, bf1...) while((s32[]{:T(128)}, ...), condition=%wide.region_34.35_spmd, body=%wide.region_30.34_spmd.sunk | while | flops 1372060928 | bytes 124600592 | solution.py:136
  1828.8 10.5 bitcast_convert_fusion.1
  1839.3 11.1 bitcast_convert_fusion
  1874.2 39.1 %reduce-scatter.22.cloned.1.call-done = bf16[8,256,256]{2,1,0:T(8,128)(2,1)} async-done(((bf16[8,1024,256]{2,1,0:T(8,128)(2,1)}), bf16[8,256,256]{2,1,0:T(8,128)(2,1)}) %reduce-scatter.22.cloned.1.call-update) | async-done | bytes 1048592 | tf_op jit(solution)/shard_map/reduce_scatter | solution.py:280
  1933.9 115.8 %all-reduce.4.cloned.1.call-done = (bf16[1024,256]{0,1:T(8,128)(2,1)}, bf16[1024,256]{0,1:T(8,128)(2,1)}, bf16[1024,256]{1,0:T(8,128)(2,1)}, bf16[1024,256]{1,0:...) async-done(((bf16[1024,256]{0,1:T(8,128)(2,1)}, ...) | async-done | bytes 8388624 | tf_op jit(solution)/shard_map/psum | solution.py:307
  2066.9 130.5 %reduce-scatter.26.cloned.1.call-done = f32[8,64,1024]{2,1,0:T(8,128)} async-done(((f32[8,256,1024]{2,1,0:T(8,128)}), f32[8,64,1024]{2,1,0:T(8,128)}) %reduce-scatter.26.cloned.1.call-update) | async-done | bytes 2097168 | tf_op jit(solution)/shard_map/reduce_scatter | solution.py:48
  2200.7 46.7 %all-reduce = (f32[1024]{0:T(1024)}, f32[1024]{0:T(1024)}, f32[1024]{0:T(1024)}) all-reduce(f32[1024]{0:T(1024)S(1)} %get-tuple-element.324, f32[1024]{0:T(1024)S(1)} %copy-done.66, f32[1024]{0:T(1024)S(1)} %copy-done.65), channel_id=1, replica_groups=mesh['batch'=2,'seq'=4,'head'=4] {'batch','seq','head'}, use_global_device_ids=true, to_apply=%region_44.45 | all-reduce | flops 3072 | bytes 24576 | tf_op jit(solution)/shard_map/psum | solution.py:313
  2251.7 94.8 %reduce-scatter.32.cloned.1.call-done = f32[8,64,1024]{2,1,0:T(8,128)} async-done(((f32[8,256,1024]{2,1,0:T(8,128)}), f32[8,64,1024]{2,1,0:T(8,128)}) %reduce-scatter.32.cloned.1.call-update) | async-done | bytes 2097168 | tf_op jit(solution)/shard_map/reduce_scatter | solution.py:48
  (529 shorter events, 549.4 us)
Async XLA Ops:
  7.2 868.5 %copy-start = (bf16[1024,1024]{1,0:T(8,128)(2,1)S(1)}, bf16[1024,1024]{1,0:T(8,128)(2,1)}, u32[]{:S(2)}) copy-start(bf16[1024,1024]{1,0:T(8,128)(2,1)} %param.42) | copy-start | bytes 6291460
  7.2 90.1 %all-gather.12.cloned.1.call-start = ((), (), s32[]{:S(2)}) async-start(), calls=%async_computation.11 | async-start | bytes 5242880 | tf_op jit(solution)/shard_map/all_gather | solution.py:44
  14.3 121.0 %all-gather.16.cloned.1.call-start = ((), (), s32[]{:S(2)}) async-start(), calls=%async_computation.13 | async-start | bytes 5242880 | tf_op jit(solution)/shard_map/all_gather | solution.py:201
  101.8 70.2 %all-gather.14.cloned.1.call-start = ((), (), s32[]{:S(2)}) async-start(), calls=%async_computation.12 | async-start | bytes 5242880 | tf_op jit(solution)/shard_map/all_gather | solution.py:202
  106.3 153.4 %all-gather.18.cloned.1.call-start = ((), (), s32[]{:S(2)}) async-start(), calls=%async_computation.15 | async-start | bytes 5242880 | tf_op jit(solution)/shard_map/all_gather | solution.py:44
  106.9 297.0 %reduce-scatter.12.cloned.1.call-start = ((), (), s32[]{:S(2)}) async-start(), calls=%async_computation.14 | async-start | bytes 10485760 | tf_op jit(solution)/shard_map/reduce_scatter | solution.py:48
  259.7 182.0 %all-gather.24.cloned.1.call-start = ((), (), s32[]{:S(2)}) async-start(), calls=%async_computation.18 | async-start | bytes 5242880 | tf_op jit(solution)/shard_map/all_gather | solution.py:203
  265.1 213.2 %all-gather.20.cloned.1.call-start = ((), (), s32[]{:S(2)}) async-start(), calls=%async_computation.16 | async-start | bytes 5242880 | tf_op jit(solution)/shard_map/all_gather | solution.py:204
  270.5 290.4 %all-gather.22.cloned.1.call-start = ((), (), s32[]{:S(2)}) async-start(), calls=%async_computation.17 | async-start | bytes 5242880 | tf_op jit(solution)/shard_map/all_gather | solution.py:44
  408.4 380.3 %reduce-scatter.14.cloned.1.call-start = ((), (), s32[]{:S(2)}) async-start(), calls=%async_computation.19 | async-start | bytes 10485760 | tf_op jit(solution)/shard_map/reduce_scatter | solution.py:48
  645.7 146.8 %copy-start.57 = (f32[1024]{0:T(1024)S(1)}, f32[1024]{0:T(1024)}, u32[]{:S(2)}) copy-start(f32[1024]{0:T(1024)} %param.41) | copy-start | bytes 12292
  645.7 230.0 %all-gather.26.cloned.1.call-start = ((), (), s32[]{:S(2)}) async-start(), calls=%async_computation.20 | async-start | bytes 5242880 | tf_op jit(solution)/shard_map/all_gather | solution.py:44
  793.8 162.7 %all-gather.28.cloned.1.call-start = ((), (), s32[]{:S(2)}) async-start(), calls=%async_computation.22 | async-start | bytes 5242880 | tf_op jit(solution)/shard_map/all_gather | solution.py:44
  794.5 326.4 %reduce-scatter.18.cloned.1.call-start = ((), (), s32[]{:S(2)}) async-start(), calls=%async_computation.23 | async-start | bytes 10485760 | tf_op jit(solution)/shard_map/reduce_scatter | solution.py:48
  978.0 290.6 %reduce-scatter.16.cloned.1.call-start = ((), (), s32[]{:S(2)}) async-start(), calls=%async_computation.21 | async-start | bytes 10485760 | tf_op jit(solution)/shard_map/reduce_scatter | solution.py:48
  991.6 365.4 %all-gather.30.cloned.1.call-start = ((), (), s32[]{:S(2)}) async-start(), calls=%async_computation.24 | async-start | bytes 5242880 | tf_op jit(solution)/shard_map/all_gather | solution.py:44
  1123.9 149.9 %copy-start.14 = (bf16[8,64,1024]{2,1,0:T(8,128)(2,1)S(1)}, bf16[8,64,1024]{2,1,0:T(8,128)(2,1)}, u32[]{:S(2)}) copy-start(bf16[8,64,1024]{2,1,0:T(8,128)(2,1)} %param.28) | copy-start | bytes 3145732
  1275.1 341.6 %reduce-scatter.20.cloned.1.call-start = ((), (), s32[]{:S(2)}) async-start(), calls=%async_computation.25 | async-start | bytes 10485760 | tf_op jit(solution)/shard_map/reduce_scatter | solution.py:48
  1473.7 143.0 %copy-start.54 = (f32[1024]{0:T(1024)S(1)}, f32[1024]{0:T(1024)}, u32[]{:S(2)}) copy-start(f32[1024]{0:T(1024)} %param.36) | copy-start | bytes 12292
  1473.7 146.8 %copy-start.15 = (bf16[8,64,1024]{2,1,0:T(8,128)(2,1)S(1)}, bf16[8,64,1024]{2,1,0:T(8,128)(2,1)}, u32[]{:S(2)}) copy-start(bf16[8,64,1024]{2,1,0:T(8,128)(2,1)} %param.28) | copy-start | bytes 3145732
  1473.7 145.2 %copy-start.63 = (f32[8,64]{1,0:T(8,128)S(1)}, f32[8,64]{1,0:T(8,128)}, u32[]{:S(2)}) copy-start(f32[8,64]{1,0:T(8,128)} %copy-done.62) | copy-start | bytes 6148
  1473.7 145.2 %copy-start.56 = (f32[8,64]{1,0:T(8,128)S(1)}, f32[8,64]{1,0:T(8,128)}, u32[]{:S(2)}) copy-start(f32[8,64]{1,0:T(8,128)} %copy-done.55) | copy-start | bytes 6148
  1473.7 146.8 %copy-start.59 = (f32[8,64]{1,0:T(8,128)S(1)}, f32[8,64]{1,0:T(8,128)}, u32[]{:S(2)}) copy-start(f32[8,64]{1,0:T(8,128)} %copy-done.58) | copy-start | bytes 6148
  1473.8 230.8 %all-gather.32.cloned.1.call-start = ((), (), s32[]{:S(2)}) async-start(), calls=%async_computation.26 | async-start | bytes 5242880 | tf_op jit(solution)/shard_map/all_gather | solution.py:44
  1622.7 232.5 %reduce-scatter.28.cloned.1.call-start = ((), (), s32[]{:S(2)}) async-start(), calls=%async_computation.30 | async-start | bytes 5242880 | tf_op jit(solution)/shard_map/reduce_scatter | solution.py:245
  1623.3 236.7 %reduce-scatter.30.cloned.1.call-start = ((), (), s32[]{:S(2)}) async-start(), calls=%async_computation.31 | async-start | bytes 5242880 | tf_op jit(solution)/shard_map/reduce_scatter | solution.py:248
  1623.9 245.7 %reduce-scatter.24.cloned.1.call-start = ((), (), s32[]{:S(2)}) async-start(), calls=%async_computation.28 | async-start | bytes 5242880 | tf_op jit(solution)/shard_map/reduce_scatter | solution.py:283
  1821.9 91.4 %reduce-scatter.22.cloned.1.call-start = ((), (), s32[]{:S(2)}) async-start(), calls=%async_computation.27 | async-start | bytes 5242880 | tf_op jit(solution)/shard_map/reduce_scatter | solution.py:280
  1828.5 221.2 %all-reduce.4.cloned.1.call-start = ((), (), s32[]{:S(2)}) async-start(), calls=%async_computation.33 | async-start | bytes 16777216 | tf_op jit(solution)/shard_map/psum | solution.py:307
  1917.9 279.4 %reduce-scatter.26.cloned.1.call-start = ((), (), s32[]{:S(2)}) async-start(), calls=%async_computation.29 | async-start | bytes 10485760 | tf_op jit(solution)/shard_map/reduce_scatter | solution.py:48
  1926.6 420.0 %reduce-scatter.32.cloned.1.call-start = ((), (), s32[]{:S(2)}) async-start(), calls=%async_computation.32 | async-start | bytes 10485760 | tf_op jit(solution)/shard_map/reduce_scatter | solution.py:48
  2199.6 146.9 %copy-start.1 = (bf16[1024,1024]{1,0:T(8,128)(2,1)S(1)}, bf16[1024,1024]{1,0:T(8,128)(2,1)}, u32[]{:S(2)}) copy-start(bf16[1024,1024]{1,0:T(8,128)(2,1)} %param.42) | copy-start | bytes 6291460
  (84 other events, 2412.9 us)
Sparse Core Ops, SparseCore 0:
  14.5 82.8 all-gather.11
  101.9 33.4 all-gather.15
  137.5 34.4 all-gather.13
  173.4 80.3 all-gather.17
  259.8 144.0 reduce-scatter.11
  405.9 35.7 all-gather.23
  443.8 34.4 all-gather.19
  480.5 80.3 all-gather.21
  645.8 142.8 reduce-scatter.13
  793.9 81.6 all-gather.25
  877.2 79.2 all-gather.27
  978.1 142.8 reduce-scatter.17
  1123.3 145.1 reduce-scatter.15
  1275.3 81.6 all-gather.29
  1473.8 142.8 reduce-scatter.19
  1622.9 81.6 all-gather.31
  1706.9 43.0 reduce-scatter.27
  1752.5 44.5 reduce-scatter.29
  1822.0 43.5 reduce-scatter.23
  1868.7 44.5 reduce-scatter.21
  1919.9 129.8 all-reduce.3
  2052.2 145.0 reduce-scatter.25
  2200.4 146.1 reduce-scatter.31
where the time goes:
time: 2360 us; the launch traced here: 2350 us
  waiting for transfers between devices  1670 us (71%)
  matrix products  372 us (16%)
  local copies, waits for them, and re-layouts  177 us (8%)
  other arithmetic  73.3 us (3%)
  blocking collectives  46.7 us (2%)
    reduce_scatter x7, waiting for transfers between devices, collect(): lax.psum_scatter(partial_rows, 'head', scatter_dimension=1, tiled=True)  918 us
    all_gather x7, waiting for transfers between devices, spread(): return lax.all_gather(token_rows, 'head', axis=1, tiled=True)  473 us
    psum x1, waiting for transfers between devices, body(): lax.psum(grad_w_mem_key.astype(jnp.bfloat16), ('batch', 'seq'))  116 us
    sub x16, matrix products, softmax_of(): weights = jnp.exp(scores - highest)  104 us
    dynamic_slice x56, local copies, waits for them, and re-layouts, grouped(): result = lax.map(lambda block_items: function(*block_items), stacked)  69.2 us
    dot_general x10, matrix products, project(): jnp.einsum('rtd,de->rte', token_rows, matrix, preferred_element_type=jnp....  59.1 us
    dot_general x10, matrix products, weight_grad(): jnp.einsum('rtd,rte->de', token_rows, grad_rows, preferred_element_type=j...  48.7 us
  transfers between devices with their start and end apart: 23, of which 19 were waited for; matrix products, arithmetic and copies ran while one was open for 15% of the time, Pallas kernels for 0%

commit v1 on v0

v1 whole, which is shorter than its diff:
```python
import jax
import jax.numpy as jnp
from jax import lax
from jax.sharding import Mesh
from jax.sharding import PartitionSpec as P

HEAD_DIM = 64
LEN = 1024
EPSILON = 1e-05
MASKED = -1000000000.0
BF = jnp.bfloat16
F32 = jnp.float32
SWAP = [(0, 1), (1, 0)]


def dot(left, right, left_dim, right_dim):
    return lax.dot_general(
        left, right, (((left_dim,), (right_dim,)), ((), ())), preferred_element_type=F32
    )


def normalize(activity, gain):
    centre = jnp.mean(activity, -1, keepdims=True)
    shifted = activity - centre
    variance = jnp.mean(shifted * shifted, -1, keepdims=True)
    return (shifted * lax.rsqrt(variance + EPSILON) * gain).astype(BF)


def normalize_back(activity, gain, grad):
    centre = jnp.mean(activity, -1, keepdims=True)
    shifted = activity - centre
    variance = jnp.mean(shifted * shifted, -1, keepdims=True)
    rate = lax.rsqrt(variance + EPSILON)
    unit = shifted * rate
    scaled = grad * gain
    inner = scaled - jnp.mean(scaled, -1, keepdims=True)
    grad_activity = rate * (inner - unit * jnp.mean(scaled * unit, -1, keepdims=True))
    return grad_activity, jnp.sum(grad * unit, 0)


def core_swap(piece):
    return lax.ppermute(piece, "core", SWAP)


def both(own):
    return jnp.concatenate([own, core_swap(own)], 0)


def own_sum(partial):
    half = partial.shape[0] // 2
    other = core_swap(partial[half:].astype(BF))
    return partial[:half] + other.astype(F32)


def to_row(tokens):
    rows, span, width = tokens.shape
    moved = lax.all_to_all(tokens, ("yy", "head"), 0, 0, tiled=True)
    return moved.reshape(rows * span, width)


def from_row(own, rows):
    parts = own.reshape(rows, own.shape[0] // rows, own.shape[1])
    return lax.all_to_all(parts, ("yy", "head"), 0, 0, tiled=True)


def gather_weight(piece):
    rows, width = piece.shape
    along = lax.all_gather(piece, "head", axis=0, tiled=False)
    for axis in ("yy", "batch"):
        along = lax.all_gather(along, axis, axis=1, tiled=False)
    return along.reshape(along.shape[0], -1, width)


def halve(grads, axis, dim):
    count = lax.axis_size(axis)
    if count == 2:
        index = lax.axis_index(axis)
        mine = lax.dynamic_index_in_dim(grads, index, dim, keepdims=False)
        other = lax.dynamic_index_in_dim(grads, 1 - index, dim, keepdims=False)
        return (mine.astype(F32) + lax.ppermute(other, axis, SWAP).astype(F32)).astype(BF)
    return lax.psum_scatter(grads, axis, scatter_dimension=dim, tiled=False)


def sum_weight(grads):
    heads, total, width = grads.shape
    nx, ny = lax.axis_size("batch"), lax.axis_size("yy")
    cut = grads.astype(BF).reshape(heads, nx, ny, total // (nx * ny), width)
    first = halve(halve(cut[: heads // 2], "batch", 1), "yy", 1)
    second = halve(halve(cut[heads // 2 :], "yy", 2), "batch", 1)
    cut = jnp.concatenate([first, second], 0)
    cut = lax.all_to_all(cut, "head", 0, 0, tiled=True)
    summed = jnp.sum(cut.astype(F32), 0).astype(BF)
    summed = lax.all_gather(summed, "yy", axis=0, tiled=True)
    return lax.all_gather(summed, "batch", axis=0, tiled=True)


def chances_of(query, keys, allowed):
    scores = jnp.einsum("qhe,khe->hqk", query, keys, preferred_element_type=F32)
    scores = jnp.where(allowed[None], scores * HEAD_DIM**-0.5, MASKED)
    weights = jnp.exp(scores - jnp.max(scores, -1, keepdims=True))
    return weights / jnp.sum(weights, -1, keepdims=True)


def heads_of(matrix):
    return matrix.reshape(matrix.shape[0], -1, HEAD_DIM)


def attend(query, keys, values, allowed):
    chances = chances_of(heads_of(query), heads_of(keys), allowed)
    mixed = jnp.einsum("hqk,khe->qhe", chances.astype(BF), heads_of(values), preferred_element_type=F32)
    return mixed.astype(BF).reshape(query.shape)


def attend_back(query, keys, values, allowed, grad):
    query, keys, values, grad = (heads_of(m) for m in (query, keys, values, grad))
    chances = chances_of(query, keys, allowed)
    grad_chances = jnp.einsum("qhe,khe->hqk", grad, values, preferred_element_type=F32)
    inner = jnp.sum(chances * grad_chances, -1, keepdims=True)
    grad_scores = (chances * (grad_chances - inner)).astype(BF)
    scale = HEAD_DIM**-0.5
    gq = jnp.einsum("hqk,khe->qhe", grad_scores, keys, preferred_element_type=F32) * scale
    gk = jnp.einsum("hqk,qhe->khe", grad_scores, query, preferred_element_type=F32) * scale
    gv = jnp.einsum("hqk,qhe->khe", chances.astype(BF), grad, preferred_element_type=F32)
    return tuple(m.astype(BF).reshape(m.shape[0], -1) for m in (gq, gk, gv))


def body(
    inputs,
    memory,
    cotangent,
    tgt_lengths,
    src_ids,
    gain_one,
    w_query,
    w_key,
    w_value,
    w_out,
    gain_two,
    w_cross_query,
    w_mem_key,
    w_mem_value,
    w_cross_out,
    gain_three,
    w_up,
    w_down,
):
    nx, ny, nz = (lax.axis_size(a) for a in ("batch", "yy", "head"))
    ix, iy, core, iz = (lax.axis_index(a) for a in ("batch", "yy", "core", "head"))
    rows = inputs.shape[0]
    nxy, place = nx * ny, ix * ny + iy

    def column_part(*matrices):
        parts = []
        for matrix in matrices:
            deep, wide = matrix.shape[0] // nxy, matrix.shape[1] // 2
            parts.append(lax.dynamic_slice(matrix, (place * deep, core * wide), (deep, wide)))
        return jnp.concatenate(parts, 1) if len(parts) > 1 else parts[0]

    def row_part(matrix):
        deep = matrix.shape[0] // 2 // nxy
        return lax.dynamic_slice_in_dim(matrix, (core * nxy + place) * deep, deep, 0)

    def spread(tokens, gathered):
        return jnp.einsum("td,zdf->tzf", tokens, gathered, preferred_element_type=F32)

    def spread_back(grads, gathered):
        return jnp.einsum("tzf,zdf->td", grads, gathered, preferred_element_type=F32)

    def flat(matrix):
        return matrix.reshape(matrix.shape[0], -1)

    def tall(gathered):
        return gathered.reshape(-1, gathered.shape[2])

    row = iy * nz + iz
    lengths = lax.dynamic_index_in_dim(tgt_lengths, row, 0, keepdims=False)
    source_ids = lax.dynamic_index_in_dim(src_ids, row, 0, keepdims=False)
    positions = jnp.arange(LEN, dtype=jnp.int32)
    ends = jnp.cumsum(lengths)[:-1]
    target_ids = jnp.sum((positions[:, None] >= ends[None, :]).astype(jnp.int32), -1)

    def ordered(values):
        cut = values.reshape(ny, 2, -1)
        own = lax.dynamic_index_in_dim(cut, core, 1, keepdims=False)
        other = lax.dynamic_index_in_dim(cut, 1 - core, 1, keepdims=False)
        return jnp.concatenate([own.reshape(-1), other.reshape(-1)])

    target_ids, source_ids, positions = ordered(target_ids), ordered(source_ids), ordered(positions)
    self_allowed = (target_ids[:, None] == target_ids[None, :]) & (
        positions[None, :] <= positions[:, None]
    )
    cross_allowed = target_ids[:, None] == source_ids[None, :]

    residual = to_row(inputs).astype(F32)
    source = both(to_row(memory))
    cot_own = to_row(cotangent)
    cot = both(cot_own)

    w_self = gather_weight(column_part(w_query, w_key, w_value))
    w_o = tall(gather_weight(row_part(w_out)))
    w_mem = gather_weight(column_part(w_mem_key, w_mem_value))
    w_cq = gather_weight(column_part(w_cross_query))
    w_co = tall(gather_weight(row_part(w_cross_out)))
    w_u = gather_weight(column_part(w_up))
    w_d = tall(gather_weight(row_part(w_down)))

    normed_one = both(normalize(residual, gain_one))
    qkv = spread(normed_one, w_self).astype(BF)
    part = w_query.shape[1] // 2
    q, k, v = (flat(qkv[:, :, i * part : (i + 1) * part]) for i in range(3))
    mkv = spread(source, w_mem).astype(BF)
    mk, mv = (flat(mkv[:, :, i * part : (i + 1) * part]) for i in range(2))

    self_mixed = attend(q, k, v, self_allowed)
    after_self = residual + own_sum(dot(self_mixed, w_o, 1, 0))
    normed_two = both(normalize(after_self, gain_two))
    cq = flat(spread(normed_two, w_cq).astype(BF))
    cross_mixed = attend(cq, mk, mv, cross_allowed)
    after_cross = after_self + own_sum(dot(cross_mixed, w_co, 1, 0))
    normed_three = both(normalize(after_cross, gain_three))
    hidden_pre = spread(normed_three, w_u)
    hidden_act, gate_pull = jax.vjp(lambda p: jax.nn.gelu(p, approximate=True), hidden_pre)
    hidden_act = flat(hidden_act.astype(BF))
    output = (after_cross + own_sum(dot(hidden_act, w_d, 1, 0))).astype(BF)
    output = from_row(output, rows)

    def stacked(grads):
        return grads.reshape(nz, -1, grads.shape[1])

    g_down = sum_weight(stacked(dot(hidden_act, cot, 0, 0)))
    grad_pre = gate_pull(dot(cot, w_d, 1, 1).reshape(hidden_pre.shape))[0].astype(BF)
    g_up = sum_weight(jnp.einsum("td,tzf->zdf", normed_three, grad_pre, preferred_element_type=F32))
    third_back = own_sum(spread_back(grad_pre, w_u))
    step, grad_gain_three = normalize_back(after_cross, gain_three, third_back)
    grad_after_cross = cot_own.astype(F32) + step

    cross_grad = both(grad_after_cross.astype(BF))
    g_co = sum_weight(stacked(dot(cross_mixed, cross_grad, 0, 0)))
    grad_cross_mixed = dot(cross_grad, w_co, 1, 1).astype(BF)
    gcq, gmk, gmv = attend_back(cq, mk, mv, cross_allowed, grad_cross_mixed)

    def three(matrix):
        return matrix.reshape(matrix.shape[0], nz, -1)

    gcq = three(gcq)
    gmkv = jnp.concatenate([three(gmk), three(gmv)], 2)
    g_cq = sum_weight(jnp.einsum("td,tzf->zdf", normed_two, gcq, preferred_element_type=F32))
    g_mem = sum_weight(jnp.einsum("td,tzf->zdf", source, gmkv, preferred_element_type=F32))
    second_back = own_sum(spread_back(gcq, w_cq))
    grad_memory = own_sum(spread_back(gmkv, w_mem))
    grad_memory = from_row(grad_memory.astype(BF), rows).astype(F32)
    step, grad_gain_two = normalize_back(after_self, gain_two, second_back)
    grad_after_self = grad_after_cross + step

    self_grad = both(grad_after_self.astype(BF))
    g_o = sum_weight(stacked(dot(self_mixed, self_grad, 0, 0)))
    grad_self_mixed = dot(self_grad, w_o, 1, 1).astype(BF)
    gq, gk, gv = attend_back(q, k, v, self_allowed, grad_self_mixed)
    gqkv = jnp.concatenate([three(gq), three(gk), three(gv)], 2)
    g_self = sum_weight(jnp.einsum("td,tzf->zdf", normed_one, gqkv, preferred_element_type=F32))
    first_back = own_sum(spread_back(gqkv, w_self))
    step, grad_gain_one = normalize_back(residual, gain_one, first_back)
    grad_inputs = from_row((grad_after_self + step).astype(BF), rows).astype(F32)

    gains = lax.psum(
        jnp.stack([grad_gain_one, grad_gain_two, grad_gain_three]), ("batch", "yy", "core", "head")
    )

    def cored(grads, dim):
        other = core_swap(grads)
        low = jnp.where(core == 0, grads, other)
        high = jnp.where(core == 0, other, grads)
        return low.astype(F32), high.astype(F32)

    def columns(grads, count):
        low, high = cored(grads, 1)
        wide = grads.shape[1] // count
        return [
            jnp.concatenate([low[:, i * wide : (i + 1) * wide], high[:, i * wide : (i + 1) * wide]], 1)
            for i in range(count)
        ]

    def tall_rows(grads):
        return jnp.concatenate(cored(grads, 0), 0)

    grad_q, grad_k, grad_v = columns(g_self, 3)
    grad_mk, grad_mv = columns(g_mem, 2)
    return (
        output,
        grad_inputs,
        grad_memory,
        gains[0],
        grad_q,
        grad_k,
        grad_v,
        tall_rows(g_o),
        gains[1],
        columns(g_cq, 1)[0],
        grad_mk,
        grad_mv,
        tall_rows(g_co),
        gains[2],
        columns(g_up, 1)[0],
        tall_rows(g_down),
    )


def solution(mesh):
    nb, ns, nh = (mesh.shape[a] for a in ("batch", "seq", "head"))
    fine = Mesh(mesh.devices.reshape(nb, ns // 2, 2, nh), ("batch", "yy", "core", "head"))
    tokens = P("batch", ("yy", "core", "head"), None)
    ids = P("batch", None)
    wide, tall = P(None, "head"), P("head", None)
    return jax.shard_map(
        body,
        mesh=fine,
        in_specs=(
            tokens, tokens, tokens, ids, ids,
            P(), wide, wide, wide, tall,
            P(), wide, wide, wide, tall,
            P(), wide, tall,
        ),
        out_specs=(
            tokens, tokens, tokens,
            P(), wide, wide, wide, tall,
            P(), wide, wide, wide, tall,
            P(), wide, tall,
        ),
        check_vma=False,
    )
```

time: 2360 us -> 1250 us (0.53)
  waiting for transfers between devices: 1670 us -> 250 us
  blocking collectives: 46.7 us -> 231 us
  starting transfers between devices: 2.94 us -> 119 us
  matrix products: 372 us -> 292 us
  other arithmetic: 73.3 us -> 149 us
    reduce_scatter x11 -> x0, waiting for transfers between devices: 958 us -> none  [the longest x7 918 us: collect(): lax.psum_scatter(partial_rows, 'head', scatter_dimension=1, tiled=True)]
    all_gather x11 -> x15, waiting for transfers between devices: 590 us -> 146 us  [the longest x11 138 us: gather_weight(): along = lax.all_gather(along, axis, axis=1, tiled=False)]
    all_gather x0 -> x20, blocking collectives: none -> 186 us  [the longest x5 87.1 us: gather_weight(): along = lax.all_gather(piece, 'head', axis=0, tiled=False)]
    psum x1 -> x0, waiting for transfers between devices: 116 us -> none  [body(): lax.psum(grad_w_mem_key.astype(jnp.bfloat16), ('batch', 'seq'))]
    convert_element_type x21 -> x41, other arithmetic: 32 us -> 102 us  [the longest x2 56.2 us: attend_back(): grad_scores = (chances * (grad_chances - inner)).astype(BF)]
    sub x16 -> x2, matrix products: 104 us -> 35.5 us  [chances_of(): weights = jnp.exp(scores - jnp.max(scores, -1, keepdims=True))]
    ppermute x0 -> x49, waiting for transfers between devices: none -> 59.8 us  [the longest x28 58.2 us: halve(): lax.ppermute(other, axis, SWAP).astype(F32)]
    all_to_all x0 -> x13, starting transfers between devices: none -> 58.9 us  [the longest x7 33.2 us: sum_weight(): cut = lax.all_to_all(cut, 'head', 0, 0, tiled=True)]
  transfers between devices with their start and end apart: 23 -> 77, of which waited for: 19 -> 20; matrix products, arithmetic and copies ran while one was open for 15% -> 45% of each run, Pallas kernels for 0% -> 0%
where the time goes in v1:
time: 1250 us; the launch traced here: 1240 us
  matrix products  292 us (23%)
  waiting for transfers between devices  250 us (20%)
  blocking collectives  231 us (18%)
  local copies, waits for them, and re-layouts  187 us (15%)
  other arithmetic  149 us (12%)
  starting transfers between devices  119 us (10%)
  between operations  15.9 us (1%)
    all_gather x11, waiting for transfers between devices, gather_weight(): along = lax.all_gather(along, axis, axis=1, tiled=False)  138 us
    all_gather x5, blocking collectives, gather_weight(): along = lax.all_gather(piece, 'head', axis=0, tiled=False)  87.1 us
    ppermute x28, waiting for transfers between devices, halve(): lax.ppermute(other, axis, SWAP).astype(F32)  58.2 us
    convert_element_type x2, other arithmetic, attend_back(): grad_scores = (chances * (grad_chances - inner)).astype(BF)  56.2 us
    dot_general x9, matrix products, dot(): lax.dot_general(left, right, (((left_dim,), (right_dim,)), ((), ())), pre...  45.4 us
    psum x1, blocking collectives, body(): lax.psum(jnp.stack([grad_gain_one, grad_gain_two, grad_gain_three]), ('ba...  45.1 us
    dot_general x2, matrix products, attend_back(): jnp.einsum('qhe,khe->hqk', grad, values, preferred_element_type=F32)  43 us
    all_gather x7, blocking collectives, sum_weight(): summed = lax.all_gather(summed, 'yy', axis=0, tiled=True)  41.8 us
  transfers between devices with their start and end apart: 77, of which 20 were waited for; matrix products, arithmetic and copies ran while one was open for 45% of the time, Pallas kernels for 0%

profile of v1, /device:TPU:1, one launch (start us, length us, event | category | flops | bytes accessed | tf_op | source)
XLA Modules:
  0.0 1243.4 jit_solution(6885625940092216870)
XLA Ops:
  10.0 18.5 %all-gather = bf16[1024,384]{1,0:T(8,128)(2,1)} all-gather(bf16[256,384]{1,0:T(8,128)(2,1)S(1)} %pad_maximum_fusion.27), channel_id=2, replica_groups=mesh['batch'=2,'yy'=2,'core'=2,'head'=4] {'head'}, dimensions={0}, use_global_device_ids=true | all-gather | bytes 983040 | tf_op jit(solution)/shard_map/all_gather | solution.py:68
  28.6 13.8 %all-gather.6 = bf16[1024,256]{1,0:T(8,128)(2,1)} all-gather(bf16[256,256]{1,0:T(8,128)(2,1)S(1)} %pad_maximum_fusion.28), channel_id=8, replica_groups=mesh['batch'=2,'yy'=2,'core'=2,'head'=4] {'head'}, dimensions={0}, use_global_device_ids=true | all-gather | bytes 655360 | tf_op jit(solution)/shard_map/all_gather | solution.py:68
  44.3 13.9 %all-gather.41.cloned.1.call-done = bf16[4,512,384]{2,1,0:T(8,128)(2,1)} async-done(((bf16[4,256,384]{2,1,0:T(8,128)(2,1)}), bf16[4,512,384]{2,1,0:T(8,128)(2,1)}) %all-gather.41.cloned.1.call-update) | async-done | bytes 1572880 | tf_op jit(solution)/shard_map/all_gather | solution.py:70
  61.8 12.2 all-gather.3
  74.0 11.8 all-gather.4
  86.8 11.4 all-gather.9
  120.7 31.2 %all-gather.12 = bf16[128,1024]{1,0:T(8,128)(2,1)S(1)} all-gather(bf16[32,1024]{1,0:T(8,128)(2,1)S(1)} %constant_dynamic-slice_fusion.23), channel_id=14, replica_groups=mesh['batch'=2,'yy'=2,'core'=2,'head'=4] {'head'}, dimensions={0}, use_global_device_ids=true | all-gather | bytes 327680 | tf_op jit(solution)/shard_map/all_gather | solution.py:68
  191.0 16.2 %fusion.155 = (f32[8,1024]{1,0:T(8,128)S(1)}, f32[8,1024,1024]{1,2,0:T(8,128)}) fusion(pred[1024,1024]{0,1:T(8,128)(4,1)} %get-tuple-element.103, bf16[1024,8,64]{0,2,1:T(8,128)(2,1)S(1)} %bitcast.398, bf16[1024,8,64]{0,2,1:T(8,128)(2,1)S(1)} %bitcast.396), kind=kOutput, calls=%fused_computation.342 | convolution fusion | flops 1107297280 | bytes 36732928 | tf_op jit(solution)/shard_map/sub | solution.py:100
  207.2 12.5 %fusion.65 = bf16[8,64,1024]{2,1,0:T(8,128)(2,1)S(1)} fusion(bf16[1024,8,64]{0,2,1:T(8,128)(2,1)} %bitcast.438, f32[8,1024,1024]{1,2,0:T(8,128)} %get-tuple-element.111, f32[8,1024]{1,0:T(8,128)S(1)} %get-tuple-element.110), kind=kOutput, calls=%fused_computation.138 | convolution fusion | flops 1091043328 | bytes 35684352 | tf_op jit(solution)/shard_map/hqk,khe->qhe/dot_general | solution.py:110
  241.0 32.0 %all-gather.49.cloned.1.call-done = bf16[4,4,256,256]{3,2,0,1:T(8,128)(2,1)} async-done(((bf16[4,2,256,256]{3,2,0,1:T(8,128)(2,1)}), bf16[4,4,256,256]{3,2,0,1:T(8,128)(2,1)}) %all-gather.49.cloned.1.call-update) | async-done | bytes 2097168 | tf_op jit(solution)/shard_map/all_gather | solution.py:70
  287.8 19.9 %all-gather.57.cloned.1.call-done = bf16[4,512,512]{2,1,0:T(8,128)(2,1)} async-done(((bf16[4,256,512]{2,1,0:T(8,128)(2,1)}), bf16[4,512,512]{2,1,0:T(8,128)(2,1)}) %all-gather.57.cloned.1.call-update) | async-done | bytes 2097168 | tf_op jit(solution)/shard_map/all_gather | solution.py:70
  315.0 19.3 %fusion.156 = (f32[8,1024]{1,0:T(8,128)S(1)}, f32[8,1024,1024]{1,2,0:T(8,128)}) fusion(pred[1024,1024]{0,1:T(8,128)(4,1)} %get-tuple-element.102, bf16[1024,8,64]{0,2,1:T(8,128)(2,1)} %bitcast.424, bf16[1024,8,64]{0,2,1:T(8,128)(2,1)S(1)} %bitcast.400), kind=kOutput, calls=%fused_computation.343 | convolution fusion | flops 1107297280 | bytes 36732928 | tf_op jit(solution)/shard_map/sub | solution.py:100
  334.3 13.6 %fusion.71 = bf16[8,64,1024]{2,1,0:T(8,128)(2,1)S(1)} fusion(bf16[1024,8,64]{0,2,1:T(8,128)(2,1)} %bitcast.440, f32[8,1024,1024]{1,2,0:T(8,128)} %get-tuple-element.113, f32[8,1024]{1,0:T(8,128)S(1)} %get-tuple-element.112), kind=kOutput, calls=%fused_computation.140 | convolution fusion | flops 1091043328 | bytes 35684352 | tf_op jit(solution)/shard_map/hqk,khe->qhe/dot_general | solution.py:110
  354.6 10.5 all-gather.63.cloned.1.call-done
  374.3 20.8 %all-to-all-done.3 = bf16[8,64,1024]{2,1,0:T(8,128)(2,1)S(1)} async-done(((bf16[8,64,1024]{2,1,0:T(8,128)(2,1)}), bf16[8,64,1024]{2,1,0:T(8,128)(2,1)S(1)}, u32[]{:S(2)}, u32[]{:S(2)}) %all-to-all-start.3) | async-done | bytes 1048608 | tf_op jit(solution)/shard_map/all_to_all | solution.py:57
  397.3 26.7 %all-gather.59.cloned.1.call-done = bf16[4,4,256,512]{3,2,0,1:T(8,128)(2,1)} async-done(((bf16[4,2,256,512]{3,2,0,1:T(8,128)(2,1)}), bf16[4,4,256,512]{3,2,0,1:T(8,128)(2,1)}) %all-gather.59.cloned.1.call-update) | async-done | bytes 4194320 | tf_op jit(solution)/shard_map/all_gather | solution.py:70
  439.5 13.5 %multiply_convert_fusion.2 = (bf16[1024,4,512]{0,2,1:T(8,128)(2,1)}, f32[1024,4,512]{0,2,1:T(8,128)}) fusion(bf16[4,1024,512]{1,2,0:T(8,128)(2,1)} %reshape.413, bf16[512,1024]{1,0:T(8,128)(2,1)} %collective-permute-done.5, bf16[512,1024]{1,0:T(8,128)(2,1)S(1)} %multiply_convert_fusion.7), kind=kOutput, calls=%fused_computation.29 | convolution fusion | flops 4318035968 | bytes 18874368 | tf_op jit(solution)/shard_map/td,zdf->tzf/dot_general | solution.py:164
  453.0 29.3 %all-gather.65.cloned.1.call-done = bf16[4,4,128,1024]{3,2,1,0:T(8,128)(2,1)} async-done(((bf16[4,2,128,1024]{3,2,1,0:T(8,128)(2,1)}), bf16[4,4,128,1024]{3,2,1,0:T(8,128)(2,1)}) %all-gather.65.cloned.1.call-update) | async-done | bytes 4194320 | tf_op jit(solution)/shard_map/all_gather | solution.py:70
  482.3 13.0 %fusion.16 = bf16[1024,4,512]{0,2,1:T(8,128)(2,1)S(1)} fusion(f32[1024,4,512]{0,2,1:T(8,128)} %get-tuple-element.115, bf16[4,512,1024]{2,1,0:T(8,128)(2,1)} %bitcast.461, bf16[512,1024]{1,0:T(8,128)(2,1)S(1)} %collective-permute-done.7, bf16[512,1024]{1,0:T(8,128)(2,1)S(1)} %bitcast.404), kind=kOutput, calls=%fused_computation.28 | convolution fusion | flops 4341104640 | bytes 18874368 | tf_op jit(solution)/shard_map/dot_general | solution.py:17
  588.0 22.0 %collective-permute-done.46 = bf16[2,2,128,1024]{3,2,1,0:T(8,128)(2,1)} collective-permute-done((bf16[2,2,128,1024]{3,2,1,0:T(8,128)(2,1)}, bf16[2,2,128,1024]{3,2,1,0:T(8,128)(2,1)}, u32[]{:S(2)}, u32[]{:S(2)}) %collective-permute-start.46) | collective-permute-done | bytes 1048608 | tf_op jit(solution)/shard_map/ppermute | solution.py:80
  639.4 14.4 %fusion.74 = bf16[8,64,1024]{2,1,0:T(8,128)(2,1)} fusion(bf16[1024,8,64]{0,2,1:T(8,128)(2,1)S(1)} %bitcast.464, f32[8,1024,1024]{1,2,0:T(8,128)} %get-tuple-element.113, f32[8,1024]{1,0:T(8,128)S(1)} %get-tuple-element.112), kind=kOutput, calls=%fused_computation.141 | convolution fusion | flops 1091043328 | bytes 35684352 | tf_op jit(solution)/shard_map/hqk,qhe->khe/dot_general | solution.py:123
  653.8 21.5 %multiply_reduce_fusion.1 = (f32[8,1024]{1,0:T(8,128)S(1)}, f32[8,1024,1024]{1,2,0:T(8,128)}) fusion(f32[8,1024,1024]{1,2,0:T(8,128)} %get-tuple-element.113, f32[8,1024]{1,0:T(8,128)S(1)} %get-tuple-element.112, bf16[1024,8,64]{0,2,1:T(8,128)(2,1)S(1)} %bitcast.465, bf16[1024,8,64]{0,2,1:T(8,128)(2,1)S(1)} %bitcast.441), kind=kOutput, calls=%fused_computation.5 | convolution fusion | flops 1098899456 | bytes 69271552 | tf_op jit(solution)/shard_map/qhe,khe->hqk/dot_general | solution.py:117
  675.3 28.2 %multiply_convert_fusion.1 = bf16[8,1024,1024]{1,2,0:T(8,128)(2,1)} fusion(f32[8,1024,1024]{1,2,0:T(8,128)} %get-tuple-element.117, f32[8,1024]{1,0:T(8,128)S(1)} %get-tuple-element.116, f32[8,1024,1024]{1,2,0:T(8,128)} %get-tuple-element.113, f32[8,1024]{1,0:T(8,128)S(1)} %get-tuple-element.112), kind=kLoop, calls=%fused_computation.4 | loop fusion | flops 33554432 | bytes 83951616 | tf_op jit(solution)/shard_map/convert_element_type | solution.py:119
  703.6 11.0 multiply_convert_fusion.3
  714.6 9.9 multiply_convert_fusion.6
  929.1 14.8 %fusion.68 = bf16[8,64,1024]{2,1,0:T(8,128)(2,1)} fusion(bf16[1024,8,64]{0,2,1:T(8,128)(2,1)} %bitcast.466, f32[8,1024,1024]{1,2,0:T(8,128)} %get-tuple-element.111, f32[8,1024]{1,0:T(8,128)S(1)} %copy-done.71), kind=kOutput, calls=%fused_computation.139 | convolution fusion | flops 1091043328 | bytes 35684352 | tf_op jit(solution)/shard_map/hqk,qhe->khe/dot_general | solution.py:123
  944.0 21.5 %multiply_reduce_fusion = (f32[8,1024]{1,0:T(8,128)S(1)}, f32[8,1024,1024]{1,2,0:T(8,128)}) fusion(f32[8,1024,1024]{1,2,0:T(8,128)} %get-tuple-element.111, f32[8,1024]{1,0:T(8,128)S(1)} %copy-done.71, bf16[1024,8,64]{0,2,1:T(8,128)(2,1)S(1)} %bitcast.467, bf16[1024,8,64]{0,2,1:T(8,128)(2,1)S(1)} %bitcast.439), kind=kOutput, calls=%fused_computation.3 | convolution fusion | flops 1098899456 | bytes 69271552 | tf_op jit(solution)/shard_map/qhe,khe->hqk/dot_general | solution.py:117
  965.4 28.0 %multiply_convert_fusion = bf16[8,1024,1024]{1,2,0:T(8,128)(2,1)} fusion(f32[8,1024,1024]{1,2,0:T(8,128)} %get-tuple-element.119, f32[8,1024]{1,0:T(8,128)S(1)} %get-tuple-element.118, f32[8,1024,1024]{1,2,0:T(8,128)} %get-tuple-element.111, f32[8,1024]{1,0:T(8,128)S(1)} %copy-done.71), kind=kLoop, calls=%fused_computation.2 | loop fusion | flops 33554432 | bytes 83951616 | tf_op jit(solution)/shard_map/convert_element_type | solution.py:119
  993.4 11.0 multiply_convert_fusion.4
  1080.4 11.7 collective-permute-done.20
  1138.9 13.2 %all-to-all-done.6 = bf16[4,256,384]{2,1,0:T(8,128)(2,1)S(1)} async-done(((bf16[4,256,384]{2,1,0:T(8,128)(2,1)}), bf16[4,256,384]{2,1,0:T(8,128)(2,1)S(1)}, u32[]{:S(2)}, u32[]{:S(2)}) %all-to-all-start.6) | async-done | bytes 786464 | tf_op jit(solution)/shard_map/all_to_all | solution.py:91
  1155.7 45.1 %psum.7 = f32[3,1024]{1,0:T(4,128)S(1)} all-reduce(f32[3,1024]{1,0:T(4,128)S(1)} %pad_maximum_fusion.29), channel_id=1, replica_groups=mesh['batch'=2,'yy'=2,'core'=2,'head'=4] {'batch','yy','core','head'}, use_global_device_ids=true, to_apply=%region_23.24 | all-reduce | flops 3072 | bytes 24576 | tf_op jit(solution)/shard_map/psum | solution.py:265
  (577 shorter events, 634.9 us)
Async XLA Ops:
  28.5 76.9 %all-gather.47.cloned.1.call-start = ((), (), s32[]{:S(2)}) async-start(), calls=%async_computation.18 | async-start | bytes 1572864 | tf_op jit(solution)/shard_map/all_gather | solution.py:70
  42.5 73.7 %all-gather.55.cloned.1.call-start = ((), (), s32[]{:S(2)}) async-start(), calls=%async_computation.22 | async-start | bytes 1310720 | tf_op jit(solution)/shard_map/all_gather | solution.py:68
  44.2 127.8 %all-gather.43.cloned.1.call-start = ((), (), s32[]{:S(2)}) async-start(), calls=%async_computation.16 | async-start | bytes 4718592 | tf_op jit(solution)/shard_map/all_gather | solution.py:70
  60.9 158.9 %all-gather.45.cloned.1.call-start = ((), (), s32[]{:S(2)}) async-start(), calls=%async_computation.17 | async-start | bytes 1572864 | tf_op jit(solution)/shard_map/all_gather | solution.py:70
  85.9 139.1 %all-gather.61.cloned.1.call-start = ((), (), s32[]{:S(2)}) async-start(), calls=%async_computation.25 | async-start | bytes 1310720 | tf_op jit(solution)/shard_map/all_gather | solution.py:68
  86.7 151.1 %all-gather.51.cloned.1.call-start = ((), (), s32[]{:S(2)}) async-start(), calls=%async_computation.20 | async-start | bytes 1572864 | tf_op jit(solution)/shard_map/all_gather | solution.py:70
  105.3 167.7 %all-gather.49.cloned.1.call-start = ((), (), s32[]{:S(2)}) async-start(), calls=%async_computation.19 | async-start | bytes 3145728 | tf_op jit(solution)/shard_map/all_gather | solution.py:70
  107.7 200.1 %all-gather.57.cloned.1.call-start = ((), (), s32[]{:S(2)}) async-start(), calls=%async_computation.23 | async-start | bytes 3145728 | tf_op jit(solution)/shard_map/all_gather | solution.py:70
  119.8 228.1 %all-gather.53.cloned.1.call-start = ((), (), s32[]{:S(2)}) async-start(), calls=%async_computation.21 | async-start | bytes 1572864 | tf_op jit(solution)/shard_map/all_gather | solution.py:70
  160.6 65.1 %all-to-all-start.1 = ((bf16[8,64,1024]{2,1,0:T(8,128)(2,1)}), bf16[8,64,1024]{2,1,0:T(8,128)(2,1)}, u32[]{:S(2)}, u32[]{:S(2)}) async-start(bf16[8,64,1024]{2,1,0:T(8,128)(2,1)} %param.19), calls=%async_computation.1 | async-start | bytes 2097152 | tf_op jit(solution)/shard_map/all_to_all | solution.py:57
  164.9 200.3 %all-gather.63.cloned.1.call-start = ((), (), s32[]{:S(2)}) async-start(), calls=%async_computation.26 | async-start | bytes 3145728 | tf_op jit(solution)/shard_map/all_gather | solution.py:70
  225.0 198.9 %all-gather.59.cloned.1.call-start = ((), (), s32[]{:S(2)}) async-start(), calls=%async_computation.24 | async-start | bytes 6291456 | tf_op jit(solution)/shard_map/all_gather | solution.py:70
  225.7 56.0 %collective-permute-start.2 = (bf16[512,1024]{1,0:T(8,128)(2,1)}, bf16[512,1024]{1,0:T(8,128)(2,1)}, u32[]{:S(2)}, u32[]{:S(2)}) collective-permute-start(bf16[512,1024]{1,0:T(8,128)(2,1)} %bitcast.17), channel_id=1, source_target_pairs={{0,4},{4,0},{1,5},{5,1},{2,6},{6,2},{3,7},{7,3},{8,12},{12,8},{9,1... | collective-permute-start | bytes 3145736 | tf_op jit(solution)/shard_map/ppermute | solution.py:42
  232.1 78.8 %collective-permute-start.3 = (bf16[512,1024]{1,0:T(8,128)(2,1)}, bf16[512,1024]{1,0:T(8,128)(2,1)}, u32[]{:S(2)}, u32[]{:S(2)}) collective-permute-start(bf16[512,1024]{1,0:T(8,128)(2,1)} %multiply_convert_fusion.8), channel_id=1, source_target_pairs={{0,4},{4,0},{1,5},{5,1},{2,6},{6,2},{3,7},{7,3},{8,12},{12,8},{9,1... | collective-permute-start | bytes 3145736 | tf_op jit(solution)/shard_map/ppermute | solution.py:42
  310.8 171.4 %all-gather.65.cloned.1.call-start = ((), (), s32[]{:S(2)}) async-start(), calls=%async_computation.27 | async-start | bytes 6291456 | tf_op jit(solution)/shard_map/all_gather | solution.py:70
  373.4 66.1 %collective-permute-start.5 = (bf16[512,1024]{1,0:T(8,128)(2,1)S(1)}, bf16[512,1024]{1,0:T(8,128)(2,1)}, u32[]{:S(2)}, u32[]{:S(2)}) collective-permute-start(bf16[512,1024]{1,0:T(8,128)(2,1)S(1)} %multiply_convert_fusion.7), channel_id=1, source_target_pairs={{0,4},{4,0},{1,5},{5,1},{2,6},{6,2},{3,7},{7,3},{8,12},{12,8},{9,1... | collective-permute-start | bytes 3145736 | tf_op jit(solution)/shard_map/ppermute | solution.py:42
  395.1 57.9 %collective-permute-start.7 = (bf16[512,1024]{1,0:T(8,128)(2,1)S(1)}, bf16[512,1024]{1,0:T(8,128)(2,1)S(1)}, u32[]{:S(2)}, u32[]{:S(2)}) collective-permute-start(bf16[512,1024]{1,0:T(8,128)(2,1)S(1)} %bitcast.403), channel_id=1, source_target_pairs={{0,4},{4,0},{1,5},{5,1},{2,6},{6,2},{3,7},{7,3},{8,12},{12,8},{9,1... | collective-permute-start | bytes 3145736 | tf_op jit(solution)/shard_map/ppermute | solution.py:42
  575.5 197.3 %all-to-all-start.2 = ((bf16[8,64,1024]{2,1,0:T(8,128)(2,1)}), bf16[8,64,1024]{2,1,0:T(8,128)(2,1)}, u32[]{:S(2)}, u32[]{:S(2)}) async-start(bf16[8,64,1024]{2,1,0:T(8,128)(2,1)} %bitcast.402), calls=%async_computation.2 | async-start | bytes 2097152 | tf_op jit(solution)/shard_map/all_to_all | solution.py:63
  580.7 55.7 %collective-permute-start.9 = (bf16[512,1024]{1,0:T(8,128)(2,1)}, bf16[512,1024]{1,0:T(8,128)(2,1)S(1)}, u32[]{:S(2)}, u32[]{:S(2)}) collective-permute-start(bf16[512,1024]{1,0:T(8,128)(2,1)} %get-tuple-element.27), channel_id=1, source_target_pairs={{0,4},{4,0},{1,5},{5,1},{2,6},{6,2},{3,7},{7,3},{8,12},{12,8},{9,1... | collective-permute-start | bytes 3145736 | tf_op jit(solution)/shard_map/ppermute | solution.py:42
  757.5 64.8 %collective-permute-start.29 = (bf16[2,2,256,256]{3,2,0,1:T(8,128)(2,1)}, bf16[2,2,256,256]{3,2,0,1:T(8,128)(2,1)}, u32[]{:S(2)}, u32[]{:S(2)}) collective-permute-start(bf16[2,2,256,256]{3,2,0,1:T(8,128)(2,1)} %bitcast.447), channel_id=1, source_target_pairs={{0,16},{16,0},{1,17},{17,1},{2,18},{18,2},{3,19},{19,3},{4,20},{20... | collective-permute-start | bytes 1572872 | tf_op jit(solution)/shard_map/ppermute | solution.py:80
  812.1 64.4 %collective-permute-start.13 = (bf16[512,1024]{1,0:T(8,128)(2,1)}, bf16[512,1024]{1,0:T(8,128)(2,1)}, u32[]{:S(2)}, u32[]{:S(2)}) collective-permute-start(bf16[512,1024]{1,0:T(8,128)(2,1)} %slice.348), channel_id=1, source_target_pairs={{0,4},{4,0},{1,5},{5,1},{2,6},{6,2},{3,7},{7,3},{8,12},{12,8},{9,1... | collective-permute-start | bytes 3145736 | tf_op jit(solution)/shard_map/ppermute | solution.py:42
  837.4 58.8 %collective-permute-start.38 = (bf16[128,1024]{1,0:T(8,128)(2,1)}, bf16[128,1024]{1,0:T(8,128)(2,1)}, u32[]{:S(2)}, u32[]{:S(2)}) collective-permute-start(bf16[128,1024]{1,0:T(8,128)(2,1)} %all_gather.219), channel_id=1, source_target_pairs={{0,4},{4,0},{1,5},{5,1},{2,6},{6,2},{3,7},{7,3},{8,12},{12,8},{9,1... | collective-permute-start | bytes 786440 | tf_op jit(solution)/shard_map/ppermute | solution.py:42
  858.1 251.3 %all-gather.37.cloned.1.call-start = ((), (), s32[]{:S(2)}) async-start(), calls=%async_computation.13 | async-start | bytes 1572864 | tf_op jit(solution)/shard_map/all_gather | solution.py:94
  887.2 223.8 %all-gather.39.cloned.1.call-start = ((), (), s32[]{:S(2)}) async-start(), calls=%async_computation.14 | async-start | bytes 1572864 | tf_op jit(solution)/shard_map/all_gather | solution.py:94
  901.2 194.3 %all-to-all-start.5 = ((bf16[8,64,1024]{2,1,0:T(8,128)(2,1)}), bf16[8,64,1024]{2,1,0:T(8,128)(2,1)S(1)}, u32[]{:S(2)}, u32[]{:S(2)}) async-start(bf16[8,64,1024]{2,1,0:T(8,128)(2,1)} %bitcast.66), calls=%async_computation.5 | async-start | bytes 2097152 | tf_op jit(solution)/shard_map/all_to_all | solution.py:63
  922.8 147.1 %collective-permute-start.33 = (bf16[1024,256]{1,0:T(8,128)(2,1)}, bf16[1024,256]{1,0:T(8,128)(2,1)}, u32[]{:S(2)}, u32[]{:S(2)}) collective-permute-start(bf16[1024,256]{1,0:T(8,128)(2,1)} %all_gather.217), channel_id=1, source_target_pairs={{0,4},{4,0},{1,5},{5,1},{2,6},{6,2},{3,7},{7,3},{8,12},{12,8},{9,1... | collective-permute-start | bytes 1572872 | tf_op jit(solution)/shard_map/ppermute | solution.py:42
  1018.1 56.2 %collective-permute-start.21 = (bf16[2,2,32,1024]{3,2,1,0:T(8,128)(2,1)}, bf16[2,2,32,1024]{3,2,1,0:T(8,128)(2,1)}, u32[]{:S(2)}, u32[]{:S(2)}) collective-permute-start(bf16[2,2,32,1024]{3,2,1,0:T(8,128)(2,1)} %dynamic-slice_bitcast_fusion.10), channel_id=1, source_target_pairs={{0,8},{8,0},{1,9},{9,1},{2,10},{10,2},{3,11},{11,3},{4,12},{12,4},... | collective-permute-start | bytes 786440 | tf_op jit(solution)/shard_map/ppermute | solution.py:80
  1019.3 56.2 %collective-permute-start.19 = (bf16[2,2,32,1024]{3,2,0,1:T(8,128)(2,1)}, bf16[2,2,32,1024]{3,2,0,1:T(8,128)(2,1)}, u32[]{:S(2)}, u32[]{:S(2)}) collective-permute-start(bf16[2,2,32,1024]{3,2,0,1:T(8,128)(2,1)} %bitcast.389), channel_id=1, source_target_pairs={{0,16},{16,0},{1,17},{17,1},{2,18},{18,2},{3,19},{19,3},{4,20},{20... | collective-permute-start | bytes 786440 | tf_op jit(solution)/shard_map/ppermute | solution.py:80
  1053.8 78.2 %collective-permute-start.12 = (bf16[512,1024]{1,0:T(8,128)(2,1)}, bf16[512,1024]{1,0:T(8,128)(2,1)}, u32[]{:S(2)}, u32[]{:S(2)}) collective-permute-start(bf16[512,1024]{1,0:T(8,128)(2,1)} %slice.349), channel_id=1, source_target_pairs={{0,4},{4,0},{1,5},{5,1},{2,6},{6,2},{3,7},{7,3},{8,12},{12,8},{9,1... | collective-permute-start | bytes 3145736 | tf_op jit(solution)/shard_map/ppermute | solution.py:42
  1109.4 110.7 %collective-permute-start.43 = (bf16[1024,512]{1,0:T(8,128)(2,1)}, bf16[1024,512]{1,0:T(8,128)(2,1)}, u32[]{:S(2)}, u32[]{:S(2)}) collective-permute-start(bf16[1024,512]{1,0:T(8,128)(2,1)} %all-gather.37.cloned.1.call-done), channel_id=1, source_target_pairs={{0,4},{4,0},{1,5},{5,1},{2,6},{6,2},{3,7},{7,3},{8,12},{12,8},{9,1... | collective-permute-start | bytes 3145736 | tf_op jit(solution)/shard_map/ppermute | solution.py:42
  1111.0 113.3 %collective-permute-start.48 = (bf16[512,1024]{1,0:T(8,128)(2,1)}, bf16[512,1024]{1,0:T(8,128)(2,1)}, u32[]{:S(2)}, u32[]{:S(2)}) collective-permute-start(bf16[512,1024]{1,0:T(8,128)(2,1)} %all-gather.39.cloned.1.call-done), channel_id=1, source_target_pairs={{0,4},{4,0},{1,5},{5,1},{2,6},{6,2},{3,7},{7,3},{8,12},{12,8},{9,1... | collective-permute-start | bytes 3145736 | tf_op jit(solution)/shard_map/ppermute | solution.py:42
  1152.1 76.0 %all-to-all-start.4 = ((bf16[8,64,1024]{2,1,0:T(8,128)(2,1)}), bf16[8,64,1024]{2,1,0:T(8,128)(2,1)S(1)}, u32[]{:S(2)}, u32[]{:S(2)}) async-start(bf16[8,64,1024]{2,1,0:T(8,128)(2,1)} %bitcast.60), calls=%async_computation.4 | async-start | bytes 2097152 | tf_op jit(solution)/shard_map/all_to_all | solution.py:63
  (132 other events, 2353.6 us)
Sparse Core Ops, SparseCore 0:
  28.6 29.5 all-gather.40
  59.7 23.8 all-gather.46
  85.8 30.4 all-gather.54
  118.2 43.8 all-gather.42
  163.5 21.2 all-gather.44
  186.8 27.8 all-gather.60
  216.8 20.9 all-gather.50
  239.9 33.1 all-gather.48
  274.6 33.1 all-gather.56
  309.1 21.2 all-gather.52
  332.0 33.1 all-gather.62
  367.1 56.7 all-gather.58
  425.5 56.7 all-gather.64
  870.3 21.9 all-gather.36
  896.3 23.9 all-gather.38

commit v2 on v1

v2 whole, which is shorter than its diff:
```python
import functools

import jax
import jax.numpy as jnp
from jax import lax
from jax.experimental import pallas as pl
from jax.experimental.pallas import tpu as pltpu
from jax.sharding import Mesh
from jax.sharding import PartitionSpec as P

HEAD_DIM = 64
LEN = 1024
BLOCK = 256
BLOCKS = LEN // BLOCK
EPSILON = 1e-05
MASKED = -1000000000.0
SCALE = HEAD_DIM**-0.5
BF = jnp.bfloat16
F32 = jnp.float32


def dot(left, right, left_dim, right_dim):
    return lax.dot_general(
        left, right, (((left_dim,), (right_dim,)), ((), ())), preferred_element_type=F32
    )


def normalize(activity, gain):
    centre = jnp.mean(activity, -1, keepdims=True)
    shifted = activity - centre
    variance = jnp.mean(shifted * shifted, -1, keepdims=True)
    return (shifted * lax.rsqrt(variance + EPSILON) * gain).astype(BF)


def normalize_back(activity, gain, grad):
    centre = jnp.mean(activity, -1, keepdims=True)
    shifted = activity - centre
    variance = jnp.mean(shifted * shifted, -1, keepdims=True)
    rate = lax.rsqrt(variance + EPSILON)
    unit = shifted * rate
    scaled = grad * gain
    inner = scaled - jnp.mean(scaled, -1, keepdims=True)
    grad_activity = rate * (inner - unit * jnp.mean(scaled * unit, -1, keepdims=True))
    return grad_activity, jnp.sum(grad * unit, 0)


def shift(piece, axis, step):
    count = lax.axis_size(axis)
    return lax.ppermute(piece, axis, [(i, (i + step) % count) for i in range(count)])


def core_swap(piece):
    return shift(piece, "core", 1)


def both(own):
    return jnp.concatenate([own, core_swap(own)], 0)


def own_sum(transposed, matrix):
    half = transposed.shape[1] // 2
    other = core_swap(dot(transposed[:, half:], matrix, 0, 0).astype(BF))
    return dot(transposed[:, :half], matrix, 0, 0) + other.astype(F32)


def to_row(tokens):
    rows, span, width = tokens.shape
    moved = lax.all_to_all(tokens, ("yy", "head"), 0, 0, tiled=True)
    return moved.reshape(rows * span, width)


def from_row(own, rows):
    parts = own.reshape(rows, own.shape[0] // rows, own.shape[1])
    return lax.all_to_all(parts, ("yy", "head"), 0, 0, tiled=True)


def ring(piece, axis):
    count = lax.axis_size(axis)
    return jnp.stack([piece] + [shift(piece, axis, k) for k in range(1, count)], 0)


def gather_weight(piece):
    along = ring(piece, "head")
    half = along.shape[0] // 2
    first = ring(ring(along[:half], "batch"), "yy")
    second = ring(ring(along[half:], "yy"), "batch")
    return first, second


def fold(grads, axis):
    count = lax.axis_size(axis)
    total = grads[0].astype(F32)
    for k in range(1, count):
        total = total + shift(grads[k], axis, -k).astype(F32)
    return total.astype(BF)


def sum_weight(grads, rows):
    nx, ny, nz = (lax.axis_size(a) for a in ("batch", "yy", "head"))
    half = grads.shape[0] // 2
    width = grads.shape[1]
    first = grads[:half].reshape(ny, nx, nz // 2, rows, width)
    second = grads[half:].reshape(nx, ny, nz // 2, rows, width)
    first = fold(fold(first, "yy"), "batch")
    second = fold(fold(second, "batch"), "yy")
    total = first[0].astype(F32)
    for k in range(1, nz):
        slot = first[k] if k < nz // 2 else second[k - nz // 2]
        total = total + shift(slot, "head", -k).astype(F32)
    return total.astype(BF)


def in_place(piece, axis):
    if lax.axis_size(axis) != 2:
        return lax.all_gather(piece, axis, axis=0, tiled=False)
    other = shift(piece, axis, 1)
    low = lax.axis_index(axis) == 0
    return jnp.stack([jnp.where(low, piece, other), jnp.where(low, other, piece)], 0)


def replicate(piece):
    return in_place(in_place(in_place(piece, "yy"), "batch"), "core")


def total_of(value):
    for axis in ("core", "yy", "batch", "head"):
        count = lax.axis_size(axis)
        step = 1
        while step < count:
            value = value + lax.ppermute(value, axis, [(i, i ^ step) for i in range(count)])
            step *= 2
    return value


def head_rows(ref, half, index, kind):
    x, z = index
    if ref.shape[5] == HEAD_DIM:
        return (0, 0, x, z, kind)
    return (0, slice(None), x, z, kind) if half == 0 else (0, x, slice(None), z, kind)


def read_head(ref, half, index, kind):
    return ref[head_rows(ref, half, index, kind)].reshape(HEAD_DIM, LEN)


def write_head(ref, half, index, kind, value):
    at = head_rows(ref, half, index, kind)
    if ref.shape[5] == HEAD_DIM:
        ref[at] = value
    else:
        ref[at] = value.reshape(-1, ref.shape[5], LEN)


def allowed_block(span_ref, base, columns, chunk):
    ahead = lax.broadcasted_iota(jnp.int32, (BLOCK, BLOCK), 0)
    if chunk < BLOCK:
        ahead = ahead + ahead // chunk * chunk
    away = ahead + (base - span_ref[0:1, columns])
    return (away >= 0) & (away <= span_ref[1:2, columns])


def span_of(index):
    return slice(index * BLOCK, (index + 1) * BLOCK)


def attend_kernel(heads, kinds, chunk, need_ref, base_ref, span_ref, *refs):
    sources = refs[: len(kinds)]
    mixed_ref, lse_ref, q_s, k_s, v_s, top_s, sum_s, acc_s = refs[len(kinds) :]
    where = [(source, kind) for source, count in zip(sources, kinds) for kind in range(count)]

    def load(half):
        for h, index in enumerate(heads):
            q, k, v = (read_head(source, half, index, kind) for source, kind in where)
            q_s[h] = (q.astype(F32) * SCALE).astype(BF)
            k_s[h] = k.T
            v_s[h] = v

    half_now = pl.program_id(0)
    for half in range(2):
        pl.when(half_now == half)(functools.partial(load, half))

    for i in range(BLOCKS):
        columns = span_of(i)
        top_s[...] = jnp.full(top_s.shape, -3e38, F32)
        sum_s[...] = jnp.zeros(sum_s.shape, F32)
        acc_s[...] = jnp.zeros(acc_s.shape, F32)
        for j in range(BLOCKS):

            @pl.when(need_ref[i * BLOCKS + j] > 0)
            def _(j=j):
                allowed = allowed_block(span_ref, base_ref[j], columns, chunk)
                for h in range(len(heads)):
                    scores = dot(k_s[h, span_of(j), :], q_s[h, :, columns], 1, 0)
                    scores = jnp.where(allowed, scores, MASKED)
                    top = jnp.maximum(top_s[h], jnp.max(scores, 0, keepdims=True))
                    fade = jnp.exp(top_s[h] - top)
                    weights = jnp.exp(scores - top)
                    top_s[h] = top
                    sum_s[h] = sum_s[h] * fade + jnp.sum(weights, 0, keepdims=True)
                    acc_s[h] = acc_s[h] * fade + dot(v_s[h, :, span_of(j)], weights.astype(BF), 1, 0)

        for h in range(len(heads)):
            lse_ref[0, h, :, columns] = top_s[h] + jnp.log(sum_s[h])
            q_s[h, :, columns] = (acc_s[h] / sum_s[h]).astype(BF)

    def store(half):
        for h, index in enumerate(heads):
            write_head(mixed_ref, half, index, 0, q_s[h])

    for half in range(2):
        pl.when(half_now == half)(functools.partial(store, half))


def attend_back_kernel(heads, kinds, chunk, need_ref, base_ref, span_ref, *refs):
    sources = refs[: len(kinds)]
    mixed_ref, grad_ref, lse_ref = refs[len(kinds) : len(kinds) + 3]
    outs = refs[len(kinds) + 3 : 2 * len(kinds) + 3]
    q_s, k_s, kt_s, v_s, g_s, inner_s, dq_s, dk_s, dv_s = refs[2 * len(kinds) + 3 :]
    where = [(source, kind) for source, count in zip(sources, kinds) for kind in range(count)]
    into = [(out, kind) for out, count in zip(outs, kinds) for kind in range(count)]

    def load(half):
        for h, index in enumerate(heads):
            q, k, v = (read_head(source, half, index, kind) for source, kind in where)
            q_s[h] = (q.astype(F32) * SCALE).astype(BF)
            kt_s[h] = k
            k_s[h] = k.T
            v_s[h] = v.T
            grad = read_head(grad_ref, half, index, 0)
            g_s[h] = grad
            mixed = read_head(mixed_ref, half, index, 0)
            inner_s[h] = jnp.sum(grad.astype(F32) * mixed.astype(F32), 0, keepdims=True)

    half_now = pl.program_id(0)
    for half in range(2):
        pl.when(half_now == half)(functools.partial(load, half))

    for acc in (dq_s, dk_s, dv_s):
        acc[...] = jnp.zeros(acc.shape, F32)

    for i in range(BLOCKS):
        columns = span_of(i)
        for j in range(BLOCKS):

            @pl.when(need_ref[i * BLOCKS + j] > 0)
            def _(j=j):
                allowed = allowed_block(span_ref, base_ref[j], columns, chunk)
                keys = span_of(j)
                for h in range(len(heads)):
                    query, grad = q_s[h, :, columns], g_s[h, :, columns]
                    scores = dot(k_s[h, keys, :], query, 1, 0)
                    scores = jnp.where(allowed, scores, MASKED)
                    chances = jnp.exp(scores - lse_ref[0, h, :, columns])
                    steep = dot(v_s[h, keys, :], grad, 1, 0)
                    back = (chances * (steep - inner_s[h, :, columns])).astype(BF)
                    dv_s[h, :, keys] += dot(grad, chances.astype(BF), 1, 1)
                    dk_s[h, :, keys] += dot(query, back, 1, 1)
                    dq_s[h, :, columns] += dot(kt_s[h, :, keys], back, 1, 0)

    def store(half):
        for h, index in enumerate(heads):
            made = (dq_s[h] * SCALE, dk_s[h], dv_s[h])
            for (out, kind), value in zip(into, made):
                write_head(out, half, index, kind, value.astype(BF))

    for half in range(2):
        pl.when(half_now == half)(functools.partial(store, half))


def by_half(shape):
    rest = (0,) * (len(shape) - 1)
    return pl.BlockSpec((1,) + tuple(shape[1:]), lambda i, *_: (i,) + rest)


class Heads:
    def __init__(self, nx, ny, nz, chunk):
        self.nx, self.ny, self.nz, self.chunk = nx, ny, nz, chunk
        self.index = [(x, z) for x in range(nx) for z in range(nz // 2)]

    def split(self, matrix, kinds):
        nx, ny, nz = self.nx, self.ny, self.nz
        rows = HEAD_DIM // ny
        if nx == ny and rows % 16 == 0:
            return matrix.reshape(2, ny, nx, nz // 2, kinds, rows, LEN)
        half = matrix.shape[0] // 2
        first = matrix[:half].reshape(ny, nx, nz // 2, kinds, rows, LEN).transpose(1, 2, 3, 0, 4, 5)
        second = matrix[half:].reshape(nx, ny, nz // 2, kinds, rows, LEN).transpose(0, 2, 3, 1, 4, 5)
        both_halves = jnp.stack([first, second], 0)
        return both_halves.reshape(2, 1, nx, nz // 2, kinds, HEAD_DIM, LEN)

    def join(self, split):
        nx, ny, nz = self.nx, self.ny, self.nz
        rows = HEAD_DIM // ny
        if split.shape[5] == rows:
            return split.reshape(-1, LEN)
        kinds = split.shape[4]
        cut = split.reshape(2, nx, nz // 2, kinds, ny, rows, LEN)
        first = cut[0].transpose(3, 0, 1, 2, 4, 5).reshape(-1, LEN)
        second = cut[1].transpose(0, 3, 1, 2, 4, 5).reshape(-1, LEN)
        return jnp.concatenate([first, second], 0)

    def call(self, kernel, kinds, tables, arrays, outs, scratch, flops):
        need, bases, spans = tables
        return pl.pallas_call(
            functools.partial(kernel, self.index, kinds, self.chunk),
            out_shape=outs,
            grid_spec=pltpu.PrefetchScalarGridSpec(
                num_scalar_prefetch=2,
                grid=(2,),
                in_specs=[pl.BlockSpec((2, LEN), lambda i, *_: (0, 0))] + [by_half(a.shape) for a in arrays],
                out_specs=[by_half(o.shape) for o in outs],
                scratch_shapes=scratch,
            ),
            compiler_params=pltpu.CompilerParams(vmem_limit_bytes=48 * 2**20),
            cost_estimate=pl.CostEstimate(flops=flops, bytes_accessed=8 * 2**20, transcendentals=4 * 2**20),
        )(need, bases, spans, *arrays)

    def attend(self, tables, sources, kinds):
        count = len(self.index)
        split = [self.split(s, k) for s, k in zip(sources, kinds)]
        like = split[0].shape
        wide = (count, HEAD_DIM, LEN)
        mixed, lse = self.call(
            attend_kernel,
            kinds,
            tables,
            split,
            [
                jax.ShapeDtypeStruct(like[:4] + (1,) + like[5:], BF),
                jax.ShapeDtypeStruct((2, count, 1, LEN), F32),
            ],
            [
                pltpu.VMEM(wide, BF),
                pltpu.VMEM((count, LEN, HEAD_DIM), BF),
                pltpu.VMEM(wide, BF),
                pltpu.VMEM((count, 1, BLOCK), F32),
                pltpu.VMEM((count, 1, BLOCK), F32),
                pltpu.VMEM((count, HEAD_DIM, BLOCK), F32),
            ],
            8 * 10**9,
        )
        return self.join(mixed), lse

    def attend_back(self, tables, sources, kinds, mixed, grad, lse):
        count = len(self.index)
        split = [self.split(s, k) for s, k in zip(sources, kinds)]
        wide, tall = (count, HEAD_DIM, LEN), (count, LEN, HEAD_DIM)
        grads = self.call(
            attend_back_kernel,
            kinds,
            tables,
            split + [self.split(mixed, 1), self.split(grad, 1), lse],
            [jax.ShapeDtypeStruct(s.shape, BF) for s in split],
            [
                pltpu.VMEM(wide, BF),
                pltpu.VMEM(tall, BF),
                pltpu.VMEM(wide, BF),
                pltpu.VMEM(tall, BF),
                pltpu.VMEM(wide, BF),
                pltpu.VMEM((count, 1, LEN), F32),
                pltpu.VMEM(wide, F32),
                pltpu.VMEM(wide, F32),
                pltpu.VMEM(wide, F32),
            ],
            20 * 10**9,
        )
        return [self.join(g) for g in grads]


def body(
    inputs,
    memory,
    cotangent,
    tgt_lengths,
    src_ids,
    gain_one,
    w_query,
    w_key,
    w_value,
    w_out,
    gain_two,
    w_cross_query,
    w_mem_key,
    w_mem_value,
    w_cross_out,
    gain_three,
    w_up,
    w_down,
):
    nx, ny, nz = (lax.axis_size(a) for a in ("batch", "yy", "head"))
    ix, iy, core, iz = (lax.axis_index(a) for a in ("batch", "yy", "core", "head"))
    rows = inputs.shape[0]
    nxy, place = nx * ny, ix * ny + iy
    chunk = LEN // (2 * ny)

    def part(matrix):
        deep = matrix.shape[0] // 2 // nxy
        return lax.dynamic_slice_in_dim(matrix, (core * nxy + place) * deep, deep, 0)

    def column_part(matrix):
        wide = matrix.shape[1] // 2
        return lax.dynamic_slice_in_dim(
            lax.dynamic_slice_in_dim(matrix, core * wide, wide, 1).T, place * (wide // nxy), wide // nxy, 0
        )

    def gathered(*parts):
        piece = jnp.concatenate(parts, 0) if len(parts) > 1 else parts[0]
        first, second = gather_weight(piece)
        width = piece.shape[1]
        return jnp.concatenate([first.reshape(-1, width), second.reshape(-1, width)], 0)

    row = iy * nz + iz
    lengths = lax.dynamic_index_in_dim(tgt_lengths, row, 0, keepdims=False)
    source_ids = lax.dynamic_index_in_dim(src_ids, row, 0, keepdims=False)
    index = jnp.arange(LEN, dtype=jnp.int32)
    within = index % (LEN // 2)
    turn = jnp.where(index < LEN // 2, core, 1 - core)
    positions = (2 * (within // chunk) + turn) * chunk + within % chunk
    ends = jnp.cumsum(lengths)
    starts = ends - lengths
    reached = positions[:, None] >= starts[None, :]
    target_ids = jnp.sum(reached.astype(jnp.int32), -1) - 1
    self_start = jnp.max(jnp.where(reached, starts[None, :], 0), -1)
    kinds = jnp.arange(lengths.shape[0], dtype=jnp.int32)
    source_start = jnp.sum((source_ids[None, :] < kinds[:, None]).astype(jnp.int32), -1)
    source_end = jnp.sum((source_ids[None, :] <= kinds[:, None]).astype(jnp.int32), -1) - 1
    mine = target_ids[:, None] == kinds[None, :]
    cross_start = jnp.sum(jnp.where(mine, source_start[None, :], 0), -1)
    cross_end = jnp.sum(jnp.where(mine, source_end[None, :], 0), -1)
    block_positions = positions.reshape(BLOCKS, BLOCK)
    lowest, highest = jnp.min(block_positions, 1), jnp.max(block_positions, 1)

    def tables_of(start, end):
        least = jnp.min(start.reshape(BLOCKS, BLOCK), 1)
        most = jnp.max(end.reshape(BLOCKS, BLOCK), 1)
        need = (least[:, None] <= highest[None, :]) & (most[:, None] >= lowest[None, :])
        return need.astype(jnp.int32).reshape(-1), lowest, jnp.stack([start, end - start], 0)

    self_tables = tables_of(self_start, positions)
    cross_tables = tables_of(cross_start, cross_end)
    heads = Heads(nx, ny, nz, chunk)

    w_self = gathered(column_part(w_query), column_part(w_key), column_part(w_value))
    residual = to_row(inputs).astype(F32)
    w_o = gathered(part(w_out))
    w_mem = gathered(column_part(w_mem_key), column_part(w_mem_value))
    w_cq = gathered(column_part(w_cross_query))
    w_co = gathered(part(w_cross_out))
    w_u = gathered(column_part(w_up))
    w_d = gathered(part(w_down))
    source = both(to_row(memory))
    cot_own = to_row(cotangent)
    cot = both(cot_own)

    normed_one = both(normalize(residual, gain_one))
    qkv = dot(w_self, normed_one, 1, 1).astype(BF)
    mkv = dot(w_mem, source, 1, 1).astype(BF)
    self_mixed, self_lse = heads.attend(self_tables, (qkv,), (3,))
    after_self = residual + own_sum(self_mixed, w_o)
    normed_two = both(normalize(after_self, gain_two))
    cq = dot(w_cq, normed_two, 1, 1).astype(BF)
    cross_mixed, cross_lse = heads.attend(cross_tables, (cq, mkv), (1, 2))
    after_cross = after_self + own_sum(cross_mixed, w_co)
    normed_three = both(normalize(after_cross, gain_three))
    hidden_pre = dot(w_u, normed_three, 1, 1)
    hidden_act, gate_pull = jax.vjp(lambda p: jax.nn.gelu(p, approximate=True), hidden_pre)
    hidden_act = hidden_act.astype(BF)
    output = (after_cross + own_sum(hidden_act, w_d)).astype(BF)
    output = from_row(output, rows)

    def weight_sum(transposed, tokens):
        grads = dot(transposed, tokens, 1, 0).astype(BF)
        return sum_weight(grads, grads.shape[0] // (nxy * nz))

    g_down = weight_sum(hidden_act, cot)
    grad_pre = gate_pull(dot(w_d, cot, 1, 1))[0].astype(BF)
    g_up = weight_sum(grad_pre, normed_three)
    step, grad_gain_three = normalize_back(after_cross, gain_three, own_sum(grad_pre, w_u))
    grad_after_cross = cot_own.astype(F32) + step

    cross_grad = both(grad_after_cross.astype(BF))
    g_co = weight_sum(cross_mixed, cross_grad)
    grad_cross_mixed = dot(w_co, cross_grad, 1, 1).astype(BF)
    gcq, gmkv = heads.attend_back(
        cross_tables, (cq, mkv), (1, 2), cross_mixed, grad_cross_mixed, cross_lse
    )
    g_cq = weight_sum(gcq, normed_two)
    g_mem = weight_sum(gmkv, source)
    grad_memory = from_row(own_sum(gmkv, w_mem).astype(BF), rows).astype(F32)
    step, grad_gain_two = normalize_back(after_self, gain_two, own_sum(gcq, w_cq))
    grad_after_self = grad_after_cross + step

    self_grad = both(grad_after_self.astype(BF))
    g_o = weight_sum(self_mixed, self_grad)
    grad_self_mixed = dot(w_o, self_grad, 1, 1).astype(BF)
    (gqkv,) = heads.attend_back(self_tables, (qkv,), (3,), self_mixed, grad_self_mixed, self_lse)
    g_self = weight_sum(gqkv, normed_one)
    step, grad_gain_one = normalize_back(residual, gain_one, own_sum(gqkv, w_self))
    grad_inputs = from_row((grad_after_self + step).astype(BF), rows).astype(F32)
    gains = total_of(jnp.stack([grad_gain_one, grad_gain_two, grad_gain_three]))

    def tall(grads):
        return replicate(grads).reshape(-1, grads.shape[1]).astype(F32)

    def columns(grads, count):
        whole = replicate(grads)
        whole = whole.reshape(whole.shape[:3] + (count, -1, grads.shape[1]))
        return [whole[:, :, :, i].reshape(-1, grads.shape[1]).T.astype(F32) for i in range(count)]

    grad_q, grad_k, grad_v = columns(g_self, 3)
    grad_mk, grad_mv = columns(g_mem, 2)
    return (
        output,
        grad_inputs,
        grad_memory,
        gains[0],
        grad_q,
        grad_k,
        grad_v,
        tall(g_o),
        gains[1],
        columns(g_cq, 1)[0],
        grad_mk,
        grad_mv,
        tall(g_co),
        gains[2],
        columns(g_up, 1)[0],
        tall(g_down),
    )


def solution(mesh):
    nb, ns, nh = (mesh.shape[a] for a in ("batch", "seq", "head"))
    fine = Mesh(mesh.devices.reshape(nb, ns // 2, 2, nh), ("batch", "yy", "core", "head"))
    tokens = P("batch", ("yy", "core", "head"), None)
    ids = P("batch", None)
    wide, tall = P(None, "head"), P("head", None)
    return jax.shard_map(
        body,
        mesh=fine,
        in_specs=(
            tokens, tokens, tokens, ids, ids,
            P(), wide, wide, wide, tall,
            P(), wide, wide, wide, tall,
            P(), wide, tall,
        ),
        out_specs=(
            tokens, tokens, tokens,
            P(), wide, wide, wide, tall,
            P(), wide, wide, wide, tall,
            P(), wide, tall,
        ),
        check_vma=False,
    )
```

time: 1250 us -> 859 us (0.69)
  blocking collectives: 231 us -> 0 us
  starting transfers between devices: 119 us -> 305 us
  matrix products: 292 us -> 110 us
  local copies, waits for them, and re-layouts: 187 us -> 53.4 us
  Pallas kernels: 0 us -> 79.4 us
  waiting for transfers between devices: 250 us -> 200 us
  other arithmetic: 149 us -> 101 us
  between operations: 15.9 us -> 3.29 us
    ppermute x49 -> x138, starting transfers between devices: 58.6 us -> 272 us  [the longest x133 267 us: shift(): lax.ppermute(piece, axis, [(i, (i + step) % count) for i in range(count)])]
    dot_general x21 -> x0, matrix products: 207 us -> none  [the longest x2 43 us: attend_back(): jnp.einsum('qhe,khe->hqk', grad, values, preferred_element_type=F32)]
    all_gather x20 -> x0, blocking collectives: 186 us -> none  [the longest x5 87.1 us: gather_weight(): along = lax.all_gather(piece, 'head', axis=0, tiled=False)]
    all_gather x15 -> x0, waiting for transfers between devices: 146 us -> none  [the longest x11 138 us: gather_weight(): along = lax.all_gather(along, axis, axis=1, tiled=False)]
    ppermute x49 -> x138, waiting for transfers between devices: 59.8 us -> 198 us  [the longest x133 177 us: shift(): lax.ppermute(piece, axis, [(i, (i + step) % count) for i in range(count)])]
    pallas_call x0 -> x4, Pallas kernels: none -> 79.4 us  [call(): pl.pallas_call(functools.partial(kernel, self.index, kinds, self.chunk),...]
    dot_general x9 -> x28, matrix products: 45.4 us -> 110 us  [dot(): lax.dot_general(left, right, (((left_dim,), (right_dim,)), ((), ())), pre...]
    another operation x2 -> x88, other arithmetic: 0.05 us -> 62.5 us  [the longest x44 46.5 us: ring(): jnp.stack([piece] + [shift(piece, axis, k) for k in range(1, count)], 0)]
  transfers between devices with their start and end apart: 77 -> 144, of which waited for: 20 -> 37; matrix products, arithmetic and copies ran while one was open for 45% -> 27% of each run, Pallas kernels for 0% -> 9%
where the time goes in v2:
time: 859 us; the launch traced here: 853 us
  starting transfers between devices  305 us (36%)
  waiting for transfers between devices  200 us (23%)
  matrix products  110 us (13%)
  other arithmetic  101 us (12%)
  Pallas kernels  79.4 us (9%)
  local copies, waits for them, and re-layouts  53.4 us (6%)
    ppermute x133, starting transfers between devices, shift(): lax.ppermute(piece, axis, [(i, (i + step) % count) for i in range(count)])  267 us
    ppermute x133, waiting for transfers between devices, shift(): lax.ppermute(piece, axis, [(i, (i + step) % count) for i in range(count)])  177 us
    dot_general x28, matrix products, dot(): lax.dot_general(left, right, (((left_dim,), (right_dim,)), ((), ())), pre...  110 us
    pallas_call x4, Pallas kernels, call(): pl.pallas_call(functools.partial(kernel, self.index, kinds, self.chunk),...  79.4 us
    another operation x44, other arithmetic, ring(): jnp.stack([piece] + [shift(piece, axis, k) for k in range(1, count)], 0)  46.5 us
    unnamed x222, local copies, waits for them, and re-layouts  24.2 us
    ppermute x5, waiting for transfers between devices, total_of(): lax.ppermute(value, axis, [(i, i ^ step) for i in range(count)])  21.8 us
  transfers between devices with their start and end apart: 144, of which 37 were waited for; matrix products, arithmetic and copies ran while one was open for 27% of the time, Pallas kernels for 9%

profile of v2, /device:TPU:1, one launch (start us, length us, event | category | flops | bytes accessed | tf_op | source)
XLA Modules:
  0.0 852.6 jit_solution(13150137308041583486)
XLA Ops:
  61.6 8.0 all-to-all-start.1
  70.8 12.0 %collective-permute-start.7 = (bf16[512,1024]{1,0:T(8,128)(2,1)S(1)}, bf16[512,1024]{1,0:T(8,128)(2,1)S(1)}, u32[]{:S(2)}, u32[]{:S(2)}) collective-permute-start(bf16[512,1024]{1,0:T(8,128)(2,1)S(1)} %fusion.26), channel_id=1, source_target_pairs={{0,4},{4,0},{1,5},{5,1},{2,6},{6,2},{3,7},{7,3},{8,12},{12,8},{9,1... | collective-permute-start | bytes 3145736 | tf_op jit(solution)/shard_map/ppermute | solution.py:49
  105.4 8.2 collective-permute-done.14
  126.1 18.9 %shard_map.297 = (bf16[2,2,2,2,1,32,1024]{6,5,4,3,2,1,0:T(8,128)(2,1)S(1)}, f32[2,4,1,1024]{3,2,1,0:T(1,128)S(1)}) custom-call(s32[16]{0:T(128)S(1)} %reshape.633.need_ref, s32[4]{0:T(128)S(1)} %fusion.147.base_ref, s32[2,1024]{1,0:T(2,128)S(1)} %pad_add_fusion.span_ref, bf16[2,2,2,2,3,32,1024]{6,5,4,3,2,1,0:T(8,128)(2,1)S(1)} %bitcast.546), custom_call_target="tpu_custom_call" | custom-call | flops 8000000000 | bytes 8388608 | tf_op jit(solution)/shard_map/pallas_call | solution.py:304
  163.4 6.8 collective-permute-start.31
  182.7 7.8 collective-permute-start.51
  203.2 19.1 %shard_map.298 = (bf16[2,2,2,2,1,32,1024]{6,5,4,3,2,1,0:T(8,128)(2,1)S(1)}, f32[2,4,1,1024]{3,2,1,0:T(1,128)S(1)}) custom-call(s32[16]{0:T(128)S(1)} %reshape.634.need_ref, s32[4]{0:T(128)S(1)} %fusion.147.base_ref, s32[2,1024]{1,0:T(2,128)S(1)} %pad_add_fusion.1.span_ref, bf16[2,2,2,2,1,32,1024]{6,5,4,3,2,1,0:T(8,128)(2,1)S(1)} %bitcast.559, ...), custom_call_target="tpu_custom_call" | custom-call | flops 8000000000 | bytes 8388608 | tf_op jit(solution)/shard_map/pallas_call | solution.py:304
  235.0 14.8 %collective-permute-done.40 = bf16[128,1024]{1,0:T(8,128)(2,1)S(1)} collective-permute-done((bf16[128,1024]{1,0:T(8,128)(2,1)S(1)}, bf16[128,1024]{1,0:T(8,128)(2,1)S(1)}, u32[]{:S(2)}, u32[]{:S(2)}) %collective-permute-start.40) | collective-permute-done | bytes 262176 | tf_op jit(solution)/shard_map/ppermute | solution.py:49
  279.6 12.7 %collective-permute-done.50 = bf16[2,2,128,1024]{3,2,1,0:T(8,128)(2,1)} collective-permute-done((bf16[2,2,128,1024]{3,2,1,0:T(8,128)(2,1)}, bf16[2,2,128,1024]{3,2,1,0:T(8,128)(2,1)}, u32[]{:S(2)}, u32[]{:S(2)}) %collective-permute-start.50) | collective-permute-done | bytes 1048608 | tf_op jit(solution)/shard_map/ppermute | solution.py:49
  299.0 7.5 collective-permute-done.46
  308.1 6.7 collective-permute-done.42
  316.2 11.5 %multiply_convert_fusion = (bf16[2048,1024]{1,0:T(8,128)(2,1)S(1)}, f32[2048,1024]{1,0:T(8,128)}) fusion(bf16[512,1024]{1,0:T(8,128)(2,1)} %collective-permute-done.47, bf16[512,1024]{1,0:T(8,128)(2,1)} %multiply_convert_fusion.1, bf16[1024,1024]{1,0:T(8,128)(2,1)S(1)} %bitcast.587, bf16[1024,1024]{1,0:T(8,128)(2,1)S(1)} %bitcast.590), kind=kOutput, calls=%fused_computation.9 | convolution fusion | flops 4326424576 | bytes 18874368 | tf_op jit(solution)/shard_map/dot_general | solution.py:23
  327.7 16.2 %fusion.6 = bf16[2048,1024]{1,0:T(8,128)(2,1)} fusion(f32[2048,1024]{1,0:T(8,128)} %get-tuple-element.254, bf16[512,1024]{1,0:T(8,128)(2,1)S(1)} %collective-permute-done.56, bf16[512,1024]{1,0:T(8,128)(2,1)S(1)} %bitcast.564, bf16[1024,1024]{1,0:T(8,128)(2,1)S(1)} %bitcast.584, bf16[1024,1024]{1,0:T(8,128)(2,1)S(1)} %bitcast.581), kind=kOutput, calls=%fused_computation.8 | convolution fusion | flops 4349493248 | bytes 18874368 | tf_op jit(solution)/shard_map/dot_general | solution.py:23
  359.9 7.3 convolution_convert_fusion.3
  368.4 14.5 %collective-permute-done.131 = bf16[2,2,128,1024]{3,2,1,0:T(8,128)(2,1)S(1)} collective-permute-done((bf16[2,2,128,1024]{3,2,1,0:T(8,128)(2,1)S(1)}, bf16[2,2,128,1024]{3,2,1,0:T(8,128)(2,1)S(1)}, u32[]{:S(2)}, u32[]{:S(2)}) %collective-permute-start.131) | collective-permute-done | bytes 1048608 | tf_op jit(solution)/shard_map/ppermute | solution.py:49
  393.5 11.8 %collective-permute-done.121 = bf16[2,2,128,1024]{3,2,1,0:T(8,128)(2,1)S(1)} collective-permute-done((bf16[2,2,128,1024]{3,2,1,0:T(8,128)(2,1)S(1)}, bf16[2,2,128,1024]{3,2,1,0:T(8,128)(2,1)S(1)}, u32[]{:S(2)}, u32[]{:S(2)}) %collective-permute-start.121) | collective-permute-done | bytes 1048608 | tf_op jit(solution)/shard_map/ppermute | solution.py:49
  407.9 9.6 %collective-permute-done.132 = bf16[2,128,1024]{2,1,0:T(8,128)(2,1)S(1)} collective-permute-done((bf16[2,128,1024]{2,1,0:T(8,128)(2,1)S(1)}, bf16[2,128,1024]{2,1,0:T(8,128)(2,1)S(1)}, u32[]{:S(2)}, u32[]{:S(2)}) %collective-permute-start.132) | collective-permute-done | bytes 524320 | tf_op jit(solution)/shard_map/ppermute | solution.py:49
  418.6 16.0 %collective-permute-start.133 = (bf16[128,1024]{1,0:T(8,128)(2,1)S(1)}, bf16[128,1024]{1,0:T(8,128)(2,1)S(1)}, u32[]{:S(2)}, u32[]{:S(2)}) collective-permute-start(bf16[128,1024]{1,0:T(8,128)(2,1)S(1)} %get-tuple-element.156), channel_id=1, source_target_pairs={{0,2},{1,3},{2,0},{3,1},{4,6},{5,7},{6,4},{7,5},{8,10},{9,11},{10,... | collective-permute-start | bytes 786440 | tf_op jit(solution)/shard_map/ppermute | solution.py:49
  435.6 8.0 collective-permute-start.134
  449.9 8.8 %collective-permute-start.120 = (bf16[128,1024]{1,0:T(8,128)(2,1)}, bf16[128,1024]{1,0:T(8,128)(2,1)}, u32[]{:S(2)}, u32[]{:S(2)}) collective-permute-start(bf16[128,1024]{1,0:T(8,128)(2,1)} %slice_bitcast_fusion.18), channel_id=1, source_target_pairs={{0,3},{1,0},{2,1},{3,2},{4,7},{5,4},{6,5},{7,6},{8,11},{9,8},{10,9... | collective-permute-start | bytes 786440 | tf_op jit(solution)/shard_map/ppermute | solution.py:49
  478.7 21.1 %shard_map.299 = (bf16[2,2,2,2,1,32,1024]{6,5,4,3,2,1,0:T(8,128)(2,1)S(1)}, bf16[2,2,2,2,2,32,1024]{6,5,4,3,2,1,0:T(8,128)(2,1)}) custom-call(s32[16]{0:T(128)S(1)} %reshape.634.need_ref, s32[4]{0:T(128)S(1)} %fusion.147.base_ref, s32[2,1024]{1,0:T(2,128)S(1)} %pad_add_fusion.1.span_ref, bf16[2,2,2,2,1,32,1024]{6,5,4,3,2,1,0:T(8,128)(2,1)S(1)} %bitcast.560, ...), custom_call_target="tpu_custom_call" | custom-call | flops 20000000000 | bytes 8388608 | tf_op jit(solution)/shard_map/pallas_call | solution.py:304
  514.8 5.8 collective-permute-start.108
  529.7 11.2 %collective-permute-done.112 = bf16[2,32,1024]{2,1,0:T(8,128)(2,1)S(1)} collective-permute-done((bf16[2,32,1024]{2,1,0:T(8,128)(2,1)S(1)}, bf16[2,32,1024]{2,1,0:T(8,128)(2,1)S(1)}, u32[]{:S(2)}, u32[]{:S(2)}) %collective-permute-start.112) | collective-permute-done | bytes 131104 | tf_op jit(solution)/shard_map/ppermute | solution.py:49
  543.7 35.1 %collective-permute-start.113 = (bf16[32,1024]{1,0:T(8,128)(2,1)S(1)}, bf16[32,1024]{1,0:T(8,128)(2,1)S(1)}, u32[]{:S(2)}, u32[]{:S(2)}) collective-permute-start(bf16[32,1024]{1,0:T(8,128)(2,1)S(1)} %get-tuple-element.220), channel_id=1, source_target_pairs={{0,2},{1,3},{2,0},{3,1},{4,6},{5,7},{6,4},{7,5},{8,10},{9,11},{10,... | collective-permute-start | bytes 196616 | tf_op jit(solution)/shard_map/ppermute | solution.py:49
  587.3 7.4 collective-permute-start.59
  608.4 8.8 %collective-permute-done.126 = bf16[2,128,1024]{2,1,0:T(8,128)(2,1)S(1)} collective-permute-done((bf16[2,128,1024]{2,1,0:T(8,128)(2,1)S(1)}, bf16[2,128,1024]{2,1,0:T(8,128)(2,1)S(1)}, u32[]{:S(2)}, u32[]{:S(2)}) %collective-permute-start.126) | collective-permute-done | bytes 524320 | tf_op jit(solution)/shard_map/ppermute | solution.py:49
  688.3 20.4 %shard_map.300 = bf16[2,2,2,2,3,32,1024]{6,5,4,3,2,1,0:T(8,128)(2,1)S(1)} custom-call(s32[16]{0:T(128)S(1)} %reshape.633.need_ref, s32[4]{0:T(128)S(1)} %fusion.147.base_ref, s32[2,1024]{1,0:T(2,128)S(1)} %pad_add_fusion.span_ref, bf16[2,2,2,2,3,32,1024]{6,5,4,3,2,1,0:T(8,128)(2,1)} %bitcast.547, bf16[2,2,2,2,1,32,1024]{6,5,4,3,2,1,0:T(8,128)(2,1)S(1)} %copy-done.7, ...), custom_call_target="tpu_custom_call" | custom-call | flops 20000000000 | bytes 8388608 | tf_op jit(solution)/shard_map/pallas_call | solution.py:304
  740.5 9.1 %collective-permute-done.86 = bf16[2,32,1024]{2,1,0:T(8,128)(2,1)S(1)} collective-permute-done((bf16[2,32,1024]{2,1,0:T(8,128)(2,1)S(1)}, bf16[2,32,1024]{2,1,0:T(8,128)(2,1)S(1)}, u32[]{:S(2)}, u32[]{:S(2)}) %collective-permute-start.86) | collective-permute-done | bytes 131104 | tf_op jit(solution)/shard_map/ppermute | solution.py:49
  773.9 11.3 %collective-permute-done.73 = bf16[96,1024]{1,0:T(8,128)(2,1)S(1)} collective-permute-done((bf16[96,1024]{1,0:T(8,128)(2,1)S(1)}, bf16[96,1024]{1,0:T(8,128)(2,1)S(1)}, u32[]{:S(2)}, u32[]{:S(2)}) %collective-permute-start.73) | collective-permute-done | bytes 196640 | tf_op jit(solution)/shard_map/ppermute | solution.py:49
  793.1 6.4 collective-permute-done.76
  805.9 7.0 all-to-all-start.4
  814.5 18.1 %collective-permute-done.66 = f32[3,1024]{1,0:T(4,128)S(1)} collective-permute-done((f32[3,1024]{1,0:T(4,128)S(1)}, f32[3,1024]{1,0:T(4,128)S(1)}, u32[]{:S(2)}, u32[]{:S(2)}) %collective-permute-start.66) | collective-permute-done | bytes 12320 | tf_op jit(solution)/shard_map/ppermute | solution.py:130
  (745 shorter events, 461.5 us)
Async XLA Ops:
  2.3 46.7 %collective-permute-start.35 = (bf16[32,1024]{1,0:T(8,128)(2,1)}, bf16[32,1024]{1,0:T(8,128)(2,1)}, u32[]{:S(2)}, u32[]{:S(2)}) collective-permute-start(bf16[32,1024]{1,0:T(8,128)(2,1)} %constant_dynamic-slice_fusion.2), channel_id=1, source_target_pairs={{0,2},{1,3},{2,0},{3,1},{4,6},{5,7},{6,4},{7,5},{8,10},{9,11},{10,... | collective-permute-start | bytes 196616 | tf_op jit(solution)/shard_map/ppermute | solution.py:49
  5.4 47.3 %collective-permute-start.32 = (bf16[32,1024]{1,0:T(8,128)(2,1)}, bf16[32,1024]{1,0:T(8,128)(2,1)}, u32[]{:S(2)}, u32[]{:S(2)}) collective-permute-start(bf16[32,1024]{1,0:T(8,128)(2,1)} %constant_dynamic-slice_fusion.2), channel_id=1, source_target_pairs={{0,1},{1,2},{2,3},{3,0},{4,5},{5,6},{6,7},{7,4},{8,9},{9,10},{10,1... | collective-permute-start | bytes 196616 | tf_op jit(solution)/shard_map/ppermute | solution.py:49
  10.3 51.3 %all-to-all-start = ((bf16[8,64,1024]{2,1,0:T(8,128)(2,1)}), bf16[8,64,1024]{2,1,0:T(8,128)(2,1)S(1)}, u32[]{:S(2)}, u32[]{:S(2)}) async-start(bf16[8,64,1024]{2,1,0:T(8,128)(2,1)} %param.18), calls=%async_computation | async-start | bytes 2097152 | tf_op jit(solution)/shard_map/all_to_all | solution.py:68
  57.0 39.0 %collective-permute-start.13 = (bf16[2,32,1024]{2,1,0:T(8,128)(2,1)}, bf16[2,32,1024]{2,1,0:T(8,128)(2,1)}, u32[]{:S(2)}, u32[]{:S(2)}) collective-permute-start(bf16[2,32,1024]{2,1,0:T(8,128)(2,1)} %get-tuple-element.243), channel_id=1, source_target_pairs={{0,8},{8,0},{1,9},{9,1},{2,10},{10,2},{3,11},{11,3},{4,12},{12,4},... | collective-permute-start | bytes 393224 | tf_op jit(solution)/shard_map/ppermute | solution.py:49
  60.3 53.7 %collective-permute-start.2 = (bf16[2,2,96,1024]{3,2,1,0:T(8,128)(2,1)}, bf16[2,2,96,1024]{3,2,1,0:T(8,128)(2,1)}, u32[]{:S(2)}, u32[]{:S(2)}) collective-permute-start(bf16[2,2,96,1024]{3,2,1,0:T(8,128)(2,1)} %get-tuple-element.151), channel_id=1, source_target_pairs={{0,8},{8,0},{1,9},{9,1},{2,10},{10,2},{3,11},{11,3},{4,12},{12,4},... | collective-permute-start | bytes 2359304 | tf_op jit(solution)/shard_map/ppermute | solution.py:49
  61.6 101.7 %all-to-all-start.1 = ((bf16[8,64,1024]{2,1,0:T(8,128)(2,1)}), bf16[8,64,1024]{2,1,0:T(8,128)(2,1)}, u32[]{:S(2)}, u32[]{:S(2)}) async-start(bf16[8,64,1024]{2,1,0:T(8,128)(2,1)} %param.19), calls=%async_computation.1 | async-start | bytes 2097152 | tf_op jit(solution)/shard_map/all_to_all | solution.py:68
  70.8 48.7 %collective-permute-start.7 = (bf16[512,1024]{1,0:T(8,128)(2,1)S(1)}, bf16[512,1024]{1,0:T(8,128)(2,1)S(1)}, u32[]{:S(2)}, u32[]{:S(2)}) collective-permute-start(bf16[512,1024]{1,0:T(8,128)(2,1)S(1)} %fusion.26), channel_id=1, source_target_pairs={{0,4},{4,0},{1,5},{5,1},{2,6},{6,2},{3,7},{7,3},{8,12},{12,8},{9,1... | collective-permute-start | bytes 3145736 | tf_op jit(solution)/shard_map/ppermute | solution.py:49
  104.4 42.3 %collective-permute-start.27 = (bf16[64,1024]{1,0:T(8,128)(2,1)S(1)}, bf16[64,1024]{1,0:T(8,128)(2,1)S(1)}, u32[]{:S(2)}, u32[]{:S(2)}) collective-permute-start(bf16[64,1024]{1,0:T(8,128)(2,1)S(1)} %copy-done.78), channel_id=1, source_target_pairs={{0,2},{1,3},{2,0},{3,1},{4,6},{5,7},{6,4},{7,5},{8,10},{9,11},{10,... | collective-permute-start | bytes 393224 | tf_op jit(solution)/shard_map/ppermute | solution.py:49
  118.9 38.8 %collective-permute-start.48 = (bf16[128,1024]{1,0:T(8,128)(2,1)S(1)}, bf16[128,1024]{1,0:T(8,128)(2,1)S(1)}, u32[]{:S(2)}, u32[]{:S(2)}) collective-permute-start(bf16[128,1024]{1,0:T(8,128)(2,1)S(1)} %copy-done.75), channel_id=1, source_target_pairs={{0,1},{1,2},{2,3},{3,0},{4,5},{5,6},{6,7},{7,4},{8,9},{9,10},{10,1... | collective-permute-start | bytes 786440 | tf_op jit(solution)/shard_map/ppermute | solution.py:49
  182.7 41.4 %collective-permute-start.51 = (bf16[128,1024]{1,0:T(8,128)(2,1)S(1)}, bf16[128,1024]{1,0:T(8,128)(2,1)S(1)}, u32[]{:S(2)}, u32[]{:S(2)}) collective-permute-start(bf16[128,1024]{1,0:T(8,128)(2,1)S(1)} %copy-done.76), channel_id=1, source_target_pairs={{0,2},{1,3},{2,0},{3,1},{4,6},{5,7},{6,4},{7,5},{8,10},{9,11},{10,... | collective-permute-start | bytes 786440 | tf_op jit(solution)/shard_map/ppermute | solution.py:49
  192.5 38.6 %collective-permute-start.43 = (bf16[128,1024]{1,0:T(8,128)(2,1)S(1)}, bf16[128,1024]{1,0:T(8,128)(2,1)S(1)}, u32[]{:S(2)}, u32[]{:S(2)}) collective-permute-start(bf16[128,1024]{1,0:T(8,128)(2,1)S(1)} %bitcast.611), channel_id=1, source_target_pairs={{0,2},{1,3},{2,0},{3,1},{4,6},{5,7},{6,4},{7,5},{8,10},{9,11},{10,... | collective-permute-start | bytes 786440 | tf_op jit(solution)/shard_map/ppermute | solution.py:49
  195.7 38.2 %collective-permute-start.44 = (bf16[128,1024]{1,0:T(8,128)(2,1)S(1)}, bf16[128,1024]{1,0:T(8,128)(2,1)S(1)}, u32[]{:S(2)}, u32[]{:S(2)}) collective-permute-start(bf16[128,1024]{1,0:T(8,128)(2,1)S(1)} %bitcast.612), channel_id=1, source_target_pairs={{0,3},{1,0},{2,1},{3,2},{4,7},{5,4},{6,5},{7,6},{8,11},{9,8},{10,9... | collective-permute-start | bytes 786440 | tf_op jit(solution)/shard_map/ppermute | solution.py:49
  201.3 54.9 %collective-permute-start.49 = (bf16[2,128,1024]{2,1,0:T(8,128)(2,1)}, bf16[2,128,1024]{2,1,0:T(8,128)(2,1)}, u32[]{:S(2)}, u32[]{:S(2)}) collective-permute-start(bf16[2,128,1024]{2,1,0:T(8,128)(2,1)} %get-tuple-element.171), channel_id=1, source_target_pairs={{0,16},{16,0},{1,17},{17,1},{2,18},{18,2},{3,19},{19,3},{4,20},{20... | collective-permute-start | bytes 1572872 | tf_op jit(solution)/shard_map/ppermute | solution.py:49
  227.4 42.2 %collective-permute-start.39 = (bf16[512,1024]{1,0:T(8,128)(2,1)}, bf16[512,1024]{1,0:T(8,128)(2,1)}, u32[]{:S(2)}, u32[]{:S(2)}) collective-permute-start(bf16[512,1024]{1,0:T(8,128)(2,1)} %convolution_convert_fusion.14), channel_id=1, source_target_pairs={{0,4},{4,0},{1,5},{5,1},{2,6},{6,2},{3,7},{7,3},{8,12},{12,8},{9,1... | collective-permute-start | bytes 3145736 | tf_op jit(solution)/shard_map/ppermute | solution.py:49
  266.2 40.3 %collective-permute-start.46 = (bf16[2,2,128,1024]{3,2,1,0:T(8,128)(2,1)}, bf16[2,2,128,1024]{3,2,1,0:T(8,128)(2,1)}, u32[]{:S(2)}, u32[]{:S(2)}) collective-permute-start(bf16[2,2,128,1024]{3,2,1,0:T(8,128)(2,1)} %get-tuple-element.147), channel_id=1, source_target_pairs={{0,16},{16,0},{1,17},{17,1},{2,18},{18,2},{3,19},{19,3},{4,20},{20... | collective-permute-start | bytes 3145736 | tf_op jit(solution)/shard_map/ppermute | solution.py:49
  269.5 45.3 %collective-permute-start.42 = (bf16[2,2,128,1024]{3,2,1,0:T(8,128)(2,1)}, bf16[2,2,128,1024]{3,2,1,0:T(8,128)(2,1)}, u32[]{:S(2)}, u32[]{:S(2)}) collective-permute-start(bf16[2,2,128,1024]{3,2,1,0:T(8,128)(2,1)} %get-tuple-element.145), channel_id=1, source_target_pairs={{0,8},{8,0},{1,9},{9,1},{2,10},{10,2},{3,11},{11,3},{4,12},{12,4},... | collective-permute-start | bytes 3145736 | tf_op jit(solution)/shard_map/ppermute | solution.py:49
  273.7 42.5 %collective-permute-start.47 = (bf16[512,1024]{1,0:T(8,128)(2,1)}, bf16[512,1024]{1,0:T(8,128)(2,1)}, u32[]{:S(2)}, u32[]{:S(2)}) collective-permute-start(bf16[512,1024]{1,0:T(8,128)(2,1)} %multiply_convert_fusion.1), channel_id=1, source_target_pairs={{0,4},{4,0},{1,5},{5,1},{2,6},{6,2},{3,7},{7,3},{8,12},{12,8},{9,1... | collective-permute-start | bytes 3145736 | tf_op jit(solution)/shard_map/ppermute | solution.py:49
  350.3 96.2 %collective-permute-start.55 = (bf16[512,1024]{1,0:T(8,128)(2,1)S(1)}, bf16[512,1024]{1,0:T(8,128)(2,1)S(1)}, u32[]{:S(2)}, u32[]{:S(2)}) collective-permute-start(bf16[512,1024]{1,0:T(8,128)(2,1)S(1)} %fusion.44), channel_id=1, source_target_pairs={{0,4},{4,0},{1,5},{5,1},{2,6},{6,2},{3,7},{7,3},{8,12},{12,8},{9,1... | collective-permute-start | bytes 3145736 | tf_op jit(solution)/shard_map/ppermute | solution.py:49
  367.7 37.6 %collective-permute-start.121 = (bf16[2,2,128,1024]{3,2,1,0:T(8,128)(2,1)S(1)}, bf16[2,2,128,1024]{3,2,1,0:T(8,128)(2,1)S(1)}, u32[]{:S(2)}, u32[]{:S(2)}) collective-permute-start(bf16[2,2,128,1024]{3,2,1,0:T(8,128)(2,1)S(1)} %bitcast.622), channel_id=1, source_target_pairs={{0,16},{16,0},{1,17},{17,1},{2,18},{18,2},{3,19},{19,3},{4,20},{20... | collective-permute-start | bytes 3145736 | tf_op jit(solution)/shard_map/ppermute | solution.py:49
  405.3 70.4 %collective-permute-start.58 = (bf16[512,1024]{1,0:T(8,128)(2,1)}, bf16[512,1024]{1,0:T(8,128)(2,1)}, u32[]{:S(2)}, u32[]{:S(2)}) collective-permute-start(bf16[512,1024]{1,0:T(8,128)(2,1)} %get-tuple-element.93), channel_id=1, source_target_pairs={{0,4},{4,0},{1,5},{5,1},{2,6},{6,2},{3,7},{7,3},{8,12},{12,8},{9,1... | collective-permute-start | bytes 3145736 | tf_op jit(solution)/shard_map/ppermute | solution.py:49
  462.0 168.9 %all-to-all-start.2 = ((bf16[8,64,1024]{2,1,0:T(8,128)(2,1)}), bf16[8,64,1024]{2,1,0:T(8,128)(2,1)}, u32[]{:S(2)}, u32[]{:S(2)}) async-start(bf16[8,64,1024]{2,1,0:T(8,128)(2,1)} %bitcast.609), calls=%async_computation.2 | async-start | bytes 2097152 | tf_op jit(solution)/shard_map/all_to_all | solution.py:74
  467.7 54.1 %collective-permute-start.135 = (bf16[128,1024]{1,0:T(8,128)(2,1)S(1)}, bf16[128,1024]{1,0:T(8,128)(2,1)S(1)}, u32[]{:S(2)}, u32[]{:S(2)}) collective-permute-start(bf16[128,1024]{1,0:T(8,128)(2,1)S(1)} %fusion.89), channel_id=1, source_target_pairs={{0,8},{8,0},{1,9},{9,1},{2,10},{10,2},{3,11},{11,3},{4,12},{12,4},... | collective-permute-start | bytes 786440 | tf_op jit(solution)/shard_map/ppermute | solution.py:49
  475.6 46.2 %collective-permute-start.125 = (bf16[128,1024]{1,0:T(8,128)(2,1)S(1)}, bf16[128,1024]{1,0:T(8,128)(2,1)S(1)}, u32[]{:S(2)}, u32[]{:S(2)}) collective-permute-start(bf16[128,1024]{1,0:T(8,128)(2,1)S(1)} %fusion.92), channel_id=1, source_target_pairs={{0,8},{8,0},{1,9},{9,1},{2,10},{10,2},{3,11},{11,3},{4,12},{12,4},... | collective-permute-start | bytes 786440 | tf_op jit(solution)/shard_map/ppermute | solution.py:49
  521.8 77.5 %collective-permute-start.101 = (bf16[2,2,64,1024]{3,2,1,0:T(8,128)(2,1)S(1)}, bf16[2,2,64,1024]{3,2,1,0:T(8,128)(2,1)S(1)}, u32[]{:S(2)}, u32[]{:S(2)}) collective-permute-start(bf16[2,2,64,1024]{3,2,1,0:T(8,128)(2,1)S(1)} %bitcast.642), channel_id=1, source_target_pairs={{0,16},{16,0},{1,17},{17,1},{2,18},{18,2},{3,19},{19,3},{4,20},{20... | collective-permute-start | bytes 1572872 | tf_op jit(solution)/shard_map/ppermute | solution.py:49
  522.4 80.9 %collective-permute-start.98 = (bf16[2,2,64,1024]{3,2,1,0:T(8,128)(2,1)S(1)}, bf16[2,2,64,1024]{3,2,1,0:T(8,128)(2,1)S(1)}, u32[]{:S(2)}, u32[]{:S(2)}) collective-permute-start(bf16[2,2,64,1024]{3,2,1,0:T(8,128)(2,1)S(1)} %bitcast.641), channel_id=1, source_target_pairs={{0,8},{8,0},{1,9},{9,1},{2,10},{10,2},{3,11},{11,3},{4,12},{12,4},... | collective-permute-start | bytes 1572872 | tf_op jit(solution)/shard_map/ppermute | solution.py:49
  528.9 50.0 %collective-permute-start.109 = (bf16[2,32,1024]{2,1,0:T(8,128)(2,1)S(1)}, bf16[2,32,1024]{2,1,0:T(8,128)(2,1)S(1)}, u32[]{:S(2)}, u32[]{:S(2)}) collective-permute-start(bf16[2,32,1024]{2,1,0:T(8,128)(2,1)S(1)} %slice_bitcast_fusion.30), channel_id=1, source_target_pairs={{0,16},{16,0},{1,17},{17,1},{2,18},{18,2},{3,19},{19,3},{4,20},{20... | collective-permute-start | bytes 393224 | tf_op jit(solution)/shard_map/ppermute | solution.py:49
  540.9 38.1 %collective-permute-start.89 = (bf16[2,32,1024]{2,1,0:T(8,128)(2,1)S(1)}, bf16[2,32,1024]{2,1,0:T(8,128)(2,1)S(1)}, u32[]{:S(2)}, u32[]{:S(2)}) collective-permute-start(bf16[2,32,1024]{2,1,0:T(8,128)(2,1)S(1)} %slice_bitcast_fusion.38), channel_id=1, source_target_pairs={{0,16},{16,0},{1,17},{17,1},{2,18},{18,2},{3,19},{19,3},{4,20},{20... | collective-permute-start | bytes 393224 | tf_op jit(solution)/shard_map/ppermute | solution.py:49
  543.7 38.6 %collective-permute-start.113 = (bf16[32,1024]{1,0:T(8,128)(2,1)S(1)}, bf16[32,1024]{1,0:T(8,128)(2,1)S(1)}, u32[]{:S(2)}, u32[]{:S(2)}) collective-permute-start(bf16[32,1024]{1,0:T(8,128)(2,1)S(1)} %get-tuple-element.220), channel_id=1, source_target_pairs={{0,2},{1,3},{2,0},{3,1},{4,6},{5,7},{6,4},{7,5},{8,10},{9,11},{10,... | collective-permute-start | bytes 196616 | tf_op jit(solution)/shard_map/ppermute | solution.py:49
  587.3 60.7 %collective-permute-start.59 = (bf16[512,1024]{1,0:T(8,128)(2,1)}, bf16[512,1024]{1,0:T(8,128)(2,1)}, u32[]{:S(2)}, u32[]{:S(2)}) collective-permute-start(bf16[512,1024]{1,0:T(8,128)(2,1)} %convolution_convert_fusion.13), channel_id=1, source_target_pairs={{0,4},{4,0},{1,5},{5,1},{2,6},{6,2},{3,7},{7,3},{8,12},{12,8},{9,1... | collective-permute-start | bytes 3145736 | tf_op jit(solution)/shard_map/ppermute | solution.py:49
  656.7 101.4 %all-to-all-start.5 = ((bf16[8,64,1024]{2,1,0:T(8,128)(2,1)}), bf16[8,64,1024]{2,1,0:T(8,128)(2,1)}, u32[]{:S(2)}, u32[]{:S(2)}) async-start(bf16[8,64,1024]{2,1,0:T(8,128)(2,1)} %bitcast.610), calls=%async_computation.5 | async-start | bytes 2097152 | tf_op jit(solution)/shard_map/all_to_all | solution.py:74
  800.5 39.1 %collective-permute-start.77 = (bf16[2,2,96,1024]{3,2,1,0:T(8,128)(2,1)}, bf16[2,2,96,1024]{3,2,1,0:T(8,128)(2,1)}, u32[]{:S(2)}, u32[]{:S(2)}) collective-permute-start(bf16[2,2,96,1024]{3,2,1,0:T(8,128)(2,1)} %pad_maximum_fusion.61), channel_id=1, source_target_pairs={{0,4},{4,0},{1,5},{5,1},{2,6},{6,2},{3,7},{7,3},{8,12},{12,8},{9,1... | collective-permute-start | bytes 2359304 | tf_op jit(solution)/shard_map/ppermute | solution.py:49
  805.9 42.6 %all-to-all-start.4 = ((bf16[8,64,1024]{2,1,0:T(8,128)(2,1)}), bf16[8,64,1024]{2,1,0:T(8,128)(2,1)S(1)}, u32[]{:S(2)}, u32[]{:S(2)}) async-start(bf16[8,64,1024]{2,1,0:T(8,128)(2,1)} %bitcast.123), calls=%async_computation.4 | async-start | bytes 2097152 | tf_op jit(solution)/shard_map/all_to_all | solution.py:74
  (216 other events, 3148.3 us)

commit v3 on v2

--- a/solution.py
+++ b/solution.py
@@ -15,6 +15,8 @@
 EPSILON = 1e-05
 MASKED = -1000000000.0
 SCALE = HEAD_DIM**-0.5
+GELU_A = 0.7978845608028654
+GELU_B = 0.044715
 BF = jnp.bfloat16
 F32 = jnp.float32
 
@@ -74,40 +76,94 @@
     return lax.all_to_all(parts, ("yy", "head"), 0, 0, tiled=True)
 
 
-def ring(piece, axis):
-    count = lax.axis_size(axis)
-    return jnp.stack([piece] + [shift(piece, axis, k) for k in range(1, count)], 0)
-
-
-def gather_weight(piece):
-    along = ring(piece, "head")
-    half = along.shape[0] // 2
-    first = ring(ring(along[:half], "batch"), "yy")
-    second = ring(ring(along[half:], "yy"), "batch")
-    return first, second
-
-
-def fold(grads, axis):
-    count = lax.axis_size(axis)
-    total = grads[0].astype(F32)
-    for k in range(1, count):
-        total = total + shift(grads[k], axis, -k).astype(F32)
-    return total.astype(BF)
-
-
-def sum_weight(grads, rows):
-    nx, ny, nz = (lax.axis_size(a) for a in ("batch", "yy", "head"))
-    half = grads.shape[0] // 2
-    width = grads.shape[1]
-    first = grads[:half].reshape(ny, nx, nz // 2, rows, width)
-    second = grads[half:].reshape(nx, ny, nz // 2, rows, width)
-    first = fold(fold(first, "yy"), "batch")
-    second = fold(fold(second, "batch"), "yy")
-    total = first[0].astype(F32)
-    for k in range(1, nz):
-        slot = first[k] if k < nz // 2 else second[k - nz // 2]
-        total = total + shift(slot, "head", -k).astype(F32)
-    return total.astype(BF)
+def tied(values, *others):
+    return lax.optimization_barrier((values, others))[0]
+
+
+def meet(values, *moves):
+    values, got = lax.optimization_barrier((values, [m.got for m in moves]))
+    for move, pieces in zip(moves, got):
+        move.got = pieces
+    return values
+
+
+def others_of(axis):
+    return range(1, lax.axis_size(axis))
+
+
+class Gather:
+    def __init__(self, parts, *others):
+        self.deep = [p.shape[0] for p in parts]
+        self.mine = tied(jnp.concatenate(parts, 0), *others)
+        self.got = [shift(self.mine, "head", k) for k in others_of("head")]
+
+    def send(self, first, second, one, two):
+        self.mine = first, second
+        self.got = [shift(first, one, k) for k in others_of(one)] + [shift(second, two, k) for k in others_of(two)]
+        self.cut = len(others_of(one))
+
+    def two(self):
+        along = jnp.stack([self.mine] + self.got, 0)
+        half = along.shape[0] // 2
+        self.send(along[:half], along[half:], "batch", "yy")
+
+    def slots(self):
+        first, second = self.mine
+        return [first] + self.got[: self.cut], [second] + self.got[self.cut :]
+
+    def three(self):
+        first, second = self.slots()
+        self.send(jnp.stack(first, 0), jnp.stack(second, 0), "yy", "batch")
+
+    def result(self):
+        first, second = self.slots()
+        made, at = [], 0
+        for deep in self.deep:
+            cut = [slot[..., at : at + deep, :].reshape(-1, slot.shape[-1]) for slot in first + second]
+            made.append(jnp.concatenate(cut, 0))
+            at += deep
+        return made
+
+
+class Sum:
+    def __init__(self, grads):
+        nx, ny, self.nz = (lax.axis_size(a) for a in ("batch", "yy", "head"))
+        width = grads[0].shape[1]
+        half = [g.shape[0] // 2 for g in grads]
+        first = [g[:n].reshape(ny, nx, self.nz // 2, -1, width) for g, n in zip(grads, half)]
+        second = [g[n:].reshape(nx, ny, self.nz // 2, -1, width) for g, n in zip(grads, half)]
+        self.send(first, second, "yy", "batch")
+
+    def send(self, first, second, one, two):
+        def slot(grads, k):
+            return jnp.concatenate([g[k] for g in grads], -2)
+
+        self.mine = slot(first, 0), slot(second, 0)
+        self.got = [shift(slot(first, k), one, -k) for k in others_of(one)]
+        self.cut = len(self.got)
+        self.got = self.got + [shift(slot(second, k), two, -k) for k in others_of(two)]
+
+    def add(self, mine, got):
+        total = mine.astype(F32)
+        for piece in got:
+            total = total + piece.astype(F32)
+        return total.astype(BF)
+
+    def sums(self):
+        first, second = self.mine
+        return self.add(first, self.got[: self.cut]), self.add(second, self.got[self.cut :])
+
+    def two(self):
+        first, second = self.sums()
+        self.send([first], [second], "batch", "yy")
+
+    def three(self):
+        first, second = self.sums()
+        slots = [first[k] if k < self.nz // 2 else second[k - self.nz // 2] for k in range(self.nz)]
+        self.mine, self.got = slots[0], [shift(slots[k], "head", -k) for k in range(1, self.nz)]
+
+    def result(self):
+        return self.add(self.mine, self.got)
 
 
 def in_place(piece, axis):
@@ -118,8 +174,49 @@
     return jnp.stack([jnp.where(low, piece, other), jnp.where(low, other, piece)], 0)
 
 
+def gathered(piece):
+    sizes = tuple(lax.axis_size(a) for a in ("core", "batch", "yy"))
+    return lax.all_gather(piece, ("core", "batch", "yy"), axis=0, tiled=True).reshape(sizes + piece.shape)
+
+
 def replicate(piece):
     return in_place(in_place(in_place(piece, "yy"), "batch"), "core")
+
+
+def unfold_kernel(kinds, source_ref, *outs):
+    at = 0
+    for (size, turned), out in zip(kinds, outs):
+        piece = source_ref[..., at : at + size, :].reshape(-1, source_ref.shape[-1]).astype(F32)
+        out[...] = piece.T if turned else piece
+        at += size
+
+
+def unfold(whole, kinds):
+    width = whole.shape[-1]
+    count = whole.shape[0] * whole.shape[1] * whole.shape[2]
+    if any(size % 16 for size, _ in kinds):
+        made, at = [], 0
+        for size, turned in kinds:
+            piece = whole[..., at : at + size, :].reshape(-1, width)
+            made.append((piece.T if turned else piece).astype(F32))
+            at += size
+        return made
+    step = 256
+    return pl.pallas_call(
+        functools.partial(unfold_kernel, kinds),
+        out_shape=[
+            jax.ShapeDtypeStruct((width, count * size) if turned else (count * size, width), F32) for size, turned in kinds
+        ],
+        grid=(width // step,),
+        in_specs=[pl.BlockSpec(whole.shape[:4] + (step,), lambda i: (0, 0, 0, 0, i))],
+        out_specs=[
+            pl.BlockSpec((step, count * size), lambda i: (i, 0))
+            if turned
+            else pl.BlockSpec((count * size, step), lambda i: (0, i))
+            for size, turned in kinds
+        ],
+        compiler_params=pltpu.CompilerParams(vmem_limit_bytes=32 * 2**20),
+    )(whole)
 
 
 def total_of(value):
@@ -163,10 +260,24 @@
     return slice(index * BLOCK, (index + 1) * BLOCK)
 
 
+def per_block(need_ref, base_ref, span_ref, columns, chunk, i, j, work):
+    need = need_ref[i * BLOCKS + j]
+
+    @pl.when(need == 1)
+    def _():
+        allowed = allowed_block(span_ref, base_ref[j], columns, chunk)
+        work(lambda scores: jnp.where(allowed, scores, MASKED))
+
+    @pl.when(need == 2)
+    def _():
+        work(lambda scores: scores)
+
+
 def attend_kernel(heads, kinds, chunk, need_ref, base_ref, span_ref, *refs):
     sources = refs[: len(kinds)]
     mixed_ref, lse_ref, q_s, k_s, v_s, top_s, sum_s, acc_s = refs[len(kinds) :]
     where = [(source, kind) for source, count in zip(sources, kinds) for kind in range(count)]
+    every = range(len(heads))
 
     def load(half):
         for h, index in enumerate(heads):
@@ -185,21 +296,22 @@
         sum_s[...] = jnp.zeros(sum_s.shape, F32)
         acc_s[...] = jnp.zeros(acc_s.shape, F32)
         for j in range(BLOCKS):
-
-            @pl.when(need_ref[i * BLOCKS + j] > 0)
-            def _(j=j):
-                allowed = allowed_block(span_ref, base_ref[j], columns, chunk)
-                for h in range(len(heads)):
-                    scores = dot(k_s[h, span_of(j), :], q_s[h, :, columns], 1, 0)
-                    scores = jnp.where(allowed, scores, MASKED)
-                    top = jnp.maximum(top_s[h], jnp.max(scores, 0, keepdims=True))
-                    fade = jnp.exp(top_s[h] - top)
-                    weights = jnp.exp(scores - top)
-                    top_s[h] = top
-                    sum_s[h] = sum_s[h] * fade + jnp.sum(weights, 0, keepdims=True)
-                    acc_s[h] = acc_s[h] * fade + dot(v_s[h, :, span_of(j)], weights.astype(BF), 1, 0)
-
-        for h in range(len(heads)):
+            keys = span_of(j)
+
+            def work(mask, keys=keys, columns=columns):
+                scores = [mask(dot(k_s[h, keys, :], q_s[h, :, columns], 1, 0)) for h in every]
+                tops = [jnp.maximum(top_s[h], jnp.max(scores[h], 0, keepdims=True)) for h in every]
+                weights = [jnp.exp(scores[h] - tops[h]) for h in every]
+                fades = [jnp.exp(top_s[h] - tops[h]) for h in every]
+                mixed = [dot(v_s[h, :, keys], weights[h].astype(BF), 1, 0) for h in every]
+                for h in every:
+                    top_s[h] = tops[h]
+                    sum_s[h] = sum_s[h] * fades[h] + jnp.sum(weights[h], 0, keepdims=True)
+                    acc_s[h] = acc_s[h] * fades[h] + mixed[h]
+
+            per_block(need_ref, base_ref, span_ref, columns, chunk, i, j, work)
+
+        for h in every:
             lse_ref[0, h, :, columns] = top_s[h] + jnp.log(sum_s[h])
             q_s[h, :, columns] = (acc_s[h] / sum_s[h]).astype(BF)
 
@@ -218,6 +330,7 @@
     q_s, k_s, kt_s, v_s, g_s, inner_s, dq_s, dk_s, dv_s = refs[2 * len(kinds) + 3 :]
     where = [(source, kind) for source, count in zip(sources, kinds) for kind in range(count)]
     into = [(out, kind) for out, count in zip(outs, kinds) for kind in range(count)]
+    every = range(len(heads))
 
     def load(half):
         for h, index in enumerate(heads):
@@ -241,21 +354,21 @@
     for i in range(BLOCKS):
         columns = span_of(i)
         for j in range(BLOCKS):
-
-            @pl.when(need_ref[i * BLOCKS + j] > 0)
-            def _(j=j):
-                allowed = allowed_block(span_ref, base_ref[j], columns, chunk)
-                keys = span_of(j)
-                for h in range(len(heads)):
-                    query, grad = q_s[h, :, columns], g_s[h, :, columns]
-                    scores = dot(k_s[h, keys, :], query, 1, 0)
-                    scores = jnp.where(allowed, scores, MASKED)
-                    chances = jnp.exp(scores - lse_ref[0, h, :, columns])
-                    steep = dot(v_s[h, keys, :], grad, 1, 0)
-                    back = (chances * (steep - inner_s[h, :, columns])).astype(BF)
-                    dv_s[h, :, keys] += dot(grad, chances.astype(BF), 1, 1)
-                    dk_s[h, :, keys] += dot(query, back, 1, 1)
-                    dq_s[h, :, columns] += dot(kt_s[h, :, keys], back, 1, 0)
+            keys = span_of(j)
+
+            def work(mask, keys=keys, columns=columns):
+                scores = [mask(dot(k_s[h, keys, :], q_s[h, :, columns], 1, 0)) for h in every]
+                steep = [dot(v_s[h, keys, :], g_s[h, :, columns], 1, 0) for h in every]
+                chances = [jnp.exp(scores[h] - lse_ref[0, h, :, columns]) for h in every]
+                back = [(chances[h] * (steep[h] - inner_s[h, :, columns])).astype(BF) for h in every]
+                for h in every:
+                    dv_s[h, :, keys] += dot(g_s[h, :, columns], chances[h].astype(BF), 1, 1)
+                for h in every:
+                    dk_s[h, :, keys] += dot(q_s[h, :, columns], back[h], 1, 1)
+                for h in every:
+                    dq_s[h, :, columns] += dot(kt_s[h, :, keys], back[h], 1, 0)
+
+            per_block(need_ref, base_ref, span_ref, columns, chunk, i, j, work)
 
     def store(half):
         for h, index in enumerate(heads):
@@ -337,7 +450,7 @@
                 pltpu.VMEM((count, 1, BLOCK), F32),
                 pltpu.VMEM((count, HEAD_DIM, BLOCK), F32),
             ],
-            8 * 10**9,
+            40 * 10**9,
         )
         return self.join(mixed), lse
 
@@ -362,7 +475,7 @@
                 pltpu.VMEM(wide, F32),
                 pltpu.VMEM(wide, F32),
             ],
-            20 * 10**9,
+            46 * 10**9,
         )
         return [self.join(g) for g in grads]
 
@@ -397,17 +510,13 @@
         deep = matrix.shape[0] // 2 // nxy
         return lax.dynamic_slice_in_dim(matrix, (core * nxy + place) * deep, deep, 0)
 
-    def column_part(matrix):
-        wide = matrix.shape[1] // 2
-        return lax.dynamic_slice_in_dim(
-            lax.dynamic_slice_in_dim(matrix, core * wide, wide, 1).T, place * (wide // nxy), wide // nxy, 0
-        )
-
-    def gathered(*parts):
-        piece = jnp.concatenate(parts, 0) if len(parts) > 1 else parts[0]
-        first, second = gather_weight(piece)
-        width = piece.shape[1]
-        return jnp.concatenate([first.reshape(-1, width), second.reshape(-1, width)], 0)
+    def column_parts(*matrices):
+        parts = []
+        for matrix in matrices:
+            wide = matrix.shape[1] // 2
+            turned = lax.dynamic_slice_in_dim(matrix, core * wide, wide, 1).T
+            parts.append(lax.dynamic_slice_in_dim(turned, place * (wide // nxy), wide // nxy, 0))
+        return jnp.concatenate(parts, 0)
 
     row = iy * nz + iz
     lengths = lax.dynamic_index_in_dim(tgt_lengths, row, 0, keepdims=False)
@@ -433,82 +542,129 @@
     def tables_of(start, end):
         least = jnp.min(start.reshape(BLOCKS, BLOCK), 1)
         most = jnp.max(end.reshape(BLOCKS, BLOCK), 1)
-        need = (least[:, None] <= highest[None, :]) & (most[:, None] >= lowest[None, :])
-        return need.astype(jnp.int32).reshape(-1), lowest, jnp.stack([start, end - start], 0)
+        some = (least[:, None] <= highest[None, :]) & (most[:, None] >= lowest[None, :])
+        last, first = jnp.max(start.reshape(BLOCKS, BLOCK), 1), jnp.min(end.reshape(BLOCKS, BLOCK), 1)
+        whole = (last[:, None] <= lowest[None, :]) & (first[:, None] >= highest[None, :])
+        need = jnp.where(whole, 2, some.astype(jnp.int32))
+        return need.reshape(-1), lowest, jnp.stack([start, end - start], 0)
 
     self_tables = tables_of(self_start, positions)
     cross_tables = tables_of(cross_start, cross_end)
     heads = Heads(nx, ny, nz, chunk)
 
-    w_self = gathered(column_part(w_query), column_part(w_key), column_part(w_value))
     residual = to_row(inputs).astype(F32)
-    w_o = gathered(part(w_out))
-    w_mem = gathered(column_part(w_mem_key), column_part(w_mem_value))
-    w_cq = gathered(column_part(w_cross_query))
-    w_co = gathered(part(w_cross_out))
-    w_u = gathered(column_part(w_up))
-    w_d = gathered(part(w_down))
-    source = both(to_row(memory))
-    cot_own = to_row(cotangent)
-    cot = both(cot_own)
-
-    normed_one = both(normalize(residual, gain_one))
+    self_weights = Gather([column_parts(w_query, w_key, w_value)])
+    residual = to_row(tied(inputs, self_weights.mine)).astype(F32)
+    self_weights.two()
+    residual = meet(residual, self_weights)
+    self_weights.three()
+    cross_weights = Gather(
+        [part(w_out), column_parts(w_mem_key, w_mem_value), column_parts(w_cross_query), part(w_cross_out)],
+        residual,
+    )
+    normed_one = both(normalize(tied(residual, self_weights.mine, cross_weights.mine), gain_one))
+    normed_one = meet(normed_one, self_weights)
+    (w_self,) = self_weights.result()
     qkv = dot(w_self, normed_one, 1, 1).astype(BF)
+    qkv = meet(qkv, cross_weights)
+    cross_weights.two()
+    up_weights = Gather([column_parts(w_up)], cross_weights.mine)
+    qkv = tied(qkv, cross_weights.mine, up_weights.mine)
+    self_mixed, self_lse = heads.attend(self_tables, (qkv,), (3,))
+    self_mixed = meet(self_mixed, cross_weights, up_weights)
+    cross_weights.three()
+    down_weights = Gather([part(w_down)], up_weights.got, cross_weights.mine)
+    self_mixed = meet(self_mixed, cross_weights)
+    up_weights.two()
+    source_own = to_row(tied(memory, self_mixed))
+    self_mixed = tied(self_mixed, up_weights.mine)
+    w_o, w_mem, w_cq, w_co = cross_weights.result()
+    after_self = residual + own_sum(self_mixed, w_o)
+    normed_two = meet(normalize(after_self, gain_two), up_weights, down_weights)
+    up_weights.three()
+    down_weights.two()
+    normed_two, source_own = tied((normed_two, source_own), up_weights.mine, down_weights.mine)
+    source = both(source_own)
     mkv = dot(w_mem, source, 1, 1).astype(BF)
-    self_mixed, self_lse = heads.attend(self_tables, (qkv,), (3,))
-    after_self = residual + own_sum(self_mixed, w_o)
-    normed_two = both(normalize(after_self, gain_two))
+    normed_two = both(normed_two)
     cq = dot(w_cq, normed_two, 1, 1).astype(BF)
     cross_mixed, cross_lse = heads.attend(cross_tables, (cq, mkv), (1, 2))
+    cross_mixed = meet(cross_mixed, up_weights, down_weights)
+    down_weights.three()
+    cross_mixed = tied(cross_mixed, down_weights.mine)
+    cot_own = to_row(tied(cotangent, down_weights.mine))
     after_cross = after_self + own_sum(cross_mixed, w_co)
     normed_three = both(normalize(after_cross, gain_three))
+    (w_u,) = up_weights.result()
+
     hidden_pre = dot(w_u, normed_three, 1, 1)
-    hidden_act, gate_pull = jax.vjp(lambda p: jax.nn.gelu(p, approximate=True), hidden_pre)
-    hidden_act = hidden_act.astype(BF)
+    squared = hidden_pre * hidden_pre
+    bent = jnp.tanh(GELU_A * hidden_pre * (1.0 + GELU_B * squared))
+    gate = 0.5 + 0.5 * bent
+    slope = gate + (0.5 * GELU_A) * hidden_pre * (1.0 - bent * bent) * (1.0 + 3.0 * GELU_B * squared)
+    hidden_act, slope = lax.optimization_barrier(((hidden_pre * gate).astype(BF), slope.astype(BF)))
+    hidden_act = meet(hidden_act, down_weights)
+    (w_d,) = down_weights.result()
+    cot = both(tied(cot_own, hidden_act))
     output = (after_cross + own_sum(hidden_act, w_d)).astype(BF)
     output = from_row(output, rows)
 
-    def weight_sum(transposed, tokens):
-        grads = dot(transposed, tokens, 1, 0).astype(BF)
-        return sum_weight(grads, grads.shape[0] // (nxy * nz))
-
-    g_down = weight_sum(hidden_act, cot)
-    grad_pre = gate_pull(dot(w_d, cot, 1, 1))[0].astype(BF)
-    g_up = weight_sum(grad_pre, normed_three)
+    def weight_grad(transposed, tokens):
+        return dot(transposed, tokens, 1, 0).astype(BF)
+
+    g_down = weight_grad(hidden_act, cot)
+    grad_pre = (slope.astype(F32) * dot(w_d, cot, 1, 1)).astype(BF)
+    g_up = weight_grad(grad_pre, normed_three)
+    ffn_sum = Sum([g_down, g_up])
     step, grad_gain_three = normalize_back(after_cross, gain_three, own_sum(grad_pre, w_u))
     grad_after_cross = cot_own.astype(F32) + step
 
     cross_grad = both(grad_after_cross.astype(BF))
-    g_co = weight_sum(cross_mixed, cross_grad)
     grad_cross_mixed = dot(w_co, cross_grad, 1, 1).astype(BF)
     gcq, gmkv = heads.attend_back(
         cross_tables, (cq, mkv), (1, 2), cross_mixed, grad_cross_mixed, cross_lse
     )
-    g_cq = weight_sum(gcq, normed_two)
-    g_mem = weight_sum(gmkv, source)
-    grad_memory = from_row(own_sum(gmkv, w_mem).astype(BF), rows).astype(F32)
+    gcq, gmkv, output = meet((gcq, gmkv, output), ffn_sum)
+    ffn_sum.two()
+    gcq, gmkv = tied((gcq, gmkv), ffn_sum.mine)
     step, grad_gain_two = normalize_back(after_self, gain_two, own_sum(gcq, w_cq))
     grad_after_self = grad_after_cross + step
-
+    grad_after_self = meet(grad_after_self, ffn_sum)
+    ffn_sum.three()
     self_grad = both(grad_after_self.astype(BF))
-    g_o = weight_sum(self_mixed, self_grad)
+    g_co = weight_grad(cross_mixed, cross_grad)
+    g_cq = weight_grad(gcq, normed_two)
+    g_mem = weight_grad(gmkv, source)
+    cross_sum = Sum([g_co, g_cq, g_mem])
+    memory_back = own_sum(gmkv, w_mem).astype(BF)
     grad_self_mixed = dot(w_o, self_grad, 1, 1).astype(BF)
+    grad_self_mixed, memory_back = tied((grad_self_mixed, memory_back), ffn_sum.mine, cross_sum.mine)
+    grad_memory = from_row(memory_back, rows).astype(F32)
     (gqkv,) = heads.attend_back(self_tables, (qkv,), (3,), self_mixed, grad_self_mixed, self_lse)
-    g_self = weight_sum(gqkv, normed_one)
-    step, grad_gain_one = normalize_back(residual, gain_one, own_sum(gqkv, w_self))
+    gqkv = meet(gqkv, cross_sum)
+    cross_sum.two()
+    g_self = weight_grad(gqkv, normed_one)
+    g_o = weight_grad(self_mixed, self_grad)
+    self_sum = Sum([g_o, g_self])
+    first_back = own_sum(gqkv, w_self)
+    first_back = meet(tied(first_back, self_sum.mine), cross_sum, ffn_sum)
+    cross_sum.three()
+    step, grad_gain_one = normalize_back(residual, gain_one, first_back)
     grad_inputs = from_row((grad_after_self + step).astype(BF), rows).astype(F32)
     gains = total_of(jnp.stack([grad_gain_one, grad_gain_two, grad_gain_three]))
-
-    def tall(grads):
-        return replicate(grads).reshape(-1, grads.shape[1]).astype(F32)
-
-    def columns(grads, count):
-        whole = replicate(grads)
-        whole = whole.reshape(whole.shape[:3] + (count, -1, grads.shape[1]))
-        return [whole[:, :, :, i].reshape(-1, grads.shape[1]).T.astype(F32) for i in range(count)]
-
-    grad_q, grad_k, grad_v = columns(g_self, 3)
-    grad_mk, grad_mv = columns(g_mem, 2)
+    self_sum.two()
+    self_sum.three()
+
+    deep = w_query.shape[1] // 2 // nxy
+    far = w_up.shape[1] // 2 // nxy
+    grad_down, grad_up = unfold(gathered(ffn_sum.result()), [(far, False), (far, True)])
+    grad_co, grad_cq, grad_mk, grad_mv = unfold(
+        gathered(cross_sum.result()), [(deep, False), (deep, True), (deep, True), (deep, True)]
+    )
+    self_sum.got = tied(self_sum.got, grad_down, grad_up, grad_inputs, gains, grad_memory)
+    grad_o, grad_q, grad_k, grad_v = unfold(
+        replicate(self_sum.result()), [(deep, False), (deep, True), (deep, True), (deep, True)]
+    )
     return (
         output,
         grad_inputs,
@@ -517,15 +673,15 @@
         grad_q,
         grad_k,
         grad_v,
-        tall(g_o),
+        grad_o,
         gains[1],
-        columns(g_cq, 1)[0],
+        grad_cq,
         grad_mk,
         grad_mv,
-        tall(g_co),
+        grad_co,
         gains[2],
-        columns(g_up, 1)[0],
-        tall(g_down),
+        grad_up,
+        grad_down,
     )
 
 

time: 859 us -> 714 us (0.83)
  starting transfers between devices: 305 us -> 131 us
  waiting for transfers between devices: 200 us -> 242 us
  other arithmetic: 101 us -> 77.3 us
  between operations: 3.29 us -> 16.4 us
    ppermute x133 -> x66, starting transfers between devices: 267 us -> 87.1 us  [shift(): lax.ppermute(piece, axis, [(i, (i + step) % count) for i in range(count)])]
    another operation x47 -> x23, other arithmetic: 46.7 us -> 23.8 us  [the longest x20 23.5 us: three(): self.send(jnp.stack(first, 0), jnp.stack(second, 0), 'yy', 'batch')]
    ppermute x133 -> x66, waiting for transfers between devices: 177 us -> 197 us  [shift(): lax.ppermute(piece, axis, [(i, (i + step) % count) for i in range(count)])]
    all_to_all x3, waiting for transfers between devices: 1.79 us -> 17.6 us  [to_row(): moved = lax.all_to_all(tokens, ('yy', 'head'), 0, 0, tiled=True)]
    another operation x40 -> x6, other arithmetic: 15.7 us -> 2.92 us  [in_place(): jnp.stack([jnp.where(low, piece, other), jnp.where(low, other, piece)], 0)]
    slice x7 -> x11, local copies, waits for them, and re-layouts: 1.7 us -> 12.2 us  [the longest x7 7.59 us: slot(): return jnp.concatenate([g[k] for g in grads], -2)]
    pallas_call x0 -> x3, Pallas kernels: none -> 9.54 us  [unfold(): pl.pallas_call(functools.partial(unfold_kernel, kinds), out_shape=[jax.Sh...]
    convert_element_type x47 -> x17, other arithmetic: 24.1 us -> 22.1 us  [the longest x15 17.6 us: add(): return total.astype(BF)]
  transfers between devices with their start and end apart: 144 -> 79, of which waited for: 37 -> 24; matrix products, arithmetic and copies ran while one was open for 27% -> 27% of each run, Pallas kernels for 9% -> 11%
where the time goes in v3:
time: 714 us; the launch traced here: 705 us
  waiting for transfers between devices  242 us (34%)
  starting transfers between devices  131 us (18%)
  matrix products  102 us (14%)
  Pallas kernels  80.8 us (11%)
  other arithmetic  77.3 us (11%)
  local copies, waits for them, and re-layouts  55.5 us (8%)
  between operations  16.4 us (2%)
    ppermute x66, waiting for transfers between devices, shift(): lax.ppermute(piece, axis, [(i, (i + step) % count) for i in range(count)])  197 us
    dot_general x28, matrix products, dot(): lax.dot_general(left, right, (((left_dim,), (right_dim,)), ((), ())), pre...  102 us
    ppermute x66, starting transfers between devices, shift(): lax.ppermute(piece, axis, [(i, (i + step) % count) for i in range(count)])  87.1 us
    pallas_call x4, Pallas kernels, call(): pl.pallas_call(functools.partial(kernel, self.index, kinds, self.chunk),...  71.2 us
    ppermute x5, waiting for transfers between devices, total_of(): lax.ppermute(value, axis, [(i, i ^ step) for i in range(count)])  27.1 us
    unnamed x281, local copies, waits for them, and re-layouts  25.7 us
    all_to_all x3, starting transfers between devices, to_row(): moved = lax.all_to_all(tokens, ('yy', 'head'), 0, 0, tiled=True)  23.7 us
    another operation x20, other arithmetic, three(): self.send(jnp.stack(first, 0), jnp.stack(second, 0), 'yy', 'batch')  23.5 us
  transfers between devices with their start and end apart: 79, of which 24 were waited for; matrix products, arithmetic and copies ran while one was open for 27% of the time, Pallas kernels for 11%

profile of v3, /device:TPU:1, one launch (start us, length us, event | category | flops | bytes accessed | tf_op | source)
XLA Modules:
  0.0 704.6 jit_solution(15538373228577411295)
XLA Ops:
  39.9 16.9 %all-to-all-done = bf16[8,64,1024]{2,1,0:T(8,128)(2,1)S(1)} async-done(((bf16[8,64,1024]{2,1,0:T(8,128)(2,1)}), bf16[8,64,1024]{2,1,0:T(8,128)(2,1)S(1)}, u32[]{:S(2)}, u32[]{:S(2)}) %all-to-all-start) | async-done | bytes 1048608 | tf_op jit(solution)/shard_map/all_to_all | solution.py:70
  74.9 12.5 %collective-permute-done.6 = bf16[2,2,96,1024]{3,2,1,0:T(8,128)(2,1)} collective-permute-done((bf16[2,2,96,1024]{3,2,1,0:T(8,128)(2,1)}, bf16[2,2,96,1024]{3,2,1,0:T(8,128)(2,1)}, u32[]{:S(2)}, u32[]{:S(2)}) %collective-permute-start.6) | collective-permute-done | bytes 786464 | tf_op jit(solution)/shard_map/ppermute | solution.py:51
  97.0 7.3 %collective-permute-start.13 = (bf16[128,1024]{1,0:T(8,128)(2,1)S(1)}, bf16[128,1024]{1,0:T(8,128)(2,1)S(1)}, u32[]{:S(2)}, u32[]{:S(2)}) collective-permute-start(bf16[128,1024]{1,0:T(8,128)(2,1)S(1)} %bitcast.301), channel_id=1, source_target_pairs={{0,1},{1,2},{2,3},{3,0},{4,5},{5,6},{6,7},{7,4},{8,9},{9,10},{10,1... | collective-permute-start | bytes 786440 | tf_op jit(solution)/shard_map/ppermute | solution.py:51
  106.4 22.7 %shard_map.297 = (bf16[2,2,2,2,1,32,1024]{6,5,4,3,2,1,0:T(8,128)(2,1)S(1)}, f32[2,4,1,1024]{3,2,1,0:T(1,128)S(1)}) custom-call(s32[16]{0:T(128)S(1)} %select_n.214.need_ref, s32[4]{0:T(128)S(1)} %get-tuple-element.299.base_ref, s32[2,1024]{1,0:T(2,128)S(1)} %pad_add_fusion.1.span_ref, bf16[2,2,2,2,3,32,1024]{6,5,4,3,2,1,0:T(8,128)(2,1)S(1)} %bitcast.243), custom_call_target="tpu_custom_call" | custom-call | flops 40000000000 | bytes 8388608 | tf_op jit(solution)/shard_map/pallas_call | solution.py:417
  135.4 21.8 %collective-permute-done.16 = bf16[2,2,160,1024]{3,2,1,0:T(8,128)(2,1)S(1)} collective-permute-done((bf16[2,2,160,1024]{3,2,1,0:T(8,128)(2,1)S(1)}, bf16[2,2,160,1024]{3,2,1,0:T(8,128)(2,1)S(1)}, u32[]{:S(2)}, u32[]{:S(2)}) %collective-permute-start.16) | collective-permute-done | bytes 1310752 | tf_op jit(solution)/shard_map/ppermute | solution.py:51
  184.7 5.8 collective-permute-done.22
  190.5 13.0 %collective-permute-done.23 = bf16[128,1024]{1,0:T(8,128)(2,1)S(1)} collective-permute-done((bf16[128,1024]{1,0:T(8,128)(2,1)S(1)}, bf16[128,1024]{1,0:T(8,128)(2,1)S(1)}, u32[]{:S(2)}, u32[]{:S(2)}) %collective-permute-start.23) | collective-permute-done | bytes 262176 | tf_op jit(solution)/shard_map/ppermute | solution.py:51
  227.5 12.9 %shard_map.298 = (bf16[2,2,2,2,1,32,1024]{6,5,4,3,2,1,0:T(8,128)(2,1)S(1)}, f32[2,4,1,1024]{3,2,1,0:T(1,128)S(1)}) custom-call(s32[16]{0:T(128)S(1)} %select_n.206.need_ref, s32[4]{0:T(128)S(1)} %get-tuple-element.299.base_ref, s32[2,1024]{1,0:T(2,128)S(1)} %pad_add_fusion.span_ref, bf16[2,2,2,2,1,32,1024]{6,5,4,3,2,1,0:T(8,128)(2,1)S(1)} %bitcast.256, ...), custom_call_target="tpu_custom_call" | custom-call | flops 40000000000 | bytes 8388608 | tf_op jit(solution)/shard_map/pallas_call | solution.py:417
  240.4 11.9 %collective-permute-done.28 = bf16[2,128,1024]{2,1,0:T(8,128)(2,1)S(1)} collective-permute-done((bf16[2,128,1024]{2,1,0:T(8,128)(2,1)S(1)}, bf16[2,128,1024]{2,1,0:T(8,128)(2,1)S(1)}, u32[]{:S(2)}, u32[]{:S(2)}) %collective-permute-start.28) | collective-permute-done | bytes 524320 | tf_op jit(solution)/shard_map/ppermute | solution.py:51
  262.5 15.3 %all-to-all-start.2 = ((bf16[8,64,1024]{2,1,0:T(8,128)(2,1)}), bf16[8,64,1024]{2,1,0:T(8,128)(2,1)}, u32[]{:S(2)}, u32[]{:S(2)}) async-start(bf16[8,64,1024]{2,1,0:T(8,128)(2,1)} %param.20), calls=%async_computation.2 | async-start | bytes 2097152 | tf_op jit(solution)/shard_map/all_to_all | solution.py:70
  279.5 13.9 %add_convert_fusion = (bf16[2048,1024]{1,0:T(8,128)(2,1)}, bf16[2048,1024]{1,0:T(8,128)(2,1)}) fusion(bf16[512,1024]{1,0:T(8,128)(2,1)} %collective-permute-done.31, bf16[512,1024]{1,0:T(8,128)(2,1)} %multiply_convert_fusion.2, bf16[512,1024]{1,0:T(8,128)(2,1)} %bitcast.76, bf16[512,1024]{1,0:T(8,128)(2,1)} %bitcast.290, bf16[512,1024]{1,0:T(8,128)(2,1)} %bitcast.401, ...), kind=kOutput, calls=%fused_computation.1 | convolution fusion | flops 4353687552 | bytes 14680064 | tf_op jit(solution)/shard_map/dot_general | solution.py:25
  293.5 20.2 %collective-permute-done.32 = bf16[2,2,128,1024]{3,2,1,0:T(8,128)(2,1)} collective-permute-done((bf16[2,2,128,1024]{3,2,1,0:T(8,128)(2,1)}, bf16[2,2,128,1024]{3,2,1,0:T(8,128)(2,1)}, u32[]{:S(2)}, u32[]{:S(2)}) %collective-permute-start.32) | collective-permute-done | bytes 1048608 | tf_op jit(solution)/shard_map/ppermute | solution.py:51
  314.9 5.3 fusion.17
  322.1 9.1 %multiply_convert_fusion = bf16[2048,1024]{1,0:T(8,128)(2,1)} fusion(bf16[2048,1024]{1,0:T(8,128)(2,1)S(1)} %copy-done.132, bf16[1024,1024]{1,0:T(8,128)(2,1)S(1)} %constant_dynamic-update-slice_fusion.4, bf16[512,1024]{1,0:T(8,128)(2,1)} %bitcast.80, bf16[512,1024]{1,0:T(8,128)(2,1)S(1)} %bitcast.298, bf16[512,1024]{1,0:T(8,128)(2,1)} %bitcast.78, ...), kind=kOutput, calls=%fused_computation | convolution fusion | flops 4318035968 | bytes 14680064 | tf_op jit(solution)/shard_map/dot_general | solution.py:25
  331.2 5.4 fusion.20
  336.8 4.9 add_convert_fusion.11
  346.3 7.5 %convolution_convert_fusion.3 = bf16[2048,1024]{1,0:T(8,128)(2,1)S(1)} fusion(bf16[2048,1024]{1,0:T(8,128)(2,1)} %get-tuple-element.153, bf16[1024,1024]{1,0:T(8,128)(2,1)} %copy-done.81), kind=kOutput, calls=%fused_computation.12 | convolution fusion | flops 4297064448 | bytes 10485760 | tf_op jit(solution)/shard_map/dot_general | solution.py:25
  353.9 5.1 multiply_reduce_fusion
  363.3 6.3 convolution_convert_fusion.2
  379.5 19.0 %shard_map.299 = (bf16[2,2,2,2,1,32,1024]{6,5,4,3,2,1,0:T(8,128)(2,1)S(1)}, bf16[2,2,2,2,2,32,1024]{6,5,4,3,2,1,0:T(8,128)(2,1)}) custom-call(s32[16]{0:T(128)S(1)} %select_n.206.need_ref, s32[4]{0:T(128)S(1)} %get-tuple-element.299.base_ref, s32[2,1024]{1,0:T(2,128)S(1)} %pad_add_fusion.span_ref, bf16[2,2,2,2,1,32,1024]{6,5,4,3,2,1,0:T(8,128)(2,1)S(1)} %bitcast.257, ...), custom_call_target="tpu_custom_call" | custom-call | flops 46000001024 | bytes 8388608 | tf_op jit(solution)/shard_map/pallas_call | solution.py:417
  399.5 22.8 %collective-permute-done.38 = bf16[2,2,256,1024]{3,2,1,0:T(8,128)(2,1)} collective-permute-done((bf16[2,2,256,1024]{3,2,1,0:T(8,128)(2,1)}, bf16[2,2,256,1024]{3,2,1,0:T(8,128)(2,1)}, u32[]{:S(2)}, u32[]{:S(2)}) %collective-permute-start.38) | collective-permute-done | bytes 2097184 | tf_op jit(solution)/shard_map/ppermute | solution.py:51
  450.5 6.5 collective-permute-done.41
  473.3 16.5 %shard_map.300 = bf16[2,2,2,2,3,32,1024]{6,5,4,3,2,1,0:T(8,128)(2,1)S(1)} custom-call(s32[16]{0:T(128)S(1)} %select_n.214.need_ref, s32[4]{0:T(128)S(1)} %get-tuple-element.299.base_ref, s32[2,1024]{1,0:T(2,128)S(1)} %copy-done.5, bf16[2,2,2,2,3,32,1024]{6,5,4,3,2,1,0:T(8,128)(2,1)} %bitcast.244, bf16[2,2,2,2,1,32,1024]{6,5,4,3,2,1,0:T(8,128)(2,1)S(1)} %copy-done.11, ...), custom_call_target="tpu_custom_call" | custom-call | flops 46000001024 | bytes 8388608 | tf_op jit(solution)/shard_map/pallas_call | solution.py:417
  502.3 10.6 %collective-permute-done.51 = bf16[256,1024]{1,0:T(8,128)(2,1)S(1)} collective-permute-done((bf16[256,1024]{1,0:T(8,128)(2,1)}, bf16[256,1024]{1,0:T(8,128)(2,1)S(1)}, u32[]{:S(2)}, u32[]{:S(2)}) %collective-permute-start.51) | collective-permute-done | bytes 524320 | tf_op jit(solution)/shard_map/ppermute | solution.py:51
  529.2 6.4 all-to-all-start.5
  540.7 33.0 %collective-permute-done.58 = bf16[2,2,128,1024]{3,2,1,0:T(8,128)(2,1)} collective-permute-done((bf16[2,2,128,1024]{3,2,1,0:T(8,128)(2,1)}, bf16[2,2,128,1024]{3,2,1,0:T(8,128)(2,1)}, u32[]{:S(2)}, u32[]{:S(2)}) %collective-permute-start.58) | collective-permute-done | bytes 1048608 | tf_op jit(solution)/shard_map/ppermute | solution.py:51
  593.9 6.8 collective-permute-done.69
  604.0 16.1 %collective-permute-start.60 = (bf16[128,1024]{1,0:T(8,128)(2,1)S(1)}, bf16[128,1024]{1,0:T(8,128)(2,1)S(1)}, u32[]{:S(2)}, u32[]{:S(2)}) collective-permute-start(bf16[128,1024]{1,0:T(8,128)(2,1)S(1)} %slice_bitcast_fusion.22), channel_id=1, source_target_pairs={{0,3},{1,0},{2,1},{3,2},{4,7},{5,4},{6,5},{7,6},{8,11},{9,8},{10,9... | collective-permute-start | bytes 786440 | tf_op jit(solution)/shard_map/ppermute | solution.py:51
  626.8 6.0 collective-permute-done.56
  633.6 18.3 %collective-permute-done.57 = f32[3,1024]{1,0:T(4,128)S(1)} collective-permute-done((f32[3,1024]{1,0:T(4,128)S(1)}, f32[3,1024]{1,0:T(4,128)S(1)}, u32[]{:S(2)}, u32[]{:S(2)}) %collective-permute-start.57) | collective-permute-done | bytes 12320 | tf_op jit(solution)/shard_map/ppermute | solution.py:227
  663.1 7.2 %collective-permute-done.65 = bf16[128,1024]{1,0:T(8,128)(2,1)S(1)} collective-permute-done((bf16[128,1024]{1,0:T(8,128)(2,1)S(1)}, bf16[128,1024]{1,0:T(8,128)(2,1)S(1)}, u32[]{:S(2)}, u32[]{:S(2)}) %collective-permute-start.65) | collective-permute-done | bytes 262176 | tf_op jit(solution)/shard_map/ppermute | solution.py:51
  670.8 11.7 %collective-permute-done.66 = bf16[2,128,1024]{2,1,0:T(8,128)(2,1)S(1)} collective-permute-done((bf16[2,128,1024]{2,1,0:T(8,128)(2,1)S(1)}, bf16[2,128,1024]{2,1,0:T(8,128)(2,1)S(1)}, u32[]{:S(2)}, u32[]{:S(2)}) %collective-permute-start.66) | collective-permute-done | bytes 524320 | tf_op jit(solution)/shard_map/ppermute | solution.py:51
  (586 shorter events, 289.5 us)
Async XLA Ops:
  15.6 41.3 %all-to-all-start = ((bf16[8,64,1024]{2,1,0:T(8,128)(2,1)}), bf16[8,64,1024]{2,1,0:T(8,128)(2,1)S(1)}, u32[]{:S(2)}, u32[]{:S(2)}) async-start(bf16[8,64,1024]{2,1,0:T(8,128)(2,1)} %param.18), calls=%async_computation | async-start | bytes 2097152 | tf_op jit(solution)/shard_map/all_to_all | solution.py:70
  95.8 33.3 %collective-permute-start.11 = (bf16[2,160,1024]{2,1,0:T(8,128)(2,1)S(1)}, bf16[2,160,1024]{2,1,0:T(8,128)(2,1)S(1)}, u32[]{:S(2)}, u32[]{:S(2)}) collective-permute-start(bf16[2,160,1024]{2,1,0:T(8,128)(2,1)S(1)} %get-tuple-element.268), channel_id=1, source_target_pairs={{0,16},{16,0},{1,17},{17,1},{2,18},{18,2},{3,19},{19,3},{4,20},{20... | collective-permute-start | bytes 1966088 | tf_op jit(solution)/shard_map/ppermute | solution.py:51
  96.2 32.9 %collective-permute-start.12 = (bf16[2,160,1024]{2,1,0:T(8,128)(2,1)S(1)}, bf16[2,160,1024]{2,1,0:T(8,128)(2,1)S(1)}, u32[]{:S(2)}, u32[]{:S(2)}) collective-permute-start(bf16[2,160,1024]{2,1,0:T(8,128)(2,1)S(1)} %get-tuple-element.266), channel_id=1, source_target_pairs={{0,8},{8,0},{1,9},{9,1},{2,10},{10,2},{3,11},{11,3},{4,12},{12,4},... | collective-permute-start | bytes 1966088 | tf_op jit(solution)/shard_map/ppermute | solution.py:51
  97.0 32.1 %collective-permute-start.13 = (bf16[128,1024]{1,0:T(8,128)(2,1)S(1)}, bf16[128,1024]{1,0:T(8,128)(2,1)S(1)}, u32[]{:S(2)}, u32[]{:S(2)}) collective-permute-start(bf16[128,1024]{1,0:T(8,128)(2,1)S(1)} %bitcast.301), channel_id=1, source_target_pairs={{0,1},{1,2},{2,3},{3,0},{4,5},{5,6},{6,7},{7,4},{8,9},{9,10},{10,1... | collective-permute-start | bytes 786440 | tf_op jit(solution)/shard_map/ppermute | solution.py:51
  166.2 37.4 %collective-permute-start.19 = (bf16[2,128,1024]{2,1,0:T(8,128)(2,1)}, bf16[2,128,1024]{2,1,0:T(8,128)(2,1)}, u32[]{:S(2)}, u32[]{:S(2)}) collective-permute-start(bf16[2,128,1024]{2,1,0:T(8,128)(2,1)} %get-tuple-element.282), channel_id=1, source_target_pairs={{0,16},{16,0},{1,17},{17,1},{2,18},{18,2},{3,19},{19,3},{4,20},{20... | collective-permute-start | bytes 1572872 | tf_op jit(solution)/shard_map/ppermute | solution.py:51
  167.5 36.1 %collective-permute-start.20 = (bf16[2,128,1024]{2,1,0:T(8,128)(2,1)}, bf16[2,128,1024]{2,1,0:T(8,128)(2,1)}, u32[]{:S(2)}, u32[]{:S(2)}) collective-permute-start(bf16[2,128,1024]{2,1,0:T(8,128)(2,1)} %get-tuple-element.280), channel_id=1, source_target_pairs={{0,8},{8,0},{1,9},{9,1},{2,10},{10,2},{3,11},{11,3},{4,12},{12,4},... | collective-permute-start | bytes 1572872 | tf_op jit(solution)/shard_map/ppermute | solution.py:51
  172.2 40.3 %all-to-all-start.1 = ((bf16[8,64,1024]{2,1,0:T(8,128)(2,1)}), bf16[8,64,1024]{2,1,0:T(8,128)(2,1)}, u32[]{:S(2)}, u32[]{:S(2)}) async-start(bf16[8,64,1024]{2,1,0:T(8,128)(2,1)} %param.19), calls=%async_computation.1 | async-start | bytes 2097152 | tf_op jit(solution)/shard_map/all_to_all | solution.py:70
  216.4 35.9 %collective-permute-start.26 = (bf16[2,2,128,1024]{3,2,1,0:T(8,128)(2,1)S(1)}, bf16[2,2,128,1024]{3,2,1,0:T(8,128)(2,1)S(1)}, u32[]{:S(2)}, u32[]{:S(2)}) collective-permute-start(bf16[2,2,128,1024]{3,2,1,0:T(8,128)(2,1)S(1)} %copy-done.54), channel_id=1, source_target_pairs={{0,8},{8,0},{1,9},{9,1},{2,10},{10,2},{3,11},{11,3},{4,12},{12,4},... | collective-permute-start | bytes 3145736 | tf_op jit(solution)/shard_map/ppermute | solution.py:51
  217.1 35.2 %collective-permute-start.27 = (bf16[2,2,128,1024]{3,2,1,0:T(8,128)(2,1)S(1)}, bf16[2,2,128,1024]{3,2,1,0:T(8,128)(2,1)}, u32[]{:S(2)}, u32[]{:S(2)}) collective-permute-start(bf16[2,2,128,1024]{3,2,1,0:T(8,128)(2,1)S(1)} %copy-done.57), channel_id=1, source_target_pairs={{0,16},{16,0},{1,17},{17,1},{2,18},{18,2},{3,19},{19,3},{4,20},{20... | collective-permute-start | bytes 3145736 | tf_op jit(solution)/shard_map/ppermute | solution.py:51
  218.1 34.2 %collective-permute-start.28 = (bf16[2,128,1024]{2,1,0:T(8,128)(2,1)S(1)}, bf16[2,128,1024]{2,1,0:T(8,128)(2,1)S(1)}, u32[]{:S(2)}, u32[]{:S(2)}) collective-permute-start(bf16[2,128,1024]{2,1,0:T(8,128)(2,1)S(1)} %copy-done.75), channel_id=1, source_target_pairs={{0,16},{16,0},{1,17},{17,1},{2,18},{18,2},{3,19},{19,3},{4,20},{20... | collective-permute-start | bytes 1572872 | tf_op jit(solution)/shard_map/ppermute | solution.py:51
  220.0 32.2 %collective-permute-start.29 = (bf16[2,128,1024]{2,1,0:T(8,128)(2,1)S(1)}, bf16[2,128,1024]{2,1,0:T(8,128)(2,1)S(1)}, u32[]{:S(2)}, u32[]{:S(2)}) collective-permute-start(bf16[2,128,1024]{2,1,0:T(8,128)(2,1)S(1)} %copy-done.76), channel_id=1, source_target_pairs={{0,8},{8,0},{1,9},{9,1},{2,10},{10,2},{3,11},{11,3},{4,12},{12,4},... | collective-permute-start | bytes 1572872 | tf_op jit(solution)/shard_map/ppermute | solution.py:51
  262.5 51.2 %all-to-all-start.2 = ((bf16[8,64,1024]{2,1,0:T(8,128)(2,1)}), bf16[8,64,1024]{2,1,0:T(8,128)(2,1)}, u32[]{:S(2)}, u32[]{:S(2)}) async-start(bf16[8,64,1024]{2,1,0:T(8,128)(2,1)} %param.20), calls=%async_computation.2 | async-start | bytes 2097152 | tf_op jit(solution)/shard_map/all_to_all | solution.py:70
  277.8 35.8 %collective-permute-start.32 = (bf16[2,2,128,1024]{3,2,1,0:T(8,128)(2,1)}, bf16[2,2,128,1024]{3,2,1,0:T(8,128)(2,1)}, u32[]{:S(2)}, u32[]{:S(2)}) collective-permute-start(bf16[2,2,128,1024]{3,2,1,0:T(8,128)(2,1)} %pad_maximum_fusion.23), channel_id=1, source_target_pairs={{0,8},{8,0},{1,9},{9,1},{2,10},{10,2},{3,11},{11,3},{4,12},{12,4},... | collective-permute-start | bytes 3145736 | tf_op jit(solution)/shard_map/ppermute | solution.py:51
  279.2 34.4 %collective-permute-start.33 = (bf16[2,2,128,1024]{3,2,1,0:T(8,128)(2,1)}, bf16[2,2,128,1024]{3,2,1,0:T(8,128)(2,1)}, u32[]{:S(2)}, u32[]{:S(2)}) collective-permute-start(bf16[2,2,128,1024]{3,2,1,0:T(8,128)(2,1)} %pad_maximum_fusion.24), channel_id=1, source_target_pairs={{0,16},{16,0},{1,17},{17,1},{2,18},{18,2},{3,19},{19,3},{4,20},{20... | collective-permute-start | bytes 3145736 | tf_op jit(solution)/shard_map/ppermute | solution.py:51
  341.7 57.8 %all-to-all-start.3 = ((bf16[8,64,1024]{2,1,0:T(8,128)(2,1)}), bf16[8,64,1024]{2,1,0:T(8,128)(2,1)}, u32[]{:S(2)}, u32[]{:S(2)}) async-start(bf16[8,64,1024]{2,1,0:T(8,128)(2,1)} %bitcast.293), calls=%async_computation.3 | async-start | bytes 2097152 | tf_op jit(solution)/shard_map/all_to_all | solution.py:76
  346.0 310.3 %all-gather.3.cloned.1.call-start = ((), (), s32[]{:S(2)}) async-start(), calls=%async_computation.6 | async-start | bytes 4718592 | tf_op jit(solution)/shard_map/all_gather | solution.py:179
  374.6 47.7 %collective-permute-start.38 = (bf16[2,2,256,1024]{3,2,1,0:T(8,128)(2,1)}, bf16[2,2,256,1024]{3,2,1,0:T(8,128)(2,1)}, u32[]{:S(2)}, u32[]{:S(2)}) collective-permute-start(bf16[2,2,256,1024]{3,2,1,0:T(8,128)(2,1)} %pad_maximum_fusion.7), channel_id=1, source_target_pairs={{0,8},{8,0},{1,9},{9,1},{2,10},{10,2},{3,11},{11,3},{4,12},{12,4},... | collective-permute-start | bytes 6291464 | tf_op jit(solution)/shard_map/ppermute | solution.py:51
  377.8 46.8 %collective-permute-start.39 = (bf16[2,2,256,1024]{3,2,1,0:T(8,128)(2,1)}, bf16[2,2,256,1024]{3,2,1,0:T(8,128)(2,1)}, u32[]{:S(2)}, u32[]{:S(2)}) collective-permute-start(bf16[2,2,256,1024]{3,2,1,0:T(8,128)(2,1)} %pad_maximum_fusion.8), channel_id=1, source_target_pairs={{0,16},{16,0},{1,17},{17,1},{2,18},{18,2},{3,19},{19,3},{4,20},{20... | collective-permute-start | bytes 6291464 | tf_op jit(solution)/shard_map/ppermute | solution.py:51
  446.8 43.1 %collective-permute-start.45 = (bf16[2,2,128,1024]{3,2,1,0:T(8,128)(2,1)S(1)}, bf16[2,2,128,1024]{3,2,1,0:T(8,128)(2,1)S(1)}, u32[]{:S(2)}, u32[]{:S(2)}) collective-permute-start(bf16[2,2,128,1024]{3,2,1,0:T(8,128)(2,1)S(1)} %pad_maximum_fusion.28), channel_id=1, source_target_pairs={{0,8},{8,0},{1,9},{9,1},{2,10},{10,2},{3,11},{11,3},{4,12},{12,4},... | collective-permute-start | bytes 3145736 | tf_op jit(solution)/shard_map/ppermute | solution.py:51
  447.0 42.9 %collective-permute-start.46 = (bf16[2,2,128,1024]{3,2,1,0:T(8,128)(2,1)S(1)}, bf16[2,2,128,1024]{3,2,1,0:T(8,128)(2,1)S(1)}, u32[]{:S(2)}, u32[]{:S(2)}) collective-permute-start(bf16[2,2,128,1024]{3,2,1,0:T(8,128)(2,1)S(1)} %pad_maximum_fusion.29), channel_id=1, source_target_pairs={{0,16},{16,0},{1,17},{17,1},{2,18},{18,2},{3,19},{19,3},{4,20},{20... | collective-permute-start | bytes 3145736 | tf_op jit(solution)/shard_map/ppermute | solution.py:51
  464.5 37.8 %collective-permute-start.50 = (bf16[256,1024]{1,0:T(8,128)(2,1)}, bf16[256,1024]{1,0:T(8,128)(2,1)}, u32[]{:S(2)}, u32[]{:S(2)}) collective-permute-start(bf16[256,1024]{1,0:T(8,128)(2,1)} %slice_bitcast_fusion.12), channel_id=1, source_target_pairs={{0,3},{1,0},{2,1},{3,2},{4,7},{5,4},{6,5},{7,6},{8,11},{9,8},{10,9... | collective-permute-start | bytes 1572872 | tf_op jit(solution)/shard_map/ppermute | solution.py:51
  468.9 43.9 %collective-permute-start.51 = (bf16[256,1024]{1,0:T(8,128)(2,1)}, bf16[256,1024]{1,0:T(8,128)(2,1)S(1)}, u32[]{:S(2)}, u32[]{:S(2)}) collective-permute-start(bf16[256,1024]{1,0:T(8,128)(2,1)} %get-tuple-element.256), channel_id=1, source_target_pairs={{0,2},{1,3},{2,0},{3,1},{4,6},{5,7},{6,4},{7,5},{8,10},{9,11},{10,... | collective-permute-start | bytes 1572872 | tf_op jit(solution)/shard_map/ppermute | solution.py:51
  471.3 41.6 %collective-permute-start.52 = (bf16[256,1024]{1,0:T(8,128)(2,1)}, bf16[256,1024]{1,0:T(8,128)(2,1)S(1)}, u32[]{:S(2)}, u32[]{:S(2)}) collective-permute-start(bf16[256,1024]{1,0:T(8,128)(2,1)} %get-tuple-element.255), channel_id=1, source_target_pairs={{0,1},{1,2},{2,3},{3,0},{4,5},{5,6},{6,7},{7,4},{8,9},{9,10},{10,1... | collective-permute-start | bytes 1572872 | tf_op jit(solution)/shard_map/ppermute | solution.py:51
  528.0 45.7 %collective-permute-start.58 = (bf16[2,2,128,1024]{3,2,1,0:T(8,128)(2,1)}, bf16[2,2,128,1024]{3,2,1,0:T(8,128)(2,1)}, u32[]{:S(2)}, u32[]{:S(2)}) collective-permute-start(bf16[2,2,128,1024]{3,2,1,0:T(8,128)(2,1)} %pad_maximum_fusion.32), channel_id=1, source_target_pairs={{0,8},{8,0},{1,9},{9,1},{2,10},{10,2},{3,11},{11,3},{4,12},{12,4},... | collective-permute-start | bytes 3145736 | tf_op jit(solution)/shard_map/ppermute | solution.py:51
  529.2 58.5 %all-to-all-start.5 = ((bf16[8,64,1024]{2,1,0:T(8,128)(2,1)}), bf16[8,64,1024]{2,1,0:T(8,128)(2,1)}, u32[]{:S(2)}, u32[]{:S(2)}) async-start(bf16[8,64,1024]{2,1,0:T(8,128)(2,1)} %bitcast.286), calls=%async_computation.5 | async-start | bytes 2097152 | tf_op jit(solution)/shard_map/all_to_all | solution.py:76
  537.1 47.5 %collective-permute-start.61 = (bf16[2,2,128,1024]{3,2,1,0:T(8,128)(2,1)S(1)}, bf16[2,2,128,1024]{3,2,1,0:T(8,128)(2,1)S(1)}, u32[]{:S(2)}, u32[]{:S(2)}) collective-permute-start(bf16[2,2,128,1024]{3,2,1,0:T(8,128)(2,1)S(1)} %pad_maximum_fusion.33), channel_id=1, source_target_pairs={{0,16},{16,0},{1,17},{17,1},{2,18},{18,2},{3,19},{19,3},{4,20},{20... | collective-permute-start | bytes 3145736 | tf_op jit(solution)/shard_map/ppermute | solution.py:51
  538.6 53.7 %collective-permute-start.53 = (f32[3,1024]{1,0:T(4,128)S(1)}, f32[3,1024]{1,0:T(4,128)S(1)}, u32[]{:S(2)}, u32[]{:S(2)}) collective-permute-start(f32[3,1024]{1,0:T(4,128)S(1)} %pad_maximum_fusion.47), channel_id=1, source_target_pairs={{0,4},{4,0},{1,5},{5,1},{2,6},{6,2},{3,7},{7,3},{8,12},{12,8},{9,1... | collective-permute-start | bytes 36872 | tf_op jit(solution)/shard_map/ppermute | solution.py:227
  587.7 67.0 %all-to-all-start.4 = ((bf16[8,64,1024]{2,1,0:T(8,128)(2,1)}), bf16[8,64,1024]{2,1,0:T(8,128)(2,1)S(1)}, u32[]{:S(2)}, u32[]{:S(2)}) async-start(bf16[8,64,1024]{2,1,0:T(8,128)(2,1)} %bitcast.269), calls=%async_computation.4 | async-start | bytes 2097152 | tf_op jit(solution)/shard_map/all_to_all | solution.py:76
  591.4 95.1 %all-gather.5.cloned.1.call-start = ((), (), s32[]{:S(2)}) async-start(), calls=%async_computation.7 | async-start | bytes 2359296 | tf_op jit(solution)/shard_map/all_gather | solution.py:179
  604.0 58.6 %collective-permute-start.60 = (bf16[128,1024]{1,0:T(8,128)(2,1)S(1)}, bf16[128,1024]{1,0:T(8,128)(2,1)S(1)}, u32[]{:S(2)}, u32[]{:S(2)}) collective-permute-start(bf16[128,1024]{1,0:T(8,128)(2,1)S(1)} %slice_bitcast_fusion.22), channel_id=1, source_target_pairs={{0,3},{1,0},{2,1},{3,2},{4,7},{5,4},{6,5},{7,6},{8,11},{9,8},{10,9... | collective-permute-start | bytes 786440 | tf_op jit(solution)/shard_map/ppermute | solution.py:51
  621.4 41.2 %collective-permute-start.63 = (bf16[128,1024]{1,0:T(8,128)(2,1)S(1)}, bf16[128,1024]{1,0:T(8,128)(2,1)S(1)}, u32[]{:S(2)}, u32[]{:S(2)}) collective-permute-start(bf16[128,1024]{1,0:T(8,128)(2,1)S(1)} %get-tuple-element.274), channel_id=1, source_target_pairs={{0,2},{1,3},{2,0},{3,1},{4,6},{5,7},{6,4},{7,5},{8,10},{9,11},{10,... | collective-permute-start | bytes 786440 | tf_op jit(solution)/shard_map/ppermute | solution.py:51
  621.5 41.1 %collective-permute-start.64 = (bf16[128,1024]{1,0:T(8,128)(2,1)S(1)}, bf16[128,1024]{1,0:T(8,128)(2,1)S(1)}, u32[]{:S(2)}, u32[]{:S(2)}) collective-permute-start(bf16[128,1024]{1,0:T(8,128)(2,1)S(1)} %get-tuple-element.273), channel_id=1, source_target_pairs={{0,1},{1,2},{2,3},{3,0},{4,5},{5,6},{6,7},{7,4},{8,9},{9,10},{10,1... | collective-permute-start | bytes 786440 | tf_op jit(solution)/shard_map/ppermute | solution.py:51
  (180 other events, 1975.3 us)
Sparse Core Ops, SparseCore 0:
  515.4 62.3 all-gather.2
  602.9 45.1 all-gather.4

commit v4 on v3

--- a/solution.py
+++ b/solution.py
@@ -27,23 +27,64 @@
     )
 
 
-def normalize(activity, gain):
-    centre = jnp.mean(activity, -1, keepdims=True)
-    shifted = activity - centre
-    variance = jnp.mean(shifted * shifted, -1, keepdims=True)
-    return (shifted * lax.rsqrt(variance + EPSILON) * gain).astype(BF)
-
-
-def normalize_back(activity, gain, grad):
-    centre = jnp.mean(activity, -1, keepdims=True)
-    shifted = activity - centre
-    variance = jnp.mean(shifted * shifted, -1, keepdims=True)
-    rate = lax.rsqrt(variance + EPSILON)
+STEP = 128
+
+
+def centred(activity):
+    shifted = activity - jnp.mean(activity, -1, keepdims=True)
+    return shifted, lax.rsqrt(jnp.mean(shifted * shifted, -1, keepdims=True) + EPSILON)
+
+
+def norm_kernel(terms, gain_ref, *refs):
+    activity = refs[0][...].astype(F32)
+    for ref in refs[1:terms]:
+        activity = activity + ref[...].astype(F32)
+    shifted, rate = centred(activity)
+    refs[terms][...] = (shifted * rate * gain_ref[...]).astype(BF)
+    if terms > 1:
+        refs[terms + 1][...] = activity
+
+
+def norm_back_kernel(gain_ref, activity_ref, own_ref, other_ref, onward_ref, grad_ref, rounded_ref, gain_grad_ref):
+    shifted, rate = centred(activity_ref[...].astype(F32))
     unit = shifted * rate
-    scaled = grad * gain
+    arrived = own_ref[...] + other_ref[...].astype(F32)
+    scaled = arrived * gain_ref[...]
     inner = scaled - jnp.mean(scaled, -1, keepdims=True)
-    grad_activity = rate * (inner - unit * jnp.mean(scaled * unit, -1, keepdims=True))
-    return grad_activity, jnp.sum(grad * unit, 0)
+    step = rate * (inner - unit * jnp.mean(scaled * unit, -1, keepdims=True))
+    total = onward_ref[...].astype(F32) + step
+    grad_ref[...] = total
+    rounded_ref[...] = total.astype(BF)
+
+    @pl.when(pl.program_id(0) == 0)
+    def _():
+        gain_grad_ref[...] = jnp.zeros(gain_grad_ref.shape, F32)
+
+    gain_grad_ref[...] += jnp.sum(arrived * unit, 0, keepdims=True)
+
+
+def by_rows(kernel, gain, arrays, outs, sums=0):
+    tokens, width = arrays[0].shape
+    tile, line = pl.BlockSpec((STEP, width), lambda i: (i, 0)), pl.BlockSpec((1, width), lambda i: (0, 0))
+    return pl.pallas_call(
+        kernel,
+        out_shape=[jax.ShapeDtypeStruct((tokens, width), t) for t in outs]
+        + [jax.ShapeDtypeStruct((1, width), F32)] * sums,
+        grid=(tokens // STEP,),
+        in_specs=[line] + [tile] * len(arrays),
+        out_specs=[tile] * len(outs) + [line] * sums,
+        compiler_params=pltpu.CompilerParams(vmem_limit_bytes=32 * 2**20),
+        cost_estimate=pl.CostEstimate(flops=20 * tokens * width, bytes_accessed=8 * tokens * width, transcendentals=tokens),
+    )(gain.reshape(1, width), *arrays)
+
+
+def normalize(terms, gain):
+    return by_rows(functools.partial(norm_kernel, len(terms)), gain, terms, [BF] + [F32] * (len(terms) > 1))
+
+
+def normalize_back(activity, gain, arrived, onward):
+    grad, rounded, gain_grad = by_rows(norm_back_kernel, gain, [activity, *arrived, onward], [F32, BF], 1)
+    return grad, rounded, gain_grad[0]
 
 
 def shift(piece, axis, step):
@@ -59,10 +100,15 @@
     return jnp.concatenate([own, core_swap(own)], 0)
 
 
-def own_sum(transposed, matrix):
+def own_parts(transposed, matrix):
     half = transposed.shape[1] // 2
     other = core_swap(dot(transposed[:, half:], matrix, 0, 0).astype(BF))
-    return dot(transposed[:, :half], matrix, 0, 0) + other.astype(F32)
+    return [dot(transposed[:, :half], matrix, 0, 0), other]
+
+
+def own_sum(transposed, matrix):
+    own, other = own_parts(transposed, matrix)
+    return own + other.astype(F32)
 
 
 def to_row(tokens):
@@ -229,23 +275,22 @@
     return value
 
 
-def head_rows(ref, half, index, kind):
-    x, z = index
-    if ref.shape[5] == HEAD_DIM:
-        return (0, 0, x, z, kind)
-    return (0, slice(None), x, z, kind) if half == 0 else (0, x, slice(None), z, kind)
-
-
-def read_head(ref, half, index, kind):
-    return ref[head_rows(ref, half, index, kind)].reshape(HEAD_DIM, LEN)
-
-
-def write_head(ref, half, index, kind, value):
-    at = head_rows(ref, half, index, kind)
-    if ref.shape[5] == HEAD_DIM:
-        ref[at] = value
-    else:
-        ref[at] = value.reshape(-1, ref.shape[5], LEN)
+class Rows:
+    def __init__(self, nx, ny, nz, kinds):
+        self.nx, self.ny, self.depth, self.kinds = nx, ny, nz // 2, kinds
+        self.size = HEAD_DIM // ny
+
+    def starts(self, half, index, kind):
+        x, z = index
+        slots = [y * self.nx + x if half == 0 else x * self.ny + y for y in range(self.ny)]
+        return [((slot * self.depth + z) * self.kinds + kind) * self.size for slot in slots]
+
+    def read(self, ref, half, index, kind):
+        return jnp.concatenate([ref[at : at + self.size, :] for at in self.starts(half, index, kind)], 0)
+
+    def write(self, ref, half, index, kind, value):
+        for k, at in enumerate(self.starts(half, index, kind)):
+            ref[at : at + self.size, :] = value[k * self.size : (k + 1) * self.size]
 
 
 def allowed_block(span_ref, base, columns, chunk):
@@ -273,15 +318,16 @@
         work(lambda scores: scores)
 
 
-def attend_kernel(heads, kinds, chunk, need_ref, base_ref, span_ref, *refs):
-    sources = refs[: len(kinds)]
-    mixed_ref, lse_ref, q_s, k_s, v_s, top_s, sum_s, acc_s = refs[len(kinds) :]
-    where = [(source, kind) for source, count in zip(sources, kinds) for kind in range(count)]
+def attend_kernel(heads, layouts, chunk, need_ref, base_ref, span_ref, *refs):
+    *layouts, single = layouts
+    count = len(layouts)
+    mixed_ref, lse_ref, q_s, k_s, v_s, top_s, sum_s, acc_s = refs[count:]
+    where = [(source, lay, kind) for source, lay in zip(refs[:count], layouts) for kind in range(lay.kinds)]
     every = range(len(heads))
 
     def load(half):
         for h, index in enumerate(heads):
-            q, k, v = (read_head(source, half, index, kind) for source, kind in where)
+            q, k, v = (lay.read(source, half, index, kind) for source, lay, kind in where)
             q_s[h] = (q.astype(F32) * SCALE).astype(BF)
             k_s[h] = k.T
             v_s[h] = v
@@ -317,31 +363,32 @@
 
     def store(half):
         for h, index in enumerate(heads):
-            write_head(mixed_ref, half, index, 0, q_s[h])
+            single.write(mixed_ref, half, index, 0, q_s[h])
 
     for half in range(2):
         pl.when(half_now == half)(functools.partial(store, half))
 
 
-def attend_back_kernel(heads, kinds, chunk, need_ref, base_ref, span_ref, *refs):
-    sources = refs[: len(kinds)]
-    mixed_ref, grad_ref, lse_ref = refs[len(kinds) : len(kinds) + 3]
-    outs = refs[len(kinds) + 3 : 2 * len(kinds) + 3]
-    q_s, k_s, kt_s, v_s, g_s, inner_s, dq_s, dk_s, dv_s = refs[2 * len(kinds) + 3 :]
-    where = [(source, kind) for source, count in zip(sources, kinds) for kind in range(count)]
-    into = [(out, kind) for out, count in zip(outs, kinds) for kind in range(count)]
+def attend_back_kernel(heads, layouts, chunk, need_ref, base_ref, span_ref, *refs):
+    *layouts, single = layouts
+    count = len(layouts)
+    mixed_ref, grad_ref, lse_ref = refs[count : count + 3]
+    q_s, k_s, kt_s, v_s, g_s, inner_s, dq_s, dk_s, dv_s = refs[2 * count + 3 :]
+    where = [(source, lay, kind) for source, lay in zip(refs[:count], layouts) for kind in range(lay.kinds)]
+    outs = refs[count + 3 : 2 * count + 3]
+    into = [(out, lay, kind) for out, lay in zip(outs, layouts) for kind in range(lay.kinds)]
     every = range(len(heads))
 
     def load(half):
         for h, index in enumerate(heads):
-            q, k, v = (read_head(source, half, index, kind) for source, kind in where)
+            q, k, v = (lay.read(source, half, index, kind) for source, lay, kind in where)
             q_s[h] = (q.astype(F32) * SCALE).astype(BF)
             kt_s[h] = k
             k_s[h] = k.T
             v_s[h] = v.T
-            grad = read_head(grad_ref, half, index, 0)
+            grad = single.read(grad_ref, half, index, 0)
             g_s[h] = grad
-            mixed = read_head(mixed_ref, half, index, 0)
+            mixed = single.read(mixed_ref, half, index, 0)
             inner_s[h] = jnp.sum(grad.astype(F32) * mixed.astype(F32), 0, keepdims=True)
 
     half_now = pl.program_id(0)
@@ -373,49 +420,47 @@
     def store(half):
         for h, index in enumerate(heads):
             made = (dq_s[h] * SCALE, dk_s[h], dv_s[h])
-            for (out, kind), value in zip(into, made):
-                write_head(out, half, index, kind, value.astype(BF))
+            for (out, lay, kind), value in zip(into, made):
+                lay.write(out, half, index, kind, value.astype(BF))
 
     for half in range(2):
         pl.when(half_now == half)(functools.partial(store, half))
-
-
-def by_half(shape):
-    rest = (0,) * (len(shape) - 1)
-    return pl.BlockSpec((1,) + tuple(shape[1:]), lambda i, *_: (i,) + rest)
 
 
 class Heads:
     def __init__(self, nx, ny, nz, chunk):
         self.nx, self.ny, self.nz, self.chunk = nx, ny, nz, chunk
         self.index = [(x, z) for x in range(nx) for z in range(nz // 2)]
+        self.plain = (HEAD_DIM // ny) % 16 == 0
 
     def split(self, matrix, kinds):
-        nx, ny, nz = self.nx, self.ny, self.nz
-        rows = HEAD_DIM // ny
-        if nx == ny and rows % 16 == 0:
-            return matrix.reshape(2, ny, nx, nz // 2, kinds, rows, LEN)
-        half = matrix.shape[0] // 2
-        first = matrix[:half].reshape(ny, nx, nz // 2, kinds, rows, LEN).transpose(1, 2, 3, 0, 4, 5)
-        second = matrix[half:].reshape(nx, ny, nz // 2, kinds, rows, LEN).transpose(0, 2, 3, 1, 4, 5)
-        both_halves = jnp.stack([first, second], 0)
-        return both_halves.reshape(2, 1, nx, nz // 2, kinds, HEAD_DIM, LEN)
-
-    def join(self, split):
-        nx, ny, nz = self.nx, self.ny, self.nz
-        rows = HEAD_DIM // ny
-        if split.shape[5] == rows:
-            return split.reshape(-1, LEN)
-        kinds = split.shape[4]
-        cut = split.reshape(2, nx, nz // 2, kinds, ny, rows, LEN)
+        if self.plain:
+            return matrix
+        nx, ny, deep = self.nx, self.ny, self.nz // 2
+        half, rows = matrix.shape[0] // 2, HEAD_DIM // ny
+        first = matrix[:half].reshape(ny, nx, deep, kinds, rows, LEN).transpose(1, 2, 3, 0, 4, 5)
+        second = matrix[half:].reshape(nx, ny, deep, kinds, rows, LEN).transpose(0, 2, 3, 1, 4, 5)
+        return jnp.stack([first, second], 0).reshape(-1, LEN)
+
+    def join(self, split, kinds):
+        if self.plain:
+            return split
+        nx, ny, deep = self.nx, self.ny, self.nz // 2
+        cut = split.reshape(2, nx, deep, kinds, ny, HEAD_DIM // ny, LEN)
         first = cut[0].transpose(3, 0, 1, 2, 4, 5).reshape(-1, LEN)
         second = cut[1].transpose(0, 3, 1, 2, 4, 5).reshape(-1, LEN)
         return jnp.concatenate([first, second], 0)
 
     def call(self, kernel, kinds, tables, arrays, outs, scratch, flops):
         need, bases, spans = tables
+        layouts = [Rows(self.nx, self.ny if self.plain else 1, self.nz, k) for k in kinds + (1,)]
+
+        def by_half(shape):
+            rest = (0,) * (len(shape) - 1)
+            return pl.BlockSpec((shape[0] // 2,) + tuple(shape[1:]), lambda i, *_: (i,) + rest)
+
         return pl.pallas_call(
-            functools.partial(kernel, self.index, kinds, self.chunk),
+            functools.partial(kernel, self.index, layouts, self.chunk),
             out_shape=outs,
             grid_spec=pltpu.PrefetchScalarGridSpec(
                 num_scalar_prefetch=2,
@@ -431,7 +476,6 @@
     def attend(self, tables, sources, kinds):
         count = len(self.index)
         split = [self.split(s, k) for s, k in zip(sources, kinds)]
-        like = split[0].shape
         wide = (count, HEAD_DIM, LEN)
         mixed, lse = self.call(
             attend_kernel,
@@ -439,7 +483,7 @@
             tables,
             split,
             [
-                jax.ShapeDtypeStruct(like[:4] + (1,) + like[5:], BF),
+                jax.ShapeDtypeStruct((2 * count * HEAD_DIM, LEN), BF),
                 jax.ShapeDtypeStruct((2, count, 1, LEN), F32),
             ],
             [
@@ -452,7 +496,7 @@
             ],
             40 * 10**9,
         )
-        return self.join(mixed), lse
+        return self.join(mixed, 1), lse
 
     def attend_back(self, tables, sources, kinds, mixed, grad, lse):
         count = len(self.index)
@@ -477,7 +521,7 @@
             ],
             46 * 10**9,
         )
-        return [self.join(g) for g in grads]
+        return [self.join(g, k) for g, k in zip(grads, kinds)]
 
 
 def body(
@@ -554,7 +598,7 @@
 
     residual = to_row(inputs).astype(F32)
     self_weights = Gather([column_parts(w_query, w_key, w_value)])
-    residual = to_row(tied(inputs, self_weights.mine)).astype(F32)
+    residual = to_row(tied(inputs, self_weights.got))
     self_weights.two()
     residual = meet(residual, self_weights)
     self_weights.three()
@@ -562,40 +606,45 @@
         [part(w_out), column_parts(w_mem_key, w_mem_value), column_parts(w_cross_query), part(w_cross_out)],
         residual,
     )
-    normed_one = both(normalize(tied(residual, self_weights.mine, cross_weights.mine), gain_one))
+    (normed_one,) = normalize([tied(residual, self_weights.mine, cross_weights.mine)], gain_one)
+    normed_one = both(normed_one)
     normed_one = meet(normed_one, self_weights)
     (w_self,) = self_weights.result()
     qkv = dot(w_self, normed_one, 1, 1).astype(BF)
     qkv = meet(qkv, cross_weights)
     cross_weights.two()
     up_weights = Gather([column_parts(w_up)], cross_weights.mine)
-    qkv = tied(qkv, cross_weights.mine, up_weights.mine)
+    source_own = to_row(tied(memory, up_weights.mine))
+    qkv = meet(qkv, cross_weights)
+    cross_weights.three()
+    qkv = tied(qkv, cross_weights.mine)
     self_mixed, self_lse = heads.attend(self_tables, (qkv,), (3,))
-    self_mixed = meet(self_mixed, cross_weights, up_weights)
-    cross_weights.three()
-    down_weights = Gather([part(w_down)], up_weights.got, cross_weights.mine)
-    self_mixed = meet(self_mixed, cross_weights)
+    self_mixed, source_own = meet((self_mixed, source_own), cross_weights, up_weights)
+    down_weights = Gather([part(w_down)], up_weights.got)
     up_weights.two()
-    source_own = to_row(tied(memory, self_mixed))
-    self_mixed = tied(self_mixed, up_weights.mine)
+    self_mixed = tied(self_mixed, up_weights.mine, down_weights.mine)
     w_o, w_mem, w_cq, w_co = cross_weights.result()
-    after_self = residual + own_sum(self_mixed, w_o)
-    normed_two = meet(normalize(after_self, gain_two), up_weights, down_weights)
+    normed_two, after_self = normalize([residual, *own_parts(self_mixed, w_o)], gain_two)
+    normed_two = meet(normed_two, up_weights, down_weights)
     up_weights.three()
     down_weights.two()
     normed_two, source_own = tied((normed_two, source_own), up_weights.mine, down_weights.mine)
+    cot_own = to_row(tied(cotangent, up_weights.mine, source_own))
     source = both(source_own)
     mkv = dot(w_mem, source, 1, 1).astype(BF)
     normed_two = both(normed_two)
     cq = dot(w_cq, normed_two, 1, 1).astype(BF)
     cross_mixed, cross_lse = heads.attend(cross_tables, (cq, mkv), (1, 2))
-    cross_mixed = meet(cross_mixed, up_weights, down_weights)
+    cross_mixed, cot_own = meet((cross_mixed, cot_own), up_weights, down_weights)
     down_weights.three()
     cross_mixed = tied(cross_mixed, down_weights.mine)
-    cot_own = to_row(tied(cotangent, down_weights.mine))
-    after_cross = after_self + own_sum(cross_mixed, w_co)
-    normed_three = both(normalize(after_cross, gain_three))
+    cot = both(cot_own)
+    normed_three, after_cross = normalize([after_self, *own_parts(cross_mixed, w_co)], gain_three)
+    normed_three = both(normed_three)
     (w_u,) = up_weights.result()
+
+    def weight_grad(transposed, tokens):
+        return dot(transposed, tokens, 1, 0).astype(BF)
 
     hidden_pre = dot(w_u, normed_three, 1, 1)
     squared = hidden_pre * hidden_pre
@@ -603,61 +652,66 @@
     gate = 0.5 + 0.5 * bent
     slope = gate + (0.5 * GELU_A) * hidden_pre * (1.0 - bent * bent) * (1.0 + 3.0 * GELU_B * squared)
     hidden_act, slope = lax.optimization_barrier(((hidden_pre * gate).astype(BF), slope.astype(BF)))
-    hidden_act = meet(hidden_act, down_weights)
+    down_sum = Sum([weight_grad(hidden_act, cot)])
+    hidden_act = meet(tied(hidden_act, down_sum.mine), down_weights)
     (w_d,) = down_weights.result()
-    cot = both(tied(cot_own, hidden_act))
     output = (after_cross + own_sum(hidden_act, w_d)).astype(BF)
     output = from_row(output, rows)
 
-    def weight_grad(transposed, tokens):
-        return dot(transposed, tokens, 1, 0).astype(BF)
-
-    g_down = weight_grad(hidden_act, cot)
     grad_pre = (slope.astype(F32) * dot(w_d, cot, 1, 1)).astype(BF)
-    g_up = weight_grad(grad_pre, normed_three)
-    ffn_sum = Sum([g_down, g_up])
-    step, grad_gain_three = normalize_back(after_cross, gain_three, own_sum(grad_pre, w_u))
-    grad_after_cross = cot_own.astype(F32) + step
-
-    cross_grad = both(grad_after_cross.astype(BF))
+    grad_pre = meet(grad_pre, down_sum)
+    down_sum.two()
+    third_back = own_parts(tied(grad_pre, down_sum.mine), w_u)
+    grad_after_cross, cross_grad, grad_gain_three = normalize_back(after_cross, gain_three, third_back, cot_own)
+
+    cross_grad = both(cross_grad)
+    up_sum = Sum([weight_grad(tied(grad_pre, down_sum.mine), normed_three)])
     grad_cross_mixed = dot(w_co, cross_grad, 1, 1).astype(BF)
+    grad_cross_mixed = meet(grad_cross_mixed, down_sum)
+    down_sum.three()
+    grad_cross_mixed = tied(grad_cross_mixed, up_sum.mine, down_sum.mine)
     gcq, gmkv = heads.attend_back(
         cross_tables, (cq, mkv), (1, 2), cross_mixed, grad_cross_mixed, cross_lse
     )
-    gcq, gmkv, output = meet((gcq, gmkv, output), ffn_sum)
-    ffn_sum.two()
-    gcq, gmkv = tied((gcq, gmkv), ffn_sum.mine)
-    step, grad_gain_two = normalize_back(after_self, gain_two, own_sum(gcq, w_cq))
-    grad_after_self = grad_after_cross + step
-    grad_after_self = meet(grad_after_self, ffn_sum)
-    ffn_sum.three()
-    self_grad = both(grad_after_self.astype(BF))
+    gcq, gmkv, output = meet((gcq, gmkv, output), up_sum, down_sum)
+    up_sum.two()
+    down_all = gathered(down_sum.result())
+    gcq, gmkv = tied((gcq, gmkv), up_sum.mine)
+    grad_after_self, self_grad, grad_gain_two = normalize_back(
+        after_self, gain_two, own_parts(gcq, w_cq), grad_after_cross
+    )
+    self_grad = meet(self_grad, up_sum)
+    up_sum.three()
+    self_grad = both(self_grad)
     g_co = weight_grad(cross_mixed, cross_grad)
     g_cq = weight_grad(gcq, normed_two)
     g_mem = weight_grad(gmkv, source)
+    g_o = weight_grad(self_mixed, self_grad)
     cross_sum = Sum([g_co, g_cq, g_mem])
     memory_back = own_sum(gmkv, w_mem).astype(BF)
     grad_self_mixed = dot(w_o, self_grad, 1, 1).astype(BF)
-    grad_self_mixed, memory_back = tied((grad_self_mixed, memory_back), ffn_sum.mine, cross_sum.mine)
-    grad_memory = from_row(memory_back, rows).astype(F32)
+    grad_self_mixed, memory_back = tied((grad_self_mixed, memory_back), up_sum.mine, cross_sum.mine, g_o)
+    grad_memory = from_row(memory_back, rows)
     (gqkv,) = heads.attend_back(self_tables, (qkv,), (3,), self_mixed, grad_self_mixed, self_lse)
-    gqkv = meet(gqkv, cross_sum)
+    gqkv, down_all = meet((gqkv, down_all), cross_sum, up_sum)
     cross_sum.two()
+    up_all = gathered(up_sum.result())
     g_self = weight_grad(gqkv, normed_one)
-    g_o = weight_grad(self_mixed, self_grad)
     self_sum = Sum([g_o, g_self])
-    first_back = own_sum(gqkv, w_self)
-    first_back = meet(tied(first_back, self_sum.mine), cross_sum, ffn_sum)
-    cross_sum.three()
-    step, grad_gain_one = normalize_back(residual, gain_one, first_back)
-    grad_inputs = from_row((grad_after_self + step).astype(BF), rows).astype(F32)
+    first_back = own_parts(tied(gqkv, self_sum.mine), w_self)
+    first_back, grad_memory = lax.optimization_barrier((first_back, grad_memory))
+    _, grad_inputs, grad_gain_one = normalize_back(residual, gain_one, first_back, grad_after_self)
+    grad_inputs = from_row(grad_inputs, rows).astype(F32)
     gains = total_of(jnp.stack([grad_gain_one, grad_gain_two, grad_gain_three]))
     self_sum.two()
+    cross_sum.got = tied(cross_sum.got, self_sum.mine)
+    cross_sum.three()
     self_sum.three()
 
     deep = w_query.shape[1] // 2 // nxy
     far = w_up.shape[1] // 2 // nxy
-    grad_down, grad_up = unfold(gathered(ffn_sum.result()), [(far, False), (far, True)])
+    (grad_down,) = unfold(down_all, [(far, False)])
+    (grad_up,) = unfold(up_all, [(far, True)])
     grad_co, grad_cq, grad_mk, grad_mv = unfold(
         gathered(cross_sum.result()), [(deep, False), (deep, True), (deep, True), (deep, True)]
     )
@@ -668,7 +722,7 @@
     return (
         output,
         grad_inputs,
-        grad_memory,
+        grad_memory.astype(F32),
         gains[0],
         grad_q,
         grad_k,

time: 714 us -> 659 us (0.923)
  waiting for transfers between devices: 242 us -> 155 us
  Pallas kernels: 80.8 us -> 97 us
  local copies, waits for them, and re-layouts: 55.5 us -> 66.5 us
  starting transfers between devices: 131 us -> 142 us
    ppermute x66 -> x73, waiting for transfers between devices: 197 us -> 140 us  [shift(): lax.ppermute(piece, axis, [(i, (i + step) % count) for i in range(count)])]
    ppermute x66 -> x73, starting transfers between devices: 87.1 us -> 107 us  [shift(): lax.ppermute(piece, axis, [(i, (i + step) % count) for i in range(count)])]
    ppermute x5, waiting for transfers between devices: 27.1 us -> 11 us  [total_of(): lax.ppermute(value, axis, [(i, i ^ step) for i in range(count)])]
    pallas_call x4 -> x10, Pallas kernels: 71.2 us -> 85.8 us  [the longest x4 72 us: call(): pl.pallas_call(functools.partial(kernel, self.index, layouts, self.chunk)...]
    all_to_all x3, waiting for transfers between devices: 17.6 us -> 3.44 us  [to_row(): moved = lax.all_to_all(tokens, ('yy', 'head'), 0, 0, tiled=True)]
    all_to_all x3, starting transfers between devices: 23.7 us -> 12.6 us  [to_row(): moved = lax.all_to_all(tokens, ('yy', 'head'), 0, 0, tiled=True)]
    convert_element_type x9 -> x2, other arithmetic: 14.5 us -> 5.58 us  [the longest x1 2.79 us: body(): grad_inputs = from_row(grad_inputs, rows).astype(F32)]
    another operation x20, other arithmetic: 23.5 us -> 31.7 us  [three(): self.send(jnp.stack(first, 0), jnp.stack(second, 0), 'yy', 'batch')]
  transfers between devices with their start and end apart: 79 -> 87, of which waited for: 24 -> 27; matrix products, arithmetic and copies ran while one was open for 27% -> 26% of each run, Pallas kernels for 11% -> 14%
where the time goes in v4:
time: 659 us; the launch traced here: 649 us
  waiting for transfers between devices  155 us (24%)
  starting transfers between devices  142 us (22%)
  matrix products  99.7 us (15%)
  Pallas kernels  97 us (15%)
  other arithmetic  72.6 us (11%)
  local copies, waits for them, and re-layouts  66.5 us (10%)
  between operations  15.8 us (2%)
    ppermute x73, waiting for transfers between devices, shift(): lax.ppermute(piece, axis, [(i, (i + step) % count) for i in range(count)])  140 us
    ppermute x73, starting transfers between devices, shift(): lax.ppermute(piece, axis, [(i, (i + step) % count) for i in range(count)])  107 us
    dot_general x28, matrix products, dot(): lax.dot_general(left, right, (((left_dim,), (right_dim,)), ((), ())), pre...  99.7 us
    pallas_call x4, Pallas kernels, call(): pl.pallas_call(functools.partial(kernel, self.index, layouts, self.chunk)...  72 us
    another operation x20, other arithmetic, three(): self.send(jnp.stack(first, 0), jnp.stack(second, 0), 'yy', 'batch')  31.7 us
    unnamed x270, local copies, waits for them, and re-layouts  29.2 us
    convert_element_type x20, other arithmetic, add(): return total.astype(BF)  24.7 us
    all_to_all x3, starting transfers between devices, from_row(): return lax.all_to_all(parts, ('yy', 'head'), 0, 0, tiled=True)  14.3 us
  transfers between devices with their start and end apart: 87, of which 27 were waited for; matrix products, arithmetic and copies ran while one was open for 26% of the time, Pallas kernels for 14%

profile of v4, /device:TPU:1, one launch (start us, length us, event | category | flops | bytes accessed | tf_op | source)
XLA Modules:
  0.0 649.2 jit_solution(8248099933340027984)
XLA Ops:
  17.7 13.0 %collective-permute-done.1 = bf16[96,1024]{1,0:T(8,128)(2,1)S(1)} collective-permute-done((bf16[96,1024]{1,0:T(8,128)(2,1)S(1)}, bf16[96,1024]{1,0:T(8,128)(2,1)S(1)}, u32[]{:S(2)}, u32[]{:S(2)}) %collective-permute-start.1) | collective-permute-done | bytes 196640 | tf_op jit(solution)/shard_map/ppermute | solution.py:92
  31.5 4.7 all-to-all-start
  54.4 7.8 %collective-permute-done.4 = bf16[2,96,1024]{2,1,0:T(8,128)(2,1)} collective-permute-done((bf16[2,96,1024]{2,1,0:T(8,128)(2,1)}, bf16[2,96,1024]{2,1,0:T(8,128)(2,1)}, u32[]{:S(2)}, u32[]{:S(2)}) %collective-permute-start.4) | collective-permute-done | bytes 393248 | tf_op jit(solution)/shard_map/ppermute | solution.py:92
  77.9 13.8 %collective-permute-done.7 = bf16[2,2,96,1024]{3,2,1,0:T(8,128)(2,1)} collective-permute-done((bf16[2,2,96,1024]{3,2,1,0:T(8,128)(2,1)}, bf16[2,2,96,1024]{3,2,1,0:T(8,128)(2,1)}, u32[]{:S(2)}, u32[]{:S(2)}) %collective-permute-start.7) | collective-permute-done | bytes 786464 | tf_op jit(solution)/shard_map/ppermute | solution.py:92
  91.7 7.0 %convolution_convert_fusion.1.refs_0_ = bf16[1536,1024]{1,0:T(8,128)(2,1)} fusion(bf16[1024,1024]{1,0:T(8,128)(2,1)S(1)} %pad_maximum_fusion.3, bf16[384,1024]{1,0:T(8,128)(2,1)} %bitcast.24, bf16[384,1024]{1,0:T(8,128)(2,1)} %bitcast.23, bf16[384,1024]{1,0:T(8,128)(2,1)} %bitcast.22, bf16[384,1024]{1,0:T(8,128)(2,1)} %bitcast.18), kind=kOutput, calls=%fused_computation.8 | convolution fusion | flops 3235381248 | bytes 8388608 | tf_op jit(solution)/shard_map/dot_general | solution.py:25
  98.7 4.5 collective-permute-done.9
  112.9 4.3 all-to-all-start.1
  127.1 22.8 %shard_map.298 = (bf16[512,1024]{1,0:T(8,128)(2,1)S(1)}, f32[2,4,1,1024]{3,2,1,0:T(1,128)S(1)}) custom-call(s32[16]{0:T(128)S(1)} %select_n.214.need_ref, s32[4]{0:T(128)S(1)} %get-tuple-element.336.base_ref, s32[2,1024]{1,0:T(2,128)S(1)} %pad_add_fusion.1.span_ref, bf16[1536,1024]{1,0:T(8,128)(2,1)S(1)} %copy-done.37), custom_call_target="tpu_custom_call" | custom-call | flops 40000000000 | bytes 8388608 | tf_op jit(solution)/shard_map/pallas_call | solution.py:462
  164.7 6.6 %collective-permute-start.18 = (bf16[512,1024]{1,0:T(8,128)(2,1)S(1)}, bf16[512,1024]{1,0:T(8,128)(2,1)S(1)}, u32[]{:S(2)}, u32[]{:S(2)}) collective-permute-start(bf16[512,1024]{1,0:T(8,128)(2,1)S(1)} %convolution_convert_fusion.15), channel_id=1, source_target_pairs={{0,4},{4,0},{1,5},{5,1},{2,6},{6,2},{3,7},{7,3},{8,12},{12,8},{9,1... | collective-permute-start | bytes 3145736 | tf_op jit(solution)/shard_map/ppermute | solution.py:92
  173.9 4.3 collective-permute-start.22
  183.0 17.9 %collective-permute-done.22 = bf16[128,1024]{1,0:T(8,128)(2,1)S(1)} collective-permute-done((bf16[128,1024]{1,0:T(8,128)(2,1)S(1)}, bf16[128,1024]{1,0:T(8,128)(2,1)S(1)}, u32[]{:S(2)}, u32[]{:S(2)}) %collective-permute-start.22) | collective-permute-done | bytes 262176 | tf_op jit(solution)/shard_map/ppermute | solution.py:92
  232.0 12.9 %shard_map.300 = (bf16[512,1024]{1,0:T(8,128)(2,1)S(1)}, f32[2,4,1,1024]{3,2,1,0:T(1,128)S(1)}) custom-call(s32[16]{0:T(128)S(1)} %select_n.206.need_ref, s32[4]{0:T(128)S(1)} %get-tuple-element.336.base_ref, s32[2,1024]{1,0:T(2,128)S(1)} %pad_add_fusion.span_ref, bf16[512,1024]{1,0:T(8,128)(2,1)S(1)} %convolution_convert_fusion.12.refs_0_, ...), custom_call_target="tpu_custom_call" | custom-call | flops 40000000000 | bytes 8388608 | tf_op jit(solution)/shard_map/pallas_call | solution.py:462
  249.8 11.8 %collective-permute-done.26 = bf16[2,2,128,1024]{3,2,1,0:T(8,128)(2,1)} collective-permute-done((bf16[2,2,128,1024]{3,2,1,0:T(8,128)(2,1)S(1)}, bf16[2,2,128,1024]{3,2,1,0:T(8,128)(2,1)}, u32[]{:S(2)}, u32[]{:S(2)}) %collective-permute-start.26) | collective-permute-done | bytes 1048608 | tf_op jit(solution)/shard_map/ppermute | solution.py:92
  274.0 13.1 %add_convert_fusion = (bf16[2048,1024]{1,0:T(8,128)(2,1)}, bf16[2048,1024]{1,0:T(8,128)(2,1)}) fusion(bf16[1024,1024]{1,0:T(8,128)(2,1)S(1)} %constant_dynamic-update-slice_fusion.4, bf16[512,1024]{1,0:T(8,128)(2,1)} %bitcast.73, bf16[512,1024]{1,0:T(8,128)(2,1)} %bitcast.72, bf16[512,1024]{1,0:T(8,128)(2,1)} %bitcast.71, bf16[512,1024]{1,0:T(8,128)(2,1)S(1)} %bitcast.280), kind=kOutput, calls=%fused_computation.1 | convolution fusion | flops 4349493248 | bytes 14680064 | tf_op jit(solution)/shard_map/dot_general | solution.py:25
  287.1 6.9 %convolution_convert_fusion.3 = bf16[2048,1024]{1,0:T(8,128)(2,1)S(1)} fusion(bf16[2048,1024]{1,0:T(8,128)(2,1)} %get-tuple-element.197, bf16[1024,1024]{1,0:T(8,128)(2,1)S(1)} %constant_dynamic-update-slice_fusion.6), kind=kOutput, calls=%fused_computation.10 | convolution fusion | flops 4297064448 | bytes 10485760 | tf_op jit(solution)/shard_map/dot_general | solution.py:25
  302.2 12.1 %multiply_convert_fusion = bf16[2048,1024]{1,0:T(8,128)(2,1)} fusion(bf16[2048,1024]{1,0:T(8,128)(2,1)} %get-tuple-element.180, bf16[1024,1024]{1,0:T(8,128)(2,1)S(1)} %constant_dynamic-update-slice_fusion.6, bf16[512,1024]{1,0:T(8,128)(2,1)S(1)} %bitcast.384, bf16[512,1024]{1,0:T(8,128)(2,1)S(1)} %bitcast.289, bf16[512,1024]{1,0:T(8,128)(2,1)S(1)} %bitcast.387, ...), kind=kOutput, calls=%fused_computation | convolution fusion | flops 4318035968 | bytes 14680064 | tf_op jit(solution)/shard_map/dot_general | solution.py:25
  344.5 4.7 convolution_convert_fusion.2
  357.2 19.3 %shard_map.303 = (bf16[512,1024]{1,0:T(8,128)(2,1)S(1)}, bf16[1024,1024]{1,0:T(8,128)(2,1)}) custom-call(s32[16]{0:T(128)S(1)} %select_n.206.need_ref, s32[4]{0:T(128)S(1)} %get-tuple-element.336.base_ref, s32[2,1024]{1,0:T(2,128)S(1)} %pad_add_fusion.span_ref, bf16[512,1024]{1,0:T(8,128)(2,1)S(1)} %copy-done.32, bf16[1024,1024]{1,0:T(8,128)(2,1)} %copy-done.36, ...), custom_call_target="tpu_custom_call" | custom-call | flops 46000001024 | bytes 8388608 | tf_op jit(solution)/shard_map/pallas_call | solution.py:462
  400.2 13.2 %collective-permute-start.48 = (bf16[2,128,1024]{2,1,0:T(8,128)(2,1)S(1)}, bf16[2,128,1024]{2,1,0:T(8,128)(2,1)S(1)}, u32[]{:S(2)}, u32[]{:S(2)}) collective-permute-start(bf16[2,128,1024]{2,1,0:T(8,128)(2,1)S(1)} %slice_bitcast_fusion.9), channel_id=1, source_target_pairs={{0,16},{16,0},{1,17},{17,1},{2,18},{18,2},{3,19},{19,3},{4,20},{20... | collective-permute-start | bytes 1572872 | tf_op jit(solution)/shard_map/ppermute | solution.py:92
  444.8 4.6 all-to-all-start.4
  451.9 16.9 %shard_map.305 = bf16[1536,1024]{1,0:T(8,128)(2,1)S(1)} custom-call(s32[16]{0:T(128)S(1)} %copy-done.22, s32[4]{0:T(128)S(1)} %get-tuple-element.336.base_ref, s32[2,1024]{1,0:T(2,128)S(1)} %copy-done.20, bf16[1536,1024]{1,0:T(8,128)(2,1)} %convolution_convert_fusion.1.refs_0_, bf16[512,1024]{1,0:T(8,128)(2,1)S(1)} %copy-done.25, ...), custom_call_target="tpu_custom_call" | custom-call | flops 46000001024 | bytes 8388608 | tf_op jit(solution)/shard_map/pallas_call | solution.py:462
  491.1 4.6 fusion.12
  497.7 4.9 collective-permute-start.75
  505.9 5.1 fusion.10.own_ref
  511.0 7.7 %collective-permute-done.76 = bf16[128,1024]{1,0:T(8,128)(2,1)S(1)} collective-permute-done((bf16[128,1024]{1,0:T(8,128)(2,1)S(1)}, bf16[128,1024]{1,0:T(8,128)(2,1)S(1)}, u32[]{:S(2)}, u32[]{:S(2)}) %collective-permute-start.76) | collective-permute-done | bytes 262176 | tf_op jit(solution)/shard_map/ppermute | solution.py:92
  531.3 4.3 shard_map.306
  536.6 5.4 all-to-all-start.5
  553.0 20.2 %collective-permute-done.67 = bf16[2,128,1024]{2,1,0:T(8,128)(2,1)S(1)} collective-permute-done((bf16[2,128,1024]{2,1,0:T(8,128)(2,1)S(1)}, bf16[2,128,1024]{2,1,0:T(8,128)(2,1)S(1)}, u32[]{:S(2)}, u32[]{:S(2)}) %collective-permute-start.67) | collective-permute-done | bytes 524320 | tf_op jit(solution)/shard_map/ppermute | solution.py:92
  581.0 5.4 collective-permute-done.61
  591.9 4.4 collective-permute-done.62
  605.7 6.5 %collective-permute-done.70 = bf16[128,1024]{1,0:T(8,128)(2,1)S(1)} collective-permute-done((bf16[128,1024]{1,0:T(8,128)(2,1)S(1)}, bf16[128,1024]{1,0:T(8,128)(2,1)S(1)}, u32[]{:S(2)}, u32[]{:S(2)}) %collective-permute-start.70) | collective-permute-done | bytes 262176 | tf_op jit(solution)/shard_map/ppermute | solution.py:92
  614.1 10.9 %collective-permute-done.71 = bf16[2,128,1024]{2,1,0:T(8,128)(2,1)S(1)} collective-permute-done((bf16[2,128,1024]{2,1,0:T(8,128)(2,1)S(1)}, bf16[2,128,1024]{2,1,0:T(8,128)(2,1)S(1)}, u32[]{:S(2)}, u32[]{:S(2)}) %collective-permute-start.71) | collective-permute-done | bytes 524320 | tf_op jit(solution)/shard_map/ppermute | solution.py:92
  (580 shorter events, 331.3 us)
Async XLA Ops:
  31.5 30.7 %all-to-all-start = ((bf16[8,64,1024]{2,1,0:T(8,128)(2,1)}), bf16[8,64,1024]{2,1,0:T(8,128)(2,1)S(1)}, u32[]{:S(2)}, u32[]{:S(2)}) async-start(bf16[8,64,1024]{2,1,0:T(8,128)(2,1)} %param.18), calls=%async_computation | async-start | bytes 2097152 | tf_op jit(solution)/shard_map/all_to_all | solution.py:116
  74.7 28.5 %collective-permute-start.9 = (bf16[160,1024]{1,0:T(8,128)(2,1)S(1)}, bf16[160,1024]{1,0:T(8,128)(2,1)S(1)}, u32[]{:S(2)}, u32[]{:S(2)}) collective-permute-start(bf16[160,1024]{1,0:T(8,128)(2,1)S(1)} %copy-done.92), channel_id=1, source_target_pairs={{0,2},{1,3},{2,0},{3,1},{4,6},{5,7},{6,4},{7,5},{8,10},{9,11},{10,... | collective-permute-start | bytes 983048 | tf_op jit(solution)/shard_map/ppermute | solution.py:92
  74.9 28.3 %collective-permute-start.8 = (bf16[160,1024]{1,0:T(8,128)(2,1)S(1)}, bf16[160,1024]{1,0:T(8,128)(2,1)S(1)}, u32[]{:S(2)}, u32[]{:S(2)}) collective-permute-start(bf16[160,1024]{1,0:T(8,128)(2,1)S(1)} %copy-done.92), channel_id=1, source_target_pairs={{0,1},{1,2},{2,3},{3,0},{4,5},{5,6},{6,7},{7,4},{8,9},{9,10},{10,1... | collective-permute-start | bytes 983048 | tf_op jit(solution)/shard_map/ppermute | solution.py:92
  108.5 45.7 %collective-permute-start.17 = (bf16[128,1024]{1,0:T(8,128)(2,1)S(1)}, bf16[128,1024]{1,0:T(8,128)(2,1)}, u32[]{:S(2)}, u32[]{:S(2)}) collective-permute-start(bf16[128,1024]{1,0:T(8,128)(2,1)S(1)} %bitcast.292), channel_id=1, source_target_pairs={{0,3},{1,0},{2,1},{3,2},{4,7},{5,4},{6,5},{7,6},{8,11},{9,8},{10,9... | collective-permute-start | bytes 786440 | tf_op jit(solution)/shard_map/ppermute | solution.py:92
  108.6 45.6 %collective-permute-start.16 = (bf16[128,1024]{1,0:T(8,128)(2,1)S(1)}, bf16[128,1024]{1,0:T(8,128)(2,1)}, u32[]{:S(2)}, u32[]{:S(2)}) collective-permute-start(bf16[128,1024]{1,0:T(8,128)(2,1)S(1)} %bitcast.293), channel_id=1, source_target_pairs={{0,2},{1,3},{2,0},{3,1},{4,6},{5,7},{6,4},{7,5},{8,10},{9,11},{10,... | collective-permute-start | bytes 786440 | tf_op jit(solution)/shard_map/ppermute | solution.py:92
  111.5 42.7 %collective-permute-start.15 = (bf16[128,1024]{1,0:T(8,128)(2,1)S(1)}, bf16[128,1024]{1,0:T(8,128)(2,1)}, u32[]{:S(2)}, u32[]{:S(2)}) collective-permute-start(bf16[128,1024]{1,0:T(8,128)(2,1)S(1)} %bitcast.294), channel_id=1, source_target_pairs={{0,1},{1,2},{2,3},{3,0},{4,5},{5,6},{6,7},{7,4},{8,9},{9,10},{10,1... | collective-permute-start | bytes 786440 | tf_op jit(solution)/shard_map/ppermute | solution.py:92
  112.9 44.8 %all-to-all-start.1 = ((bf16[8,64,1024]{2,1,0:T(8,128)(2,1)}), bf16[8,64,1024]{2,1,0:T(8,128)(2,1)}, u32[]{:S(2)}, u32[]{:S(2)}) async-start(bf16[8,64,1024]{2,1,0:T(8,128)(2,1)} %param.19), calls=%async_computation.1 | async-start | bytes 2097152 | tf_op jit(solution)/shard_map/all_to_all | solution.py:116
  123.4 34.3 %collective-permute-start.14 = (bf16[2,2,160,1024]{3,2,1,0:T(8,128)(2,1)}, bf16[2,2,160,1024]{3,2,1,0:T(8,128)(2,1)}, u32[]{:S(2)}, u32[]{:S(2)}) collective-permute-start(bf16[2,2,160,1024]{3,2,1,0:T(8,128)(2,1)} %pad_maximum_fusion.7), channel_id=1, source_target_pairs={{0,16},{16,0},{1,17},{17,1},{2,18},{18,2},{3,19},{19,3},{4,20},{20... | collective-permute-start | bytes 3932168 | tf_op jit(solution)/shard_map/ppermute | solution.py:92
  126.5 31.2 %collective-permute-start.13 = (bf16[2,2,160,1024]{3,2,1,0:T(8,128)(2,1)}, bf16[2,2,160,1024]{3,2,1,0:T(8,128)(2,1)}, u32[]{:S(2)}, u32[]{:S(2)}) collective-permute-start(bf16[2,2,160,1024]{3,2,1,0:T(8,128)(2,1)} %pad_maximum_fusion.6), channel_id=1, source_target_pairs={{0,8},{8,0},{1,9},{9,1},{2,10},{10,2},{3,11},{11,3},{4,12},{12,4},... | collective-permute-start | bytes 3932168 | tf_op jit(solution)/shard_map/ppermute | solution.py:92
  171.3 29.7 %collective-permute-start.19 = (bf16[2,128,1024]{2,1,0:T(8,128)(2,1)S(1)}, bf16[2,128,1024]{2,1,0:T(8,128)(2,1)S(1)}, u32[]{:S(2)}, u32[]{:S(2)}) collective-permute-start(bf16[2,128,1024]{2,1,0:T(8,128)(2,1)S(1)} %get-tuple-element.325), channel_id=1, source_target_pairs={{0,16},{16,0},{1,17},{17,1},{2,18},{18,2},{3,19},{19,3},{4,20},{20... | collective-permute-start | bytes 1572872 | tf_op jit(solution)/shard_map/ppermute | solution.py:92
  172.0 28.9 %collective-permute-start.20 = (bf16[2,128,1024]{2,1,0:T(8,128)(2,1)S(1)}, bf16[2,128,1024]{2,1,0:T(8,128)(2,1)S(1)}, u32[]{:S(2)}, u32[]{:S(2)}) collective-permute-start(bf16[2,128,1024]{2,1,0:T(8,128)(2,1)S(1)} %get-tuple-element.323), channel_id=1, source_target_pairs={{0,8},{8,0},{1,9},{9,1},{2,10},{10,2},{3,11},{11,3},{4,12},{12,4},... | collective-permute-start | bytes 1572872 | tf_op jit(solution)/shard_map/ppermute | solution.py:92
  214.0 31.9 %collective-permute-start.28 = (bf16[2,128,1024]{2,1,0:T(8,128)(2,1)}, bf16[2,128,1024]{2,1,0:T(8,128)(2,1)}, u32[]{:S(2)}, u32[]{:S(2)}) collective-permute-start(bf16[2,128,1024]{2,1,0:T(8,128)(2,1)} %get-tuple-element.321), channel_id=1, source_target_pairs={{0,16},{16,0},{1,17},{17,1},{2,18},{18,2},{3,19},{19,3},{4,20},{20... | collective-permute-start | bytes 1572872 | tf_op jit(solution)/shard_map/ppermute | solution.py:92
  214.9 31.0 %collective-permute-start.29 = (bf16[2,128,1024]{2,1,0:T(8,128)(2,1)}, bf16[2,128,1024]{2,1,0:T(8,128)(2,1)}, u32[]{:S(2)}, u32[]{:S(2)}) collective-permute-start(bf16[2,128,1024]{2,1,0:T(8,128)(2,1)} %get-tuple-element.319), channel_id=1, source_target_pairs={{0,8},{8,0},{1,9},{9,1},{2,10},{10,2},{3,11},{11,3},{4,12},{12,4},... | collective-permute-start | bytes 1572872 | tf_op jit(solution)/shard_map/ppermute | solution.py:92
  216.3 33.6 %collective-permute-start.27 = (bf16[2,2,128,1024]{3,2,1,0:T(8,128)(2,1)}, bf16[2,2,128,1024]{3,2,1,0:T(8,128)(2,1)}, u32[]{:S(2)}, u32[]{:S(2)}) collective-permute-start(bf16[2,2,128,1024]{3,2,1,0:T(8,128)(2,1)} %pad_maximum_fusion.11), channel_id=1, source_target_pairs={{0,16},{16,0},{1,17},{17,1},{2,18},{18,2},{3,19},{19,3},{4,20},{20... | collective-permute-start | bytes 3145736 | tf_op jit(solution)/shard_map/ppermute | solution.py:92
  216.8 44.8 %all-to-all-start.2 = ((bf16[8,64,1024]{2,1,0:T(8,128)(2,1)}), bf16[8,64,1024]{2,1,0:T(8,128)(2,1)S(1)}, u32[]{:S(2)}, u32[]{:S(2)}) async-start(bf16[8,64,1024]{2,1,0:T(8,128)(2,1)} %param.20), calls=%async_computation.2 | async-start | bytes 2097152 | tf_op jit(solution)/shard_map/all_to_all | solution.py:116
  223.2 38.4 %collective-permute-start.26 = (bf16[2,2,128,1024]{3,2,1,0:T(8,128)(2,1)S(1)}, bf16[2,2,128,1024]{3,2,1,0:T(8,128)(2,1)}, u32[]{:S(2)}, u32[]{:S(2)}) collective-permute-start(bf16[2,2,128,1024]{3,2,1,0:T(8,128)(2,1)S(1)} %copy-done.62), channel_id=1, source_target_pairs={{0,8},{8,0},{1,9},{9,1},{2,10},{10,2},{3,11},{11,3},{4,12},{12,4},... | collective-permute-start | bytes 3145736 | tf_op jit(solution)/shard_map/ppermute | solution.py:92
  317.7 61.0 %all-to-all-start.3 = ((bf16[8,64,1024]{2,1,0:T(8,128)(2,1)}), bf16[8,64,1024]{2,1,0:T(8,128)(2,1)}, u32[]{:S(2)}, u32[]{:S(2)}) async-start(bf16[8,64,1024]{2,1,0:T(8,128)(2,1)} %bitcast.284), calls=%async_computation.3 | async-start | bytes 2097152 | tf_op jit(solution)/shard_map/all_to_all | solution.py:122
  322.0 149.6 %all-gather.4.cloned.1.call-start = ((), (), s32[]{:S(2)}) async-start(), calls=%async_computation.6 | async-start | bytes 2359296 | tf_op jit(solution)/shard_map/all_gather | solution.py:225
  419.5 52.1 %collective-permute-start.52 = (bf16[2,2,128,1024]{3,2,1,0:T(8,128)(2,1)}, bf16[2,2,128,1024]{3,2,1,0:T(8,128)(2,1)}, u32[]{:S(2)}, u32[]{:S(2)}) collective-permute-start(bf16[2,2,128,1024]{3,2,1,0:T(8,128)(2,1)} %pad_maximum_fusion.17), channel_id=1, source_target_pairs={{0,8},{8,0},{1,9},{9,1},{2,10},{10,2},{3,11},{11,3},{4,12},{12,4},... | collective-permute-start | bytes 3145736 | tf_op jit(solution)/shard_map/ppermute | solution.py:92
  423.0 48.6 %collective-permute-start.53 = (bf16[2,2,128,1024]{3,2,1,0:T(8,128)(2,1)}, bf16[2,2,128,1024]{3,2,1,0:T(8,128)(2,1)}, u32[]{:S(2)}, u32[]{:S(2)}) collective-permute-start(bf16[2,2,128,1024]{3,2,1,0:T(8,128)(2,1)} %pad_maximum_fusion.18), channel_id=1, source_target_pairs={{0,16},{16,0},{1,17},{17,1},{2,18},{18,2},{3,19},{19,3},{4,20},{20... | collective-permute-start | bytes 3145736 | tf_op jit(solution)/shard_map/ppermute | solution.py:92
  431.9 39.6 %collective-permute-start.54 = (bf16[128,1024]{1,0:T(8,128)(2,1)}, bf16[128,1024]{1,0:T(8,128)(2,1)}, u32[]{:S(2)}, u32[]{:S(2)}) collective-permute-start(bf16[128,1024]{1,0:T(8,128)(2,1)} %slice_bitcast_fusion.26), channel_id=1, source_target_pairs={{0,3},{1,0},{2,1},{3,2},{4,7},{5,4},{6,5},{7,6},{8,11},{9,8},{10,9... | collective-permute-start | bytes 786440 | tf_op jit(solution)/shard_map/ppermute | solution.py:92
  436.7 34.8 %collective-permute-start.56 = (bf16[128,1024]{1,0:T(8,128)(2,1)}, bf16[128,1024]{1,0:T(8,128)(2,1)}, u32[]{:S(2)}, u32[]{:S(2)}) collective-permute-start(bf16[128,1024]{1,0:T(8,128)(2,1)} %get-tuple-element.314), channel_id=1, source_target_pairs={{0,1},{1,2},{2,3},{3,0},{4,5},{5,6},{6,7},{7,4},{8,9},{9,10},{10,1... | collective-permute-start | bytes 786440 | tf_op jit(solution)/shard_map/ppermute | solution.py:92
  439.1 32.5 %collective-permute-start.55 = (bf16[128,1024]{1,0:T(8,128)(2,1)}, bf16[128,1024]{1,0:T(8,128)(2,1)}, u32[]{:S(2)}, u32[]{:S(2)}) collective-permute-start(bf16[128,1024]{1,0:T(8,128)(2,1)} %get-tuple-element.315), channel_id=1, source_target_pairs={{0,2},{1,3},{2,0},{3,1},{4,6},{5,7},{6,4},{7,5},{8,10},{9,11},{10,... | collective-permute-start | bytes 786440 | tf_op jit(solution)/shard_map/ppermute | solution.py:92
  444.8 84.9 %all-to-all-start.4 = ((bf16[8,64,1024]{2,1,0:T(8,128)(2,1)}), bf16[8,64,1024]{2,1,0:T(8,128)(2,1)}, u32[]{:S(2)}, u32[]{:S(2)}) async-start(bf16[8,64,1024]{2,1,0:T(8,128)(2,1)} %bitcast.283), calls=%async_computation.4 | async-start | bytes 2097152 | tf_op jit(solution)/shard_map/all_to_all | solution.py:122
  449.4 149.7 %all-gather.6.cloned.1.call-start = ((), (), s32[]{:S(2)}) async-start(), calls=%async_computation.7 | async-start | bytes 2359296 | tf_op jit(solution)/shard_map/all_gather | solution.py:225
  473.7 157.8 %all-gather.8.cloned.1.call-start = ((), (), s32[]{:S(2)}) async-start(), calls=%async_computation.8 | async-start | bytes 2359296 | tf_op jit(solution)/shard_map/all_gather | solution.py:225
  488.6 35.1 %collective-permute-start.63 = (bf16[2,2,128,1024]{3,2,1,0:T(8,128)(2,1)}, bf16[2,2,128,1024]{3,2,1,0:T(8,128)(2,1)}, u32[]{:S(2)}, u32[]{:S(2)}) collective-permute-start(bf16[2,2,128,1024]{3,2,1,0:T(8,128)(2,1)} %pad_maximum_fusion.21), channel_id=1, source_target_pairs={{0,8},{8,0},{1,9},{9,1},{2,10},{10,2},{3,11},{11,3},{4,12},{12,4},... | collective-permute-start | bytes 3145736 | tf_op jit(solution)/shard_map/ppermute | solution.py:92
  491.1 53.2 %collective-permute-start.66 = (bf16[2,2,128,1024]{3,2,1,0:T(8,128)(2,1)}, bf16[2,2,128,1024]{3,2,1,0:T(8,128)(2,1)}, u32[]{:S(2)}, u32[]{:S(2)}) collective-permute-start(bf16[2,2,128,1024]{3,2,1,0:T(8,128)(2,1)} %pad_maximum_fusion.22), channel_id=1, source_target_pairs={{0,16},{16,0},{1,17},{17,1},{2,18},{18,2},{3,19},{19,3},{4,20},{20... | collective-permute-start | bytes 3145736 | tf_op jit(solution)/shard_map/ppermute | solution.py:92
  495.8 33.9 %collective-permute-start.57 = (bf16[512,1024]{1,0:T(8,128)(2,1)}, bf16[512,1024]{1,0:T(8,128)(2,1)}, u32[]{:S(2)}, u32[]{:S(2)}) collective-permute-start(bf16[512,1024]{1,0:T(8,128)(2,1)} %fusion.12), channel_id=1, source_target_pairs={{0,4},{4,0},{1,5},{5,1},{2,6},{6,2},{3,7},{7,3},{8,12},{12,8},{9,1... | collective-permute-start | bytes 3145736 | tf_op jit(solution)/shard_map/ppermute | solution.py:92
  536.6 59.7 %all-to-all-start.5 = ((bf16[8,64,1024]{2,1,0:T(8,128)(2,1)}), bf16[8,64,1024]{2,1,0:T(8,128)(2,1)}, u32[]{:S(2)}, u32[]{:S(2)}) async-start(bf16[8,64,1024]{2,1,0:T(8,128)(2,1)} %bitcast.261), calls=%async_computation.5 | async-start | bytes 2097152 | tf_op jit(solution)/shard_map/all_to_all | solution.py:122
  549.5 54.2 %collective-permute-start.65 = (bf16[128,1024]{1,0:T(8,128)(2,1)S(1)}, bf16[128,1024]{1,0:T(8,128)(2,1)S(1)}, u32[]{:S(2)}, u32[]{:S(2)}) collective-permute-start(bf16[128,1024]{1,0:T(8,128)(2,1)S(1)} %slice_bitcast_fusion.22), channel_id=1, source_target_pairs={{0,3},{1,0},{2,1},{3,2},{4,7},{5,4},{6,5},{7,6},{8,11},{9,8},{10,9... | collective-permute-start | bytes 786440 | tf_op jit(solution)/shard_map/ppermute | solution.py:92
  574.1 29.5 %collective-permute-start.69 = (bf16[128,1024]{1,0:T(8,128)(2,1)}, bf16[128,1024]{1,0:T(8,128)(2,1)S(1)}, u32[]{:S(2)}, u32[]{:S(2)}) collective-permute-start(bf16[128,1024]{1,0:T(8,128)(2,1)} %get-tuple-element.312), channel_id=1, source_target_pairs={{0,1},{1,2},{2,3},{3,0},{4,5},{5,6},{6,7},{7,4},{8,9},{9,10},{10,1... | collective-permute-start | bytes 786440 | tf_op jit(solution)/shard_map/ppermute | solution.py:92
  (181 other events, 1834.0 us)
Sparse Core Ops, SparseCore 0:
  398.6 48.7 all-gather.3
  473.8 42.1 all-gather.5
  519.7 48.5 all-gather.7

commit v5 on v4

--- a/solution.py
+++ b/solution.py
@@ -212,12 +212,12 @@
         return self.add(self.mine, self.got)
 
 
-def in_place(piece, axis):
+def in_place(piece, axis, beside):
     if lax.axis_size(axis) != 2:
-        return lax.all_gather(piece, axis, axis=0, tiled=False)
-    other = shift(piece, axis, 1)
+        return lax.all_gather(piece, axis, axis=0, tiled=False), beside
+    other, beside = lax.optimization_barrier((shift(piece, axis, 1), beside))
     low = lax.axis_index(axis) == 0
-    return jnp.stack([jnp.where(low, piece, other), jnp.where(low, other, piece)], 0)
+    return jnp.stack([jnp.where(low, piece, other), jnp.where(low, other, piece)], 0), beside
 
 
 def gathered(piece):
@@ -225,8 +225,12 @@
     return lax.all_gather(piece, ("core", "batch", "yy"), axis=0, tiled=True).reshape(sizes + piece.shape)
 
 
-def replicate(piece):
-    return in_place(in_place(in_place(piece, "yy"), "batch"), "core")
+def replicate(piece, *beside):
+    done = []
+    for axis, values in zip(("yy", "batch", "core"), beside):
+        piece, values = in_place(piece, axis, values)
+        done.append(values)
+    return piece, *done
 
 
 def unfold_kernel(kinds, source_ref, *outs):
@@ -265,13 +269,12 @@
     )(whole)
 
 
-def total_of(value):
-    for axis in ("core", "yy", "batch", "head"):
-        count = lax.axis_size(axis)
-        step = 1
-        while step < count:
-            value = value + lax.ppermute(value, axis, [(i, i ^ step) for i in range(count)])
-            step *= 2
+def total_of(value, axis):
+    count = lax.axis_size(axis)
+    step = 1
+    while step < count:
+        value = value + lax.ppermute(value, axis, [(i, i ^ step) for i in range(count)])
+        step *= 2
     return value
 
 
@@ -469,7 +472,7 @@
                 out_specs=[by_half(o.shape) for o in outs],
                 scratch_shapes=scratch,
             ),
-            compiler_params=pltpu.CompilerParams(vmem_limit_bytes=48 * 2**20),
+            compiler_params=pltpu.CompilerParams(vmem_limit_bytes=30 * 2**20),
             cost_estimate=pl.CostEstimate(flops=flops, bytes_accessed=8 * 2**20, transcendentals=4 * 2**20),
         )(need, bases, spans, *arrays)
 
@@ -625,15 +628,17 @@
     self_mixed = tied(self_mixed, up_weights.mine, down_weights.mine)
     w_o, w_mem, w_cq, w_co = cross_weights.result()
     normed_two, after_self = normalize([residual, *own_parts(self_mixed, w_o)], gain_two)
-    normed_two = meet(normed_two, up_weights, down_weights)
+    normed_two = meet(normed_two, up_weights)
     up_weights.three()
-    down_weights.two()
-    normed_two, source_own = tied((normed_two, source_own), up_weights.mine, down_weights.mine)
-    cot_own = to_row(tied(cotangent, up_weights.mine, source_own))
+    normed_two, source_own = tied((normed_two, source_own), up_weights.mine)
     source = both(source_own)
     mkv = dot(w_mem, source, 1, 1).astype(BF)
     normed_two = both(normed_two)
     cq = dot(w_cq, normed_two, 1, 1).astype(BF)
+    cq, mkv = meet((cq, mkv), down_weights)
+    down_weights.two()
+    cq = tied(cq, down_weights.mine)
+    cot_own = to_row(tied(cotangent, down_weights.mine))
     cross_mixed, cross_lse = heads.attend(cross_tables, (cq, mkv), (1, 2))
     cross_mixed, cot_own = meet((cross_mixed, cot_own), up_weights, down_weights)
     down_weights.three()
@@ -675,7 +680,7 @@
     )
     gcq, gmkv, output = meet((gcq, gmkv, output), up_sum, down_sum)
     up_sum.two()
-    down_all = gathered(down_sum.result())
+    down_total = down_sum.result()
     gcq, gmkv = tied((gcq, gmkv), up_sum.mine)
     grad_after_self, self_grad, grad_gain_two = normalize_back(
         after_self, gain_two, own_parts(gcq, w_cq), grad_after_cross
@@ -690,39 +695,52 @@
     cross_sum = Sum([g_co, g_cq, g_mem])
     memory_back = own_sum(gmkv, w_mem).astype(BF)
     grad_self_mixed = dot(w_o, self_grad, 1, 1).astype(BF)
-    grad_self_mixed, memory_back = tied((grad_self_mixed, memory_back), up_sum.mine, cross_sum.mine, g_o)
+    grad_self_mixed, memory_back, g_o, down_total = meet(
+        (grad_self_mixed, memory_back, g_o, down_total), cross_sum
+    )
+    down_all = gathered(down_total)
+    cross_sum.two()
+    grad_self_mixed = tied(grad_self_mixed, up_sum.mine, cross_sum.mine)
     grad_memory = from_row(memory_back, rows)
     (gqkv,) = heads.attend_back(self_tables, (qkv,), (3,), self_mixed, grad_self_mixed, self_lse)
-    gqkv, down_all = meet((gqkv, down_all), cross_sum, up_sum)
-    cross_sum.two()
-    up_all = gathered(up_sum.result())
+    gqkv = meet(gqkv, cross_sum, up_sum)
     g_self = weight_grad(gqkv, normed_one)
+    gqkv, g_self, cross_sum.got = lax.optimization_barrier((gqkv, g_self, cross_sum.got))
     self_sum = Sum([g_o, g_self])
-    first_back = own_parts(tied(gqkv, self_sum.mine), w_self)
-    first_back, grad_memory = lax.optimization_barrier((first_back, grad_memory))
+    cross_sum.three()
+    first_back, grad_memory, up_total = meet((own_parts(gqkv, w_self), grad_memory, up_sum.result()), self_sum)
+    self_sum.two()
+    up_all = gathered(up_total)
     _, grad_inputs, grad_gain_one = normalize_back(residual, gain_one, first_back, grad_after_self)
+    grad_inputs, cross_sum.got = lax.optimization_barrier((grad_inputs, cross_sum.got))
     grad_inputs = from_row(grad_inputs, rows).astype(F32)
-    gains = total_of(jnp.stack([grad_gain_one, grad_gain_two, grad_gain_three]))
-    self_sum.two()
-    cross_sum.got = tied(cross_sum.got, self_sum.mine)
-    cross_sum.three()
+    gains = jnp.stack([grad_gain_one, grad_gain_two, grad_gain_three])
+    for axis in ("core", "yy", "batch"):
+        gains = total_of(gains, axis)
+    cross_total = meet(cross_sum.result(), self_sum)
     self_sum.three()
 
     deep = w_query.shape[1] // 2 // nxy
     far = w_up.shape[1] // 2 // nxy
     (grad_down,) = unfold(down_all, [(far, False)])
     (grad_up,) = unfold(up_all, [(far, True)])
-    grad_co, grad_cq, grad_mk, grad_mv = unfold(
-        gathered(cross_sum.result()), [(deep, False), (deep, True), (deep, True), (deep, True)]
-    )
-    self_sum.got = tied(self_sum.got, grad_down, grad_up, grad_inputs, gains, grad_memory)
+    cross_grads = unfold(gathered(cross_total), [(deep, False), (deep, True), (deep, True), (deep, True)])
+    grad_memory = grad_memory.astype(F32)
+    self_sum.got, grad_down, grad_memory, gains = lax.optimization_barrier(
+        (self_sum.got, grad_down, grad_memory, gains)
+    )
+    gains = total_of(gains, "head")
+    self_all, grad_up, (grad_inputs, gains), cross_grads = replicate(
+        self_sum.result(), grad_up, (grad_inputs, gains), cross_grads
+    )
+    grad_co, grad_cq, grad_mk, grad_mv = cross_grads
     grad_o, grad_q, grad_k, grad_v = unfold(
-        replicate(self_sum.result()), [(deep, False), (deep, True), (deep, True), (deep, True)]
+        self_all, [(deep, False), (deep, True), (deep, True), (deep, True)]
     )
     return (
         output,
         grad_inputs,
-        grad_memory.astype(F32),
+        grad_memory,
         gains[0],
         grad_q,
         grad_k,

time: 659 us -> 647 us (0.982)
  Pallas kernels: 97 us -> 80.9 us
  waiting for transfers between devices: 155 us -> 163 us
    all_to_all x3, waiting for transfers between devices: 3.44 us -> 21.7 us  [to_row(): moved = lax.all_to_all(tokens, ('yy', 'head'), 0, 0, tiled=True)]
    pallas_call x4, Pallas kernels: 72 us -> 57.3 us  [call(): pl.pallas_call(functools.partial(kernel, self.index, layouts, self.chunk)...]
    ppermute x5, waiting for transfers between devices: 11 us -> 3.87 us  [total_of(): lax.ppermute(value, axis, [(i, i ^ step) for i in range(count)])]
    convert_element_type x20, other arithmetic: 24.7 us -> 31.5 us  [add(): return total.astype(BF)]
    unnamed x270 -> x284, local copies, waits for them, and re-layouts: 29.2 us -> 25.6 us
  transfers between devices with their start and end apart: 87 -> 87, of which waited for: 27 -> 28; matrix products, arithmetic and copies ran while one was open for 26% -> 28% of each run, Pallas kernels for 14% -> 12%
where the time goes in v5:
time: 647 us; the launch traced here: 638 us
  waiting for transfers between devices  163 us (25%)
  starting transfers between devices  136 us (21%)
  matrix products  103 us (16%)
  Pallas kernels  80.9 us (13%)
  other arithmetic  77 us (12%)
  local copies, waits for them, and re-layouts  61.7 us (10%)
  between operations  16.3 us (3%)
    ppermute x73, waiting for transfers between devices, shift(): lax.ppermute(piece, axis, [(i, (i + step) % count) for i in range(count)])  137 us
    dot_general x28, matrix products, dot(): lax.dot_general(left, right, (((left_dim,), (right_dim,)), ((), ())), pre...  103 us
    ppermute x73, starting transfers between devices, shift(): lax.ppermute(piece, axis, [(i, (i + step) % count) for i in range(count)])  102 us
    pallas_call x4, Pallas kernels, call(): pl.pallas_call(functools.partial(kernel, self.index, layouts, self.chunk)...  57.3 us
    convert_element_type x20, other arithmetic, add(): return total.astype(BF)  31.5 us
    another operation x20, other arithmetic, three(): self.send(jnp.stack(first, 0), jnp.stack(second, 0), 'yy', 'batch')  30.6 us
    unnamed x284, local copies, waits for them, and re-layouts  25.6 us
    all_to_all x3, waiting for transfers between devices, to_row(): moved = lax.all_to_all(tokens, ('yy', 'head'), 0, 0, tiled=True)  21.7 us
  transfers between devices with their start and end apart: 87, of which 28 were waited for; matrix products, arithmetic and copies ran while one was open for 28% of the time, Pallas kernels for 12%

profile of v5, /device:TPU:1, one launch (start us, length us, event | category | flops | bytes accessed | tf_op | source)
XLA Modules:
  0.0 637.6 jit_solution(12778913522559692282)
XLA Ops:
  17.7 13.0 %collective-permute-done.1 = bf16[96,1024]{1,0:T(8,128)(2,1)S(1)} collective-permute-done((bf16[96,1024]{1,0:T(8,128)(2,1)S(1)}, bf16[96,1024]{1,0:T(8,128)(2,1)S(1)}, u32[]{:S(2)}, u32[]{:S(2)}) %collective-permute-start.1) | collective-permute-done | bytes 196640 | tf_op jit(solution)/shard_map/ppermute | solution.py:92
  31.5 4.7 all-to-all-start
  54.4 7.8 %collective-permute-done.4 = bf16[2,96,1024]{2,1,0:T(8,128)(2,1)} collective-permute-done((bf16[2,96,1024]{2,1,0:T(8,128)(2,1)}, bf16[2,96,1024]{2,1,0:T(8,128)(2,1)}, u32[]{:S(2)}, u32[]{:S(2)}) %collective-permute-start.4) | collective-permute-done | bytes 393248 | tf_op jit(solution)/shard_map/ppermute | solution.py:92
  77.9 13.8 %collective-permute-done.7 = bf16[2,2,96,1024]{3,2,1,0:T(8,128)(2,1)} collective-permute-done((bf16[2,2,96,1024]{3,2,1,0:T(8,128)(2,1)}, bf16[2,2,96,1024]{3,2,1,0:T(8,128)(2,1)}, u32[]{:S(2)}, u32[]{:S(2)}) %collective-permute-start.7) | collective-permute-done | bytes 786464 | tf_op jit(solution)/shard_map/ppermute | solution.py:92
  91.7 7.0 %convolution_convert_fusion.1.refs_0_ = bf16[1536,1024]{1,0:T(8,128)(2,1)} fusion(bf16[1024,1024]{1,0:T(8,128)(2,1)S(1)} %pad_maximum_fusion.3, bf16[384,1024]{1,0:T(8,128)(2,1)} %bitcast.24, bf16[384,1024]{1,0:T(8,128)(2,1)} %bitcast.23, bf16[384,1024]{1,0:T(8,128)(2,1)} %bitcast.22, bf16[384,1024]{1,0:T(8,128)(2,1)} %bitcast.18), kind=kOutput, calls=%fused_computation.8 | convolution fusion | flops 3235381248 | bytes 8388608 | tf_op jit(solution)/shard_map/dot_general | solution.py:25
  127.2 11.7 %shard_map.298 = (bf16[512,1024]{1,0:T(8,128)(2,1)S(1)}, f32[2,4,1,1024]{3,2,1,0:T(1,128)S(1)}) custom-call(s32[16]{0:T(128)S(1)} %select_n.214.need_ref, s32[4]{0:T(128)S(1)} %get-tuple-element.398.base_ref, s32[2,1024]{1,0:T(2,128)S(1)} %pad_add_fusion.1.span_ref, bf16[1536,1024]{1,0:T(8,128)(2,1)S(1)} %copy-done.44), custom_call_target="tpu_custom_call" | custom-call | flops 40000000000 | bytes 8388608 | tf_op jit(solution)/shard_map/pallas_call | solution.py:465
  143.3 14.4 %all-to-all-done.1 = bf16[8,64,1024]{2,1,0:T(8,128)(2,1)} async-done(((bf16[8,64,1024]{2,1,0:T(8,128)(2,1)}), bf16[8,64,1024]{2,1,0:T(8,128)(2,1)}, u32[]{:S(2)}, u32[]{:S(2)}) %all-to-all-start.1) | async-done | bytes 1048608 | tf_op jit(solution)/shard_map/all_to_all | solution.py:116
  164.7 6.6 %collective-permute-start.18 = (bf16[512,1024]{1,0:T(8,128)(2,1)S(1)}, bf16[512,1024]{1,0:T(8,128)(2,1)S(1)}, u32[]{:S(2)}, u32[]{:S(2)}) collective-permute-start(bf16[512,1024]{1,0:T(8,128)(2,1)S(1)} %convolution_convert_fusion.15), channel_id=1, source_target_pairs={{0,4},{4,0},{1,5},{5,1},{2,6},{6,2},{3,7},{7,3},{8,12},{12,8},{9,1... | collective-permute-start | bytes 3145736 | tf_op jit(solution)/shard_map/ppermute | solution.py:92
  174.9 9.9 %collective-permute-done.19 = bf16[2,128,1024]{2,1,0:T(8,128)(2,1)S(1)} collective-permute-done((bf16[2,128,1024]{2,1,0:T(8,128)(2,1)S(1)}, bf16[2,128,1024]{2,1,0:T(8,128)(2,1)S(1)}, u32[]{:S(2)}, u32[]{:S(2)}) %collective-permute-start.19) | collective-permute-done | bytes 524320 | tf_op jit(solution)/shard_map/ppermute | solution.py:92
  192.2 5.1 collective-permute-start.24
  211.3 9.0 %collective-permute-done.24 = bf16[128,1024]{1,0:T(8,128)(2,1)S(1)} collective-permute-done((bf16[128,1024]{1,0:T(8,128)(2,1)S(1)}, bf16[128,1024]{1,0:T(8,128)(2,1)S(1)}, u32[]{:S(2)}, u32[]{:S(2)}) %collective-permute-start.24) | collective-permute-done | bytes 262176 | tf_op jit(solution)/shard_map/ppermute | solution.py:92
  228.9 13.0 %shard_map.300 = (bf16[512,1024]{1,0:T(8,128)(2,1)S(1)}, f32[2,4,1,1024]{3,2,1,0:T(1,128)S(1)}) custom-call(s32[16]{0:T(128)S(1)} %select_n.206.need_ref, s32[4]{0:T(128)S(1)} %get-tuple-element.398.base_ref, s32[2,1024]{1,0:T(2,128)S(1)} %pad_add_fusion.span_ref, bf16[512,1024]{1,0:T(8,128)(2,1)S(1)} %convolution_convert_fusion.12.refs_0_, ...), custom_call_target="tpu_custom_call" | custom-call | flops 40000000000 | bytes 8388608 | tf_op jit(solution)/shard_map/pallas_call | solution.py:465
  242.8 4.7 collective-permute-done.29
  247.5 7.3 %all-to-all-done.2 = bf16[8,64,1024]{2,1,0:T(8,128)(2,1)S(1)} async-done(((bf16[8,64,1024]{2,1,0:T(8,128)(2,1)}), bf16[8,64,1024]{2,1,0:T(8,128)(2,1)S(1)}, u32[]{:S(2)}, u32[]{:S(2)}) %all-to-all-start.2) | async-done | bytes 1048608 | tf_op jit(solution)/shard_map/all_to_all | solution.py:116
  266.7 14.1 %add_convert_fusion = (bf16[2048,1024]{1,0:T(8,128)(2,1)}, bf16[2048,1024]{1,0:T(8,128)(2,1)}) fusion(bf16[1024,1024]{1,0:T(8,128)(2,1)S(1)} %constant_dynamic-update-slice_fusion.4, bf16[512,1024]{1,0:T(8,128)(2,1)} %bitcast.73, bf16[512,1024]{1,0:T(8,128)(2,1)} %bitcast.72, bf16[512,1024]{1,0:T(8,128)(2,1)} %bitcast.71, bf16[512,1024]{1,0:T(8,128)(2,1)} %bitcast.70), kind=kOutput, calls=%fused_computation.1 | convolution fusion | flops 4349493248 | bytes 14680064 | tf_op jit(solution)/shard_map/dot_general | solution.py:25
  280.7 6.9 %convolution_convert_fusion.3 = bf16[2048,1024]{1,0:T(8,128)(2,1)S(1)} fusion(bf16[2048,1024]{1,0:T(8,128)(2,1)} %get-tuple-element.231, bf16[1024,1024]{1,0:T(8,128)(2,1)S(1)} %constant_dynamic-update-slice_fusion.6), kind=kOutput, calls=%fused_computation.10 | convolution fusion | flops 4297064448 | bytes 10485760 | tf_op jit(solution)/shard_map/dot_general | solution.py:25
  295.4 11.8 %multiply_convert_fusion = bf16[2048,1024]{1,0:T(8,128)(2,1)} fusion(bf16[2048,1024]{1,0:T(8,128)(2,1)} %get-tuple-element.214, bf16[1024,1024]{1,0:T(8,128)(2,1)S(1)} %constant_dynamic-update-slice_fusion.6, bf16[512,1024]{1,0:T(8,128)(2,1)S(1)} %bitcast.381, bf16[512,1024]{1,0:T(8,128)(2,1)S(1)} %bitcast.286, bf16[512,1024]{1,0:T(8,128)(2,1)S(1)} %bitcast.384, ...), kind=kOutput, calls=%fused_computation | convolution fusion | flops 4318035968 | bytes 14680064 | tf_op jit(solution)/shard_map/dot_general | solution.py:25
  324.5 4.6 fusion.15
  337.7 4.7 convolution_convert_fusion.2
  349.1 4.9 collective-permute-start.44
  354.3 17.2 %shard_map.303 = (bf16[512,1024]{1,0:T(8,128)(2,1)S(1)}, bf16[1024,1024]{1,0:T(8,128)(2,1)S(1)}) custom-call(s32[16]{0:T(128)S(1)} %select_n.206.need_ref, s32[4]{0:T(128)S(1)} %get-tuple-element.398.base_ref, s32[2,1024]{1,0:T(2,128)S(1)} %pad_add_fusion.span_ref, bf16[512,1024]{1,0:T(8,128)(2,1)S(1)} %copy-done.36, bf16[1024,1024]{1,0:T(8,128)(2,1)S(1)} %copy-done.43, ...), custom_call_target="tpu_custom_call" | custom-call | flops 46000001024 | bytes 8388608 | tf_op jit(solution)/shard_map/pallas_call | solution.py:465
  409.3 14.5 %collective-permute-start.56 = (bf16[128,1024]{1,0:T(8,128)(2,1)}, bf16[128,1024]{1,0:T(8,128)(2,1)}, u32[]{:S(2)}, u32[]{:S(2)}) collective-permute-start(bf16[128,1024]{1,0:T(8,128)(2,1)} %slice_bitcast_fusion.26), channel_id=1, source_target_pairs={{0,3},{1,0},{2,1},{3,2},{4,7},{5,4},{6,5},{7,6},{8,11},{9,8},{10,9... | collective-permute-start | bytes 786440 | tf_op jit(solution)/shard_map/ppermute | solution.py:92
  439.0 5.8 all-to-all-start.4
  451.9 15.4 %shard_map.305 = bf16[1536,1024]{1,0:T(8,128)(2,1)S(1)} custom-call(s32[16]{0:T(128)S(1)} %copy-done.26, s32[4]{0:T(128)S(1)} %get-tuple-element.398.base_ref, s32[2,1024]{1,0:T(2,128)S(1)} %copy-done.24, bf16[1536,1024]{1,0:T(8,128)(2,1)S(1)} %copy-done.45, bf16[512,1024]{1,0:T(8,128)(2,1)S(1)} %copy-done.29, bf16[512,1024]{1,0:T(8,128)(2,1)S(1)} %copy-done.37, ...), custom_call_target="tpu_custom_call" | custom-call | flops 46000001024 | bytes 8388608 | tf_op jit(solution)/shard_map/pallas_call | solution.py:465
  468.1 6.1 collective-permute-done.55
  477.9 4.7 fusion.12
  491.4 5.4 fusion.10.own_ref
  496.9 15.4 %collective-permute-done.60 = bf16[2,2,128,1024]{3,2,1,0:T(8,128)(2,1)} collective-permute-done((bf16[2,2,128,1024]{3,2,1,0:T(8,128)(2,1)}, bf16[2,2,128,1024]{3,2,1,0:T(8,128)(2,1)}, u32[]{:S(2)}, u32[]{:S(2)}) %collective-permute-start.60) | collective-permute-done | bytes 1048608 | tf_op jit(solution)/shard_map/ppermute | solution.py:92
  534.3 8.0 %collective-permute-done.63 = bf16[128,1024]{1,0:T(8,128)(2,1)} collective-permute-done((bf16[128,1024]{1,0:T(8,128)(2,1)S(1)}, bf16[128,1024]{1,0:T(8,128)(2,1)}, u32[]{:S(2)}, u32[]{:S(2)}) %collective-permute-start.63) | collective-permute-done | bytes 262176 | tf_op jit(solution)/shard_map/ppermute | solution.py:92
  542.3 5.1 all-to-all-start.5
  571.0 5.2 collective-permute-done.67
  579.2 15.9 %collective-permute-done.68 = bf16[128,1024]{1,0:T(8,128)(2,1)} collective-permute-done((bf16[128,1024]{1,0:T(8,128)(2,1)}, bf16[128,1024]{1,0:T(8,128)(2,1)}, u32[]{:S(2)}, u32[]{:S(2)}) %collective-permute-start.68) | collective-permute-done | bytes 262176 | tf_op jit(solution)/shard_map/ppermute | solution.py:92
  (594 shorter events, 327.6 us)
Async XLA Ops:
  31.5 30.7 %all-to-all-start = ((bf16[8,64,1024]{2,1,0:T(8,128)(2,1)}), bf16[8,64,1024]{2,1,0:T(8,128)(2,1)S(1)}, u32[]{:S(2)}, u32[]{:S(2)}) async-start(bf16[8,64,1024]{2,1,0:T(8,128)(2,1)} %param.18), calls=%async_computation | async-start | bytes 2097152 | tf_op jit(solution)/shard_map/all_to_all | solution.py:116
  74.7 28.5 %collective-permute-start.9 = (bf16[160,1024]{1,0:T(8,128)(2,1)S(1)}, bf16[160,1024]{1,0:T(8,128)(2,1)S(1)}, u32[]{:S(2)}, u32[]{:S(2)}) collective-permute-start(bf16[160,1024]{1,0:T(8,128)(2,1)S(1)} %copy-done.104), channel_id=1, source_target_pairs={{0,2},{1,3},{2,0},{3,1},{4,6},{5,7},{6,4},{7,5},{8,10},{9,11},{10,... | collective-permute-start | bytes 983048 | tf_op jit(solution)/shard_map/ppermute | solution.py:92
  75.0 28.3 %collective-permute-start.8 = (bf16[160,1024]{1,0:T(8,128)(2,1)S(1)}, bf16[160,1024]{1,0:T(8,128)(2,1)S(1)}, u32[]{:S(2)}, u32[]{:S(2)}) collective-permute-start(bf16[160,1024]{1,0:T(8,128)(2,1)S(1)} %copy-done.104), channel_id=1, source_target_pairs={{0,1},{1,2},{2,3},{3,0},{4,5},{5,6},{6,7},{7,4},{8,9},{9,10},{10,1... | collective-permute-start | bytes 983048 | tf_op jit(solution)/shard_map/ppermute | solution.py:92
  108.6 34.7 %collective-permute-start.17 = (bf16[128,1024]{1,0:T(8,128)(2,1)S(1)}, bf16[128,1024]{1,0:T(8,128)(2,1)}, u32[]{:S(2)}, u32[]{:S(2)}) collective-permute-start(bf16[128,1024]{1,0:T(8,128)(2,1)S(1)} %bitcast.289), channel_id=1, source_target_pairs={{0,3},{1,0},{2,1},{3,2},{4,7},{5,4},{6,5},{7,6},{8,11},{9,8},{10,9... | collective-permute-start | bytes 786440 | tf_op jit(solution)/shard_map/ppermute | solution.py:92
  108.6 34.6 %collective-permute-start.16 = (bf16[128,1024]{1,0:T(8,128)(2,1)S(1)}, bf16[128,1024]{1,0:T(8,128)(2,1)}, u32[]{:S(2)}, u32[]{:S(2)}) collective-permute-start(bf16[128,1024]{1,0:T(8,128)(2,1)S(1)} %bitcast.290), channel_id=1, source_target_pairs={{0,2},{1,3},{2,0},{3,1},{4,6},{5,7},{6,4},{7,5},{8,10},{9,11},{10,... | collective-permute-start | bytes 786440 | tf_op jit(solution)/shard_map/ppermute | solution.py:92
  111.5 31.8 %collective-permute-start.15 = (bf16[128,1024]{1,0:T(8,128)(2,1)S(1)}, bf16[128,1024]{1,0:T(8,128)(2,1)}, u32[]{:S(2)}, u32[]{:S(2)}) collective-permute-start(bf16[128,1024]{1,0:T(8,128)(2,1)S(1)} %bitcast.291), channel_id=1, source_target_pairs={{0,1},{1,2},{2,3},{3,0},{4,5},{5,6},{6,7},{7,4},{8,9},{9,10},{10,1... | collective-permute-start | bytes 786440 | tf_op jit(solution)/shard_map/ppermute | solution.py:92
  112.9 44.8 %all-to-all-start.1 = ((bf16[8,64,1024]{2,1,0:T(8,128)(2,1)}), bf16[8,64,1024]{2,1,0:T(8,128)(2,1)}, u32[]{:S(2)}, u32[]{:S(2)}) async-start(bf16[8,64,1024]{2,1,0:T(8,128)(2,1)} %param.19), calls=%async_computation.1 | async-start | bytes 2097152 | tf_op jit(solution)/shard_map/all_to_all | solution.py:116
  123.4 34.3 %collective-permute-start.14 = (bf16[2,2,160,1024]{3,2,1,0:T(8,128)(2,1)}, bf16[2,2,160,1024]{3,2,1,0:T(8,128)(2,1)}, u32[]{:S(2)}, u32[]{:S(2)}) collective-permute-start(bf16[2,2,160,1024]{3,2,1,0:T(8,128)(2,1)} %pad_maximum_fusion.7), channel_id=1, source_target_pairs={{0,16},{16,0},{1,17},{17,1},{2,18},{18,2},{3,19},{19,3},{4,20},{20... | collective-permute-start | bytes 3932168 | tf_op jit(solution)/shard_map/ppermute | solution.py:92
  126.5 31.2 %collective-permute-start.13 = (bf16[2,2,160,1024]{3,2,1,0:T(8,128)(2,1)}, bf16[2,2,160,1024]{3,2,1,0:T(8,128)(2,1)}, u32[]{:S(2)}, u32[]{:S(2)}) collective-permute-start(bf16[2,2,160,1024]{3,2,1,0:T(8,128)(2,1)} %pad_maximum_fusion.6), channel_id=1, source_target_pairs={{0,8},{8,0},{1,9},{9,1},{2,10},{10,2},{3,11},{11,3},{4,12},{12,4},... | collective-permute-start | bytes 3932168 | tf_op jit(solution)/shard_map/ppermute | solution.py:92
  192.2 28.1 %collective-permute-start.24 = (bf16[128,1024]{1,0:T(8,128)(2,1)S(1)}, bf16[128,1024]{1,0:T(8,128)(2,1)S(1)}, u32[]{:S(2)}, u32[]{:S(2)}) collective-permute-start(bf16[128,1024]{1,0:T(8,128)(2,1)S(1)} %constant_dynamic-slice_fusion), channel_id=1, source_target_pairs={{0,2},{1,3},{2,0},{3,1},{4,6},{5,7},{6,4},{7,5},{8,10},{9,11},{10,... | collective-permute-start | bytes 786440 | tf_op jit(solution)/shard_map/ppermute | solution.py:92
  202.4 40.4 %collective-permute-start.27 = (bf16[2,2,128,1024]{3,2,1,0:T(8,128)(2,1)}, bf16[2,2,128,1024]{3,2,1,0:T(8,128)(2,1)}, u32[]{:S(2)}, u32[]{:S(2)}) collective-permute-start(bf16[2,2,128,1024]{3,2,1,0:T(8,128)(2,1)} %pad_maximum_fusion.11), channel_id=1, source_target_pairs={{0,16},{16,0},{1,17},{17,1},{2,18},{18,2},{3,19},{19,3},{4,20},{20... | collective-permute-start | bytes 3145736 | tf_op jit(solution)/shard_map/ppermute | solution.py:92
  208.7 34.1 %collective-permute-start.26 = (bf16[2,2,128,1024]{3,2,1,0:T(8,128)(2,1)}, bf16[2,2,128,1024]{3,2,1,0:T(8,128)(2,1)}, u32[]{:S(2)}, u32[]{:S(2)}) collective-permute-start(bf16[2,2,128,1024]{3,2,1,0:T(8,128)(2,1)} %pad_maximum_fusion.10), channel_id=1, source_target_pairs={{0,8},{8,0},{1,9},{9,1},{2,10},{10,2},{3,11},{11,3},{4,12},{12,4},... | collective-permute-start | bytes 3145736 | tf_op jit(solution)/shard_map/ppermute | solution.py:92
  223.7 31.1 %all-to-all-start.2 = ((bf16[8,64,1024]{2,1,0:T(8,128)(2,1)}), bf16[8,64,1024]{2,1,0:T(8,128)(2,1)S(1)}, u32[]{:S(2)}, u32[]{:S(2)}) async-start(bf16[8,64,1024]{2,1,0:T(8,128)(2,1)} %param.20), calls=%async_computation.2 | async-start | bytes 2097152 | tf_op jit(solution)/shard_map/all_to_all | solution.py:116
  264.3 25.6 %collective-permute-start.34 = (bf16[2,2,128,1024]{3,2,1,0:T(8,128)(2,1)S(1)}, bf16[2,2,128,1024]{3,2,1,0:T(8,128)(2,1)S(1)}, u32[]{:S(2)}, u32[]{:S(2)}) collective-permute-start(bf16[2,2,128,1024]{3,2,1,0:T(8,128)(2,1)S(1)} %pad_maximum_fusion.13), channel_id=1, source_target_pairs={{0,16},{16,0},{1,17},{17,1},{2,18},{18,2},{3,19},{19,3},{4,20},{20... | collective-permute-start | bytes 3145736 | tf_op jit(solution)/shard_map/ppermute | solution.py:92
  264.6 25.3 %collective-permute-start.33 = (bf16[2,2,128,1024]{3,2,1,0:T(8,128)(2,1)S(1)}, bf16[2,2,128,1024]{3,2,1,0:T(8,128)(2,1)S(1)}, u32[]{:S(2)}, u32[]{:S(2)}) collective-permute-start(bf16[2,2,128,1024]{3,2,1,0:T(8,128)(2,1)S(1)} %pad_maximum_fusion.12), channel_id=1, source_target_pairs={{0,8},{8,0},{1,9},{9,1},{2,10},{10,2},{3,11},{11,3},{4,12},{12,4},... | collective-permute-start | bytes 3145736 | tf_op jit(solution)/shard_map/ppermute | solution.py:92
  310.7 63.5 %all-to-all-start.3 = ((bf16[8,64,1024]{2,1,0:T(8,128)(2,1)}), bf16[8,64,1024]{2,1,0:T(8,128)(2,1)}, u32[]{:S(2)}, u32[]{:S(2)}) async-start(bf16[8,64,1024]{2,1,0:T(8,128)(2,1)} %bitcast.281), calls=%async_computation.3 | async-start | bytes 2097152 | tf_op jit(solution)/shard_map/all_to_all | solution.py:122
  314.9 251.8 %all-gather.4.cloned.1.call-start = ((), (), s32[]{:S(2)}) async-start(), calls=%async_computation.6 | async-start | bytes 2359296 | tf_op jit(solution)/shard_map/all_gather | solution.py:225
  344.1 30.0 %collective-permute-start.42 = (bf16[2,2,128,1024]{3,2,1,0:T(8,128)(2,1)S(1)}, bf16[2,2,128,1024]{3,2,1,0:T(8,128)(2,1)}, u32[]{:S(2)}, u32[]{:S(2)}) collective-permute-start(bf16[2,2,128,1024]{3,2,1,0:T(8,128)(2,1)S(1)} %bitcast.300), channel_id=1, source_target_pairs={{0,8},{8,0},{1,9},{9,1},{2,10},{10,2},{3,11},{11,3},{4,12},{12,4},... | collective-permute-start | bytes 3145736 | tf_op jit(solution)/shard_map/ppermute | solution.py:92
  344.9 29.3 %collective-permute-start.43 = (bf16[2,2,128,1024]{3,2,1,0:T(8,128)(2,1)S(1)}, bf16[2,2,128,1024]{3,2,1,0:T(8,128)(2,1)}, u32[]{:S(2)}, u32[]{:S(2)}) collective-permute-start(bf16[2,2,128,1024]{3,2,1,0:T(8,128)(2,1)S(1)} %bitcast.299), channel_id=1, source_target_pairs={{0,16},{16,0},{1,17},{17,1},{2,18},{18,2},{3,19},{19,3},{4,20},{20... | collective-permute-start | bytes 3145736 | tf_op jit(solution)/shard_map/ppermute | solution.py:92
  392.1 37.2 %collective-permute-start.51 = (bf16[512,1024]{1,0:T(8,128)(2,1)}, bf16[512,1024]{1,0:T(8,128)(2,1)}, u32[]{:S(2)}, u32[]{:S(2)}) collective-permute-start(bf16[512,1024]{1,0:T(8,128)(2,1)} %convolution_convert_fusion.9), channel_id=1, source_target_pairs={{0,4},{4,0},{1,5},{5,1},{2,6},{6,2},{3,7},{7,3},{8,12},{12,8},{9,1... | collective-permute-start | bytes 3145736 | tf_op jit(solution)/shard_map/ppermute | solution.py:92
  396.6 42.4 %collective-permute-start.52 = (bf16[2,2,128,1024]{3,2,1,0:T(8,128)(2,1)}, bf16[2,2,128,1024]{3,2,1,0:T(8,128)(2,1)}, u32[]{:S(2)}, u32[]{:S(2)}) collective-permute-start(bf16[2,2,128,1024]{3,2,1,0:T(8,128)(2,1)} %pad_maximum_fusion.15), channel_id=1, source_target_pairs={{0,8},{8,0},{1,9},{9,1},{2,10},{10,2},{3,11},{11,3},{4,12},{12,4},... | collective-permute-start | bytes 3145736 | tf_op jit(solution)/shard_map/ppermute | solution.py:92
  402.8 36.2 %collective-permute-start.53 = (bf16[2,2,128,1024]{3,2,1,0:T(8,128)(2,1)S(1)}, bf16[2,2,128,1024]{3,2,1,0:T(8,128)(2,1)}, u32[]{:S(2)}, u32[]{:S(2)}) collective-permute-start(bf16[2,2,128,1024]{3,2,1,0:T(8,128)(2,1)S(1)} %pad_maximum_fusion.16), channel_id=1, source_target_pairs={{0,16},{16,0},{1,17},{17,1},{2,18},{18,2},{3,19},{19,3},{4,20},{20... | collective-permute-start | bytes 3145736 | tf_op jit(solution)/shard_map/ppermute | solution.py:92
  409.3 58.8 %collective-permute-start.56 = (bf16[128,1024]{1,0:T(8,128)(2,1)}, bf16[128,1024]{1,0:T(8,128)(2,1)}, u32[]{:S(2)}, u32[]{:S(2)}) collective-permute-start(bf16[128,1024]{1,0:T(8,128)(2,1)} %slice_bitcast_fusion.26), channel_id=1, source_target_pairs={{0,3},{1,0},{2,1},{3,2},{4,7},{5,4},{6,5},{7,6},{8,11},{9,8},{10,9... | collective-permute-start | bytes 786440 | tf_op jit(solution)/shard_map/ppermute | solution.py:92
  429.3 38.8 %collective-permute-start.58 = (bf16[128,1024]{1,0:T(8,128)(2,1)}, bf16[128,1024]{1,0:T(8,128)(2,1)}, u32[]{:S(2)}, u32[]{:S(2)}) collective-permute-start(bf16[128,1024]{1,0:T(8,128)(2,1)} %get-tuple-element.376), channel_id=1, source_target_pairs={{0,1},{1,2},{2,3},{3,0},{4,5},{5,6},{6,7},{7,4},{8,9},{9,10},{10,1... | collective-permute-start | bytes 786440 | tf_op jit(solution)/shard_map/ppermute | solution.py:92
  433.3 34.8 %collective-permute-start.57 = (bf16[128,1024]{1,0:T(8,128)(2,1)}, bf16[128,1024]{1,0:T(8,128)(2,1)}, u32[]{:S(2)}, u32[]{:S(2)}) collective-permute-start(bf16[128,1024]{1,0:T(8,128)(2,1)} %get-tuple-element.377), channel_id=1, source_target_pairs={{0,2},{1,3},{2,0},{3,1},{4,6},{5,7},{6,4},{7,5},{8,10},{9,11},{10,... | collective-permute-start | bytes 786440 | tf_op jit(solution)/shard_map/ppermute | solution.py:92
  439.0 74.3 %all-to-all-start.4 = ((bf16[8,64,1024]{2,1,0:T(8,128)(2,1)}), bf16[8,64,1024]{2,1,0:T(8,128)(2,1)}, u32[]{:S(2)}, u32[]{:S(2)}) async-start(bf16[8,64,1024]{2,1,0:T(8,128)(2,1)} %bitcast.280), calls=%async_computation.4 | async-start | bytes 2097152 | tf_op jit(solution)/shard_map/all_to_all | solution.py:122
  444.8 152.8 %all-gather.6.cloned.1.call-start = ((), (), s32[]{:S(2)}) async-start(), calls=%async_computation.7 | async-start | bytes 2359296 | tf_op jit(solution)/shard_map/all_gather | solution.py:225
  487.1 25.1 %collective-permute-start.60 = (bf16[2,2,128,1024]{3,2,1,0:T(8,128)(2,1)}, bf16[2,2,128,1024]{3,2,1,0:T(8,128)(2,1)}, u32[]{:S(2)}, u32[]{:S(2)}) collective-permute-start(bf16[2,2,128,1024]{3,2,1,0:T(8,128)(2,1)} %pad_maximum_fusion.17), channel_id=1, source_target_pairs={{0,8},{8,0},{1,9},{9,1},{2,10},{10,2},{3,11},{11,3},{4,12},{12,4},... | collective-permute-start | bytes 3145736 | tf_op jit(solution)/shard_map/ppermute | solution.py:92
  488.2 25.1 %collective-permute-start.61 = (bf16[2,2,128,1024]{3,2,1,0:T(8,128)(2,1)}, bf16[2,2,128,1024]{3,2,1,0:T(8,128)(2,1)}, u32[]{:S(2)}, u32[]{:S(2)}) collective-permute-start(bf16[2,2,128,1024]{3,2,1,0:T(8,128)(2,1)} %pad_maximum_fusion.18), channel_id=1, source_target_pairs={{0,16},{16,0},{1,17},{17,1},{2,18},{18,2},{3,19},{19,3},{4,20},{20... | collective-permute-start | bytes 3145736 | tf_op jit(solution)/shard_map/ppermute | solution.py:92
  542.3 66.9 %all-to-all-start.5 = ((bf16[8,64,1024]{2,1,0:T(8,128)(2,1)}), bf16[8,64,1024]{2,1,0:T(8,128)(2,1)S(1)}, u32[]{:S(2)}, u32[]{:S(2)}) async-start(bf16[8,64,1024]{2,1,0:T(8,128)(2,1)} %bitcast.261), calls=%async_computation.5 | async-start | bytes 2097152 | tf_op jit(solution)/shard_map/all_to_all | solution.py:122
  547.4 71.8 %all-gather.8.cloned.1.call-start = ((), (), s32[]{:S(2)}) async-start(), calls=%async_computation.8 | async-start | bytes 2359296 | tf_op jit(solution)/shard_map/all_gather | solution.py:225
  559.8 35.2 %collective-permute-start.68 = (bf16[128,1024]{1,0:T(8,128)(2,1)}, bf16[128,1024]{1,0:T(8,128)(2,1)}, u32[]{:S(2)}, u32[]{:S(2)}) collective-permute-start(bf16[128,1024]{1,0:T(8,128)(2,1)} %get-tuple-element.373), channel_id=1, source_target_pairs={{0,2},{1,3},{2,0},{3,1},{4,6},{5,7},{6,4},{7,5},{8,10},{9,11},{10,... | collective-permute-start | bytes 786440 | tf_op jit(solution)/shard_map/ppermute | solution.py:92
  (188 other events, 1872.4 us)
Sparse Core Ops, SparseCore 0:
  439.1 42.3 all-gather.3
  513.5 34.7 all-gather.5
  552.6 29.7 all-gather.7

commit v6 on v5

--- a/solution.py
+++ b/solution.py
@@ -628,7 +628,7 @@
     self_mixed = tied(self_mixed, up_weights.mine, down_weights.mine)
     w_o, w_mem, w_cq, w_co = cross_weights.result()
     normed_two, after_self = normalize([residual, *own_parts(self_mixed, w_o)], gain_two)
-    normed_two = meet(normed_two, up_weights)
+    normed_two, down_weights.got[0] = meet((normed_two, down_weights.got[0]), up_weights)
     up_weights.three()
     normed_two, source_own = tied((normed_two, source_own), up_weights.mine)
     source = both(source_own)
@@ -708,11 +708,12 @@
     gqkv, g_self, cross_sum.got = lax.optimization_barrier((gqkv, g_self, cross_sum.got))
     self_sum = Sum([g_o, g_self])
     cross_sum.three()
-    first_back, grad_memory, up_total = meet((own_parts(gqkv, w_self), grad_memory, up_sum.result()), self_sum)
+    first_back, grad_memory, up_total = meet(
+        (own_parts(gqkv, w_self), grad_memory, up_sum.result()), self_sum, cross_sum
+    )
     self_sum.two()
     up_all = gathered(up_total)
     _, grad_inputs, grad_gain_one = normalize_back(residual, gain_one, first_back, grad_after_self)
-    grad_inputs, cross_sum.got = lax.optimization_barrier((grad_inputs, cross_sum.got))
     grad_inputs = from_row(grad_inputs, rows).astype(F32)
     gains = jnp.stack([grad_gain_one, grad_gain_two, grad_gain_three])
     for axis in ("core", "yy", "batch"):

time: 647 us -> 626 us (0.968)
  waiting for transfers between devices: 163 us -> 142 us
    ppermute x73, waiting for transfers between devices: 137 us -> 118 us  [shift(): lax.ppermute(piece, axis, [(i, (i + step) % count) for i in range(count)])]
    unnamed x284 -> x276, local copies, waits for them, and re-layouts: 25.6 us -> 26.6 us
  transfers between devices with their start and end apart: 87 -> 87, of which waited for: 28 -> 31; matrix products, arithmetic and copies ran while one was open for 28% -> 29% of each run, Pallas kernels for 12% -> 13%
where the time goes in v6:
time: 626 us; the launch traced here: 617 us
  waiting for transfers between devices  142 us (23%)
  starting transfers between devices  135 us (22%)
  matrix products  103 us (16%)
  Pallas kernels  83.8 us (13%)
  other arithmetic  74.3 us (12%)
  local copies, waits for them, and re-layouts  63.5 us (10%)
  between operations  16.1 us (3%)
    ppermute x73, waiting for transfers between devices, shift(): lax.ppermute(piece, axis, [(i, (i + step) % count) for i in range(count)])  118 us
    dot_general x28, matrix products, dot(): lax.dot_general(left, right, (((left_dim,), (right_dim,)), ((), ())), pre...  103 us
    ppermute x73, starting transfers between devices, shift(): lax.ppermute(piece, axis, [(i, (i + step) % count) for i in range(count)])  98.9 us
    pallas_call x4, Pallas kernels, call(): pl.pallas_call(functools.partial(kernel, self.index, layouts, self.chunk)...  60.2 us
    another operation x20, other arithmetic, three(): self.send(jnp.stack(first, 0), jnp.stack(second, 0), 'yy', 'batch')  30.5 us
    convert_element_type x20, other arithmetic, add(): return total.astype(BF)  28.9 us
    unnamed x276, local copies, waits for them, and re-layouts  26.6 us
    all_to_all x3, waiting for transfers between devices, to_row(): moved = lax.all_to_all(tokens, ('yy', 'head'), 0, 0, tiled=True)  20.6 us
  transfers between devices with their start and end apart: 87, of which 31 were waited for; matrix products, arithmetic and copies ran while one was open for 29% of the time, Pallas kernels for 13%

profile of v6, /device:TPU:1, one launch (start us, length us, event | category | flops | bytes accessed | tf_op | source)
XLA Modules:
  0.0 616.9 jit_solution(16853242046714372465)
XLA Ops:
  17.7 13.0 %collective-permute-done.1 = bf16[96,1024]{1,0:T(8,128)(2,1)S(1)} collective-permute-done((bf16[96,1024]{1,0:T(8,128)(2,1)S(1)}, bf16[96,1024]{1,0:T(8,128)(2,1)S(1)}, u32[]{:S(2)}, u32[]{:S(2)}) %collective-permute-start.1) | collective-permute-done | bytes 196640 | tf_op jit(solution)/shard_map/ppermute | solution.py:92
  31.5 4.7 all-to-all-start
  54.4 7.8 %collective-permute-done.4 = bf16[2,96,1024]{2,1,0:T(8,128)(2,1)} collective-permute-done((bf16[2,96,1024]{2,1,0:T(8,128)(2,1)}, bf16[2,96,1024]{2,1,0:T(8,128)(2,1)}, u32[]{:S(2)}, u32[]{:S(2)}) %collective-permute-start.4) | collective-permute-done | bytes 393248 | tf_op jit(solution)/shard_map/ppermute | solution.py:92
  77.9 13.8 %collective-permute-done.7 = bf16[2,2,96,1024]{3,2,1,0:T(8,128)(2,1)} collective-permute-done((bf16[2,2,96,1024]{3,2,1,0:T(8,128)(2,1)}, bf16[2,2,96,1024]{3,2,1,0:T(8,128)(2,1)}, u32[]{:S(2)}, u32[]{:S(2)}) %collective-permute-start.7) | collective-permute-done | bytes 786464 | tf_op jit(solution)/shard_map/ppermute | solution.py:92
  91.7 7.0 %convolution_convert_fusion.1.refs_0_ = bf16[1536,1024]{1,0:T(8,128)(2,1)} fusion(bf16[1024,1024]{1,0:T(8,128)(2,1)S(1)} %pad_maximum_fusion.3, bf16[384,1024]{1,0:T(8,128)(2,1)} %bitcast.24, bf16[384,1024]{1,0:T(8,128)(2,1)} %bitcast.23, bf16[384,1024]{1,0:T(8,128)(2,1)} %bitcast.22, bf16[384,1024]{1,0:T(8,128)(2,1)} %bitcast.18), kind=kOutput, calls=%fused_computation.8 | convolution fusion | flops 3235381248 | bytes 8388608 | tf_op jit(solution)/shard_map/dot_general | solution.py:25
  98.7 4.5 collective-permute-done.9
  112.9 4.3 all-to-all-start.1
  127.1 11.7 %shard_map.298 = (bf16[512,1024]{1,0:T(8,128)(2,1)S(1)}, f32[2,4,1,1024]{3,2,1,0:T(1,128)S(1)}) custom-call(s32[16]{0:T(128)S(1)} %select_n.214.need_ref, s32[4]{0:T(128)S(1)} %get-tuple-element.398.base_ref, s32[2,1024]{1,0:T(2,128)S(1)} %pad_add_fusion.1.span_ref, bf16[1536,1024]{1,0:T(8,128)(2,1)S(1)} %copy-done.43), custom_call_target="tpu_custom_call" | custom-call | flops 40000000000 | bytes 8388608 | tf_op jit(solution)/shard_map/pallas_call | solution.py:465
  143.2 14.5 %all-to-all-done.1 = bf16[8,64,1024]{2,1,0:T(8,128)(2,1)} async-done(((bf16[8,64,1024]{2,1,0:T(8,128)(2,1)}), bf16[8,64,1024]{2,1,0:T(8,128)(2,1)}, u32[]{:S(2)}, u32[]{:S(2)}) %all-to-all-start.1) | async-done | bytes 1048608 | tf_op jit(solution)/shard_map/all_to_all | solution.py:116
  164.7 6.6 %collective-permute-start.18 = (bf16[512,1024]{1,0:T(8,128)(2,1)S(1)}, bf16[512,1024]{1,0:T(8,128)(2,1)S(1)}, u32[]{:S(2)}, u32[]{:S(2)}) collective-permute-start(bf16[512,1024]{1,0:T(8,128)(2,1)S(1)} %convolution_convert_fusion.15), channel_id=1, source_target_pairs={{0,4},{4,0},{1,5},{5,1},{2,6},{6,2},{3,7},{7,3},{8,12},{12,8},{9,1... | collective-permute-start | bytes 3145736 | tf_op jit(solution)/shard_map/ppermute | solution.py:92
  192.2 5.1 collective-permute-start.24
  210.3 4.4 collective-permute-done.24
  223.3 14.2 %shard_map.300 = (bf16[512,1024]{1,0:T(8,128)(2,1)S(1)}, f32[2,4,1,1024]{3,2,1,0:T(1,128)S(1)}) custom-call(s32[16]{0:T(128)S(1)} %select_n.206.need_ref, s32[4]{0:T(128)S(1)} %get-tuple-element.398.base_ref, s32[2,1024]{1,0:T(2,128)S(1)} %pad_add_fusion.span_ref, bf16[512,1024]{1,0:T(8,128)(2,1)S(1)} %convolution_convert_fusion.12.refs_0_, ...), custom_call_target="tpu_custom_call" | custom-call | flops 40000000000 | bytes 8388608 | tf_op jit(solution)/shard_map/pallas_call | solution.py:465
  241.2 6.1 all-to-all-done.2
  260.1 14.1 %add_convert_fusion = (bf16[2048,1024]{1,0:T(8,128)(2,1)}, bf16[2048,1024]{1,0:T(8,128)(2,1)}) fusion(bf16[1024,1024]{1,0:T(8,128)(2,1)S(1)} %constant_dynamic-update-slice_fusion.4, bf16[512,1024]{1,0:T(8,128)(2,1)} %bitcast.73, bf16[512,1024]{1,0:T(8,128)(2,1)} %bitcast.72, bf16[512,1024]{1,0:T(8,128)(2,1)} %bitcast.71, bf16[512,1024]{1,0:T(8,128)(2,1)} %bitcast.70), kind=kOutput, calls=%fused_computation.1 | convolution fusion | flops 4349493248 | bytes 14680064 | tf_op jit(solution)/shard_map/dot_general | solution.py:25
  274.2 6.9 %convolution_convert_fusion.3 = bf16[2048,1024]{1,0:T(8,128)(2,1)S(1)} fusion(bf16[2048,1024]{1,0:T(8,128)(2,1)} %get-tuple-element.232, bf16[1024,1024]{1,0:T(8,128)(2,1)S(1)} %constant_dynamic-update-slice_fusion.6), kind=kOutput, calls=%fused_computation.10 | convolution fusion | flops 4297064448 | bytes 10485760 | tf_op jit(solution)/shard_map/dot_general | solution.py:25
  288.9 11.9 %multiply_convert_fusion = bf16[2048,1024]{1,0:T(8,128)(2,1)} fusion(bf16[2048,1024]{1,0:T(8,128)(2,1)} %get-tuple-element.215, bf16[1024,1024]{1,0:T(8,128)(2,1)S(1)} %constant_dynamic-update-slice_fusion.6, bf16[512,1024]{1,0:T(8,128)(2,1)S(1)} %bitcast.381, bf16[512,1024]{1,0:T(8,128)(2,1)S(1)} %bitcast.286, bf16[512,1024]{1,0:T(8,128)(2,1)S(1)} %bitcast.384, ...), kind=kOutput, calls=%fused_computation | convolution fusion | flops 4318035968 | bytes 14680064 | tf_op jit(solution)/shard_map/dot_general | solution.py:25
  304.2 4.2 all-to-all-start.3
  318.1 4.6 fusion.15
  331.1 4.7 convolution_convert_fusion.2
  345.7 18.8 %shard_map.303 = (bf16[512,1024]{1,0:T(8,128)(2,1)S(1)}, bf16[1024,1024]{1,0:T(8,128)(2,1)S(1)}) custom-call(s32[16]{0:T(128)S(1)} %select_n.206.need_ref, s32[4]{0:T(128)S(1)} %get-tuple-element.398.base_ref, s32[2,1024]{1,0:T(2,128)S(1)} %pad_add_fusion.span_ref, bf16[512,1024]{1,0:T(8,128)(2,1)S(1)} %copy-done.36, bf16[1024,1024]{1,0:T(8,128)(2,1)S(1)} %copy-done.42, ...), custom_call_target="tpu_custom_call" | custom-call | flops 46000001024 | bytes 8388608 | tf_op jit(solution)/shard_map/pallas_call | solution.py:465
  386.3 10.4 %collective-permute-start.48 = (bf16[2,128,1024]{2,1,0:T(8,128)(2,1)}, bf16[2,128,1024]{2,1,0:T(8,128)(2,1)}, u32[]{:S(2)}, u32[]{:S(2)}) collective-permute-start(bf16[2,128,1024]{2,1,0:T(8,128)(2,1)} %slice_bitcast_fusion.9), channel_id=1, source_target_pairs={{0,16},{16,0},{1,17},{17,1},{2,18},{18,2},{3,19},{19,3},{4,20},{20... | collective-permute-start | bytes 1572872 | tf_op jit(solution)/shard_map/ppermute | solution.py:92
  431.2 4.4 all-to-all-start.4
  442.2 15.4 %shard_map.305 = bf16[1536,1024]{1,0:T(8,128)(2,1)S(1)} custom-call(s32[16]{0:T(128)S(1)} %copy-done.26, s32[4]{0:T(128)S(1)} %get-tuple-element.398.base_ref, s32[2,1024]{1,0:T(2,128)S(1)} %copy-done.24, bf16[1536,1024]{1,0:T(8,128)(2,1)S(1)} %copy-done.44, bf16[512,1024]{1,0:T(8,128)(2,1)S(1)} %copy-done.29, bf16[512,1024]{1,0:T(8,128)(2,1)S(1)} %copy-done.37, ...), custom_call_target="tpu_custom_call" | custom-call | flops 46000001024 | bytes 8388608 | tf_op jit(solution)/shard_map/pallas_call | solution.py:465
  458.4 7.9 %collective-permute-done.55 = bf16[2,128,1024]{2,1,0:T(8,128)(2,1)S(1)} collective-permute-done((bf16[2,128,1024]{2,1,0:T(8,128)(2,1)S(1)}, bf16[2,128,1024]{2,1,0:T(8,128)(2,1)S(1)}, u32[]{:S(2)}, u32[]{:S(2)}) %collective-permute-start.55) | collective-permute-done | bytes 524320 | tf_op jit(solution)/shard_map/ppermute | solution.py:92
  470.3 4.8 fusion.12
  475.0 4.2 collective-permute-start.59
  486.5 5.0 fusion.10.own_ref
  493.5 11.9 %collective-permute-done.63 = bf16[128,1024]{1,0:T(8,128)(2,1)} collective-permute-done((bf16[128,1024]{1,0:T(8,128)(2,1)}, bf16[128,1024]{1,0:T(8,128)(2,1)}, u32[]{:S(2)}, u32[]{:S(2)}) %collective-permute-start.63) | collective-permute-done | bytes 262176 | tf_op jit(solution)/shard_map/ppermute | solution.py:92
  515.0 4.3 shard_map.307
  542.3 4.8 collective-permute-start.71
  556.6 14.3 %collective-permute-done.68 = bf16[128,1024]{1,0:T(8,128)(2,1)} collective-permute-done((bf16[128,1024]{1,0:T(8,128)(2,1)}, bf16[128,1024]{1,0:T(8,128)(2,1)}, u32[]{:S(2)}, u32[]{:S(2)}) %collective-permute-start.68) | collective-permute-done | bytes 262176 | tf_op jit(solution)/shard_map/ppermute | solution.py:92
  (586 shorter events, 330.2 us)
Async XLA Ops:
  31.5 30.7 %all-to-all-start = ((bf16[8,64,1024]{2,1,0:T(8,128)(2,1)}), bf16[8,64,1024]{2,1,0:T(8,128)(2,1)S(1)}, u32[]{:S(2)}, u32[]{:S(2)}) async-start(bf16[8,64,1024]{2,1,0:T(8,128)(2,1)} %param.18), calls=%async_computation | async-start | bytes 2097152 | tf_op jit(solution)/shard_map/all_to_all | solution.py:116
  74.7 28.5 %collective-permute-start.9 = (bf16[160,1024]{1,0:T(8,128)(2,1)S(1)}, bf16[160,1024]{1,0:T(8,128)(2,1)S(1)}, u32[]{:S(2)}, u32[]{:S(2)}) collective-permute-start(bf16[160,1024]{1,0:T(8,128)(2,1)S(1)} %copy-done.96), channel_id=1, source_target_pairs={{0,2},{1,3},{2,0},{3,1},{4,6},{5,7},{6,4},{7,5},{8,10},{9,11},{10,... | collective-permute-start | bytes 983048 | tf_op jit(solution)/shard_map/ppermute | solution.py:92
  74.9 28.3 %collective-permute-start.8 = (bf16[160,1024]{1,0:T(8,128)(2,1)S(1)}, bf16[160,1024]{1,0:T(8,128)(2,1)S(1)}, u32[]{:S(2)}, u32[]{:S(2)}) collective-permute-start(bf16[160,1024]{1,0:T(8,128)(2,1)S(1)} %copy-done.96), channel_id=1, source_target_pairs={{0,1},{1,2},{2,3},{3,0},{4,5},{5,6},{6,7},{7,4},{8,9},{9,10},{10,1... | collective-permute-start | bytes 983048 | tf_op jit(solution)/shard_map/ppermute | solution.py:92
  108.5 34.6 %collective-permute-start.17 = (bf16[128,1024]{1,0:T(8,128)(2,1)S(1)}, bf16[128,1024]{1,0:T(8,128)(2,1)}, u32[]{:S(2)}, u32[]{:S(2)}) collective-permute-start(bf16[128,1024]{1,0:T(8,128)(2,1)S(1)} %bitcast.289), channel_id=1, source_target_pairs={{0,3},{1,0},{2,1},{3,2},{4,7},{5,4},{6,5},{7,6},{8,11},{9,8},{10,9... | collective-permute-start | bytes 786440 | tf_op jit(solution)/shard_map/ppermute | solution.py:92
  108.6 34.6 %collective-permute-start.16 = (bf16[128,1024]{1,0:T(8,128)(2,1)S(1)}, bf16[128,1024]{1,0:T(8,128)(2,1)}, u32[]{:S(2)}, u32[]{:S(2)}) collective-permute-start(bf16[128,1024]{1,0:T(8,128)(2,1)S(1)} %bitcast.290), channel_id=1, source_target_pairs={{0,2},{1,3},{2,0},{3,1},{4,6},{5,7},{6,4},{7,5},{8,10},{9,11},{10,... | collective-permute-start | bytes 786440 | tf_op jit(solution)/shard_map/ppermute | solution.py:92
  111.5 31.7 %collective-permute-start.15 = (bf16[128,1024]{1,0:T(8,128)(2,1)S(1)}, bf16[128,1024]{1,0:T(8,128)(2,1)}, u32[]{:S(2)}, u32[]{:S(2)}) collective-permute-start(bf16[128,1024]{1,0:T(8,128)(2,1)S(1)} %bitcast.291), channel_id=1, source_target_pairs={{0,1},{1,2},{2,3},{3,0},{4,5},{5,6},{6,7},{7,4},{8,9},{9,10},{10,1... | collective-permute-start | bytes 786440 | tf_op jit(solution)/shard_map/ppermute | solution.py:92
  112.9 44.8 %all-to-all-start.1 = ((bf16[8,64,1024]{2,1,0:T(8,128)(2,1)}), bf16[8,64,1024]{2,1,0:T(8,128)(2,1)}, u32[]{:S(2)}, u32[]{:S(2)}) async-start(bf16[8,64,1024]{2,1,0:T(8,128)(2,1)} %param.19), calls=%async_computation.1 | async-start | bytes 2097152 | tf_op jit(solution)/shard_map/all_to_all | solution.py:116
  123.4 34.3 %collective-permute-start.14 = (bf16[2,2,160,1024]{3,2,1,0:T(8,128)(2,1)}, bf16[2,2,160,1024]{3,2,1,0:T(8,128)(2,1)}, u32[]{:S(2)}, u32[]{:S(2)}) collective-permute-start(bf16[2,2,160,1024]{3,2,1,0:T(8,128)(2,1)} %pad_maximum_fusion.7), channel_id=1, source_target_pairs={{0,16},{16,0},{1,17},{17,1},{2,18},{18,2},{3,19},{19,3},{4,20},{20... | collective-permute-start | bytes 3932168 | tf_op jit(solution)/shard_map/ppermute | solution.py:92
  126.5 31.2 %collective-permute-start.13 = (bf16[2,2,160,1024]{3,2,1,0:T(8,128)(2,1)}, bf16[2,2,160,1024]{3,2,1,0:T(8,128)(2,1)}, u32[]{:S(2)}, u32[]{:S(2)}) collective-permute-start(bf16[2,2,160,1024]{3,2,1,0:T(8,128)(2,1)} %pad_maximum_fusion.6), channel_id=1, source_target_pairs={{0,8},{8,0},{1,9},{9,1},{2,10},{10,2},{3,11},{11,3},{4,12},{12,4},... | collective-permute-start | bytes 3932168 | tf_op jit(solution)/shard_map/ppermute | solution.py:92
  199.7 38.8 %collective-permute-start.27 = (bf16[2,2,128,1024]{3,2,1,0:T(8,128)(2,1)}, bf16[2,2,128,1024]{3,2,1,0:T(8,128)(2,1)}, u32[]{:S(2)}, u32[]{:S(2)}) collective-permute-start(bf16[2,2,128,1024]{3,2,1,0:T(8,128)(2,1)} %pad_maximum_fusion.11), channel_id=1, source_target_pairs={{0,16},{16,0},{1,17},{17,1},{2,18},{18,2},{3,19},{19,3},{4,20},{20... | collective-permute-start | bytes 3145736 | tf_op jit(solution)/shard_map/ppermute | solution.py:92
  202.1 36.4 %collective-permute-start.26 = (bf16[2,2,128,1024]{3,2,1,0:T(8,128)(2,1)}, bf16[2,2,128,1024]{3,2,1,0:T(8,128)(2,1)}, u32[]{:S(2)}, u32[]{:S(2)}) collective-permute-start(bf16[2,2,128,1024]{3,2,1,0:T(8,128)(2,1)} %pad_maximum_fusion.10), channel_id=1, source_target_pairs={{0,8},{8,0},{1,9},{9,1},{2,10},{10,2},{3,11},{11,3},{4,12},{12,4},... | collective-permute-start | bytes 3145736 | tf_op jit(solution)/shard_map/ppermute | solution.py:92
  218.1 29.2 %all-to-all-start.2 = ((bf16[8,64,1024]{2,1,0:T(8,128)(2,1)}), bf16[8,64,1024]{2,1,0:T(8,128)(2,1)S(1)}, u32[]{:S(2)}, u32[]{:S(2)}) async-start(bf16[8,64,1024]{2,1,0:T(8,128)(2,1)} %param.20), calls=%async_computation.2 | async-start | bytes 2097152 | tf_op jit(solution)/shard_map/all_to_all | solution.py:116
  257.7 25.6 %collective-permute-start.34 = (bf16[2,2,128,1024]{3,2,1,0:T(8,128)(2,1)S(1)}, bf16[2,2,128,1024]{3,2,1,0:T(8,128)(2,1)S(1)}, u32[]{:S(2)}, u32[]{:S(2)}) collective-permute-start(bf16[2,2,128,1024]{3,2,1,0:T(8,128)(2,1)S(1)} %pad_maximum_fusion.13), channel_id=1, source_target_pairs={{0,16},{16,0},{1,17},{17,1},{2,18},{18,2},{3,19},{19,3},{4,20},{20... | collective-permute-start | bytes 3145736 | tf_op jit(solution)/shard_map/ppermute | solution.py:92
  258.2 25.1 %collective-permute-start.33 = (bf16[2,2,128,1024]{3,2,1,0:T(8,128)(2,1)S(1)}, bf16[2,2,128,1024]{3,2,1,0:T(8,128)(2,1)S(1)}, u32[]{:S(2)}, u32[]{:S(2)}) collective-permute-start(bf16[2,2,128,1024]{3,2,1,0:T(8,128)(2,1)S(1)} %pad_maximum_fusion.12), channel_id=1, source_target_pairs={{0,8},{8,0},{1,9},{9,1},{2,10},{10,2},{3,11},{11,3},{4,12},{12,4},... | collective-permute-start | bytes 3145736 | tf_op jit(solution)/shard_map/ppermute | solution.py:92
  304.2 62.9 %all-to-all-start.3 = ((bf16[8,64,1024]{2,1,0:T(8,128)(2,1)}), bf16[8,64,1024]{2,1,0:T(8,128)(2,1)}, u32[]{:S(2)}, u32[]{:S(2)}) async-start(bf16[8,64,1024]{2,1,0:T(8,128)(2,1)} %bitcast.281), calls=%async_computation.3 | async-start | bytes 2097152 | tf_op jit(solution)/shard_map/all_to_all | solution.py:122
  308.4 243.2 %all-gather.4.cloned.1.call-start = ((), (), s32[]{:S(2)}) async-start(), calls=%async_computation.6 | async-start | bytes 2359296 | tf_op jit(solution)/shard_map/all_gather | solution.py:225
  337.5 29.6 %collective-permute-start.42 = (bf16[2,2,128,1024]{3,2,1,0:T(8,128)(2,1)S(1)}, bf16[2,2,128,1024]{3,2,1,0:T(8,128)(2,1)}, u32[]{:S(2)}, u32[]{:S(2)}) collective-permute-start(bf16[2,2,128,1024]{3,2,1,0:T(8,128)(2,1)S(1)} %bitcast.300), channel_id=1, source_target_pairs={{0,8},{8,0},{1,9},{9,1},{2,10},{10,2},{3,11},{11,3},{4,12},{12,4},... | collective-permute-start | bytes 3145736 | tf_op jit(solution)/shard_map/ppermute | solution.py:92
  338.3 28.8 %collective-permute-start.43 = (bf16[2,2,128,1024]{3,2,1,0:T(8,128)(2,1)S(1)}, bf16[2,2,128,1024]{3,2,1,0:T(8,128)(2,1)}, u32[]{:S(2)}, u32[]{:S(2)}) collective-permute-start(bf16[2,2,128,1024]{3,2,1,0:T(8,128)(2,1)S(1)} %bitcast.299), channel_id=1, source_target_pairs={{0,16},{16,0},{1,17},{17,1},{2,18},{18,2},{3,19},{19,3},{4,20},{20... | collective-permute-start | bytes 3145736 | tf_op jit(solution)/shard_map/ppermute | solution.py:92
  385.4 25.8 %collective-permute-start.49 = (bf16[2,128,1024]{2,1,0:T(8,128)(2,1)}, bf16[2,128,1024]{2,1,0:T(8,128)(2,1)}, u32[]{:S(2)}, u32[]{:S(2)}) collective-permute-start(bf16[2,128,1024]{2,1,0:T(8,128)(2,1)} %slice_bitcast_fusion.8), channel_id=1, source_target_pairs={{0,8},{8,0},{1,9},{9,1},{2,10},{10,2},{3,11},{11,3},{4,12},{12,4},... | collective-permute-start | bytes 1572872 | tf_op jit(solution)/shard_map/ppermute | solution.py:92
  400.2 28.8 %collective-permute-start.52 = (bf16[2,2,128,1024]{3,2,1,0:T(8,128)(2,1)}, bf16[2,2,128,1024]{3,2,1,0:T(8,128)(2,1)}, u32[]{:S(2)}, u32[]{:S(2)}) collective-permute-start(bf16[2,2,128,1024]{3,2,1,0:T(8,128)(2,1)} %pad_maximum_fusion.15), channel_id=1, source_target_pairs={{0,8},{8,0},{1,9},{9,1},{2,10},{10,2},{3,11},{11,3},{4,12},{12,4},... | collective-permute-start | bytes 3145736 | tf_op jit(solution)/shard_map/ppermute | solution.py:92
  413.4 45.0 %collective-permute-start.56 = (bf16[128,1024]{1,0:T(8,128)(2,1)}, bf16[128,1024]{1,0:T(8,128)(2,1)}, u32[]{:S(2)}, u32[]{:S(2)}) collective-permute-start(bf16[128,1024]{1,0:T(8,128)(2,1)} %slice_bitcast_fusion.26), channel_id=1, source_target_pairs={{0,3},{1,0},{2,1},{3,2},{4,7},{5,4},{6,5},{7,6},{8,11},{9,8},{10,9... | collective-permute-start | bytes 786440 | tf_op jit(solution)/shard_map/ppermute | solution.py:92
  416.3 42.1 %collective-permute-start.58 = (bf16[128,1024]{1,0:T(8,128)(2,1)}, bf16[128,1024]{1,0:T(8,128)(2,1)}, u32[]{:S(2)}, u32[]{:S(2)}) collective-permute-start(bf16[128,1024]{1,0:T(8,128)(2,1)} %get-tuple-element.376), channel_id=1, source_target_pairs={{0,1},{1,2},{2,3},{3,0},{4,5},{5,6},{6,7},{7,4},{8,9},{9,10},{10,1... | collective-permute-start | bytes 786440 | tf_op jit(solution)/shard_map/ppermute | solution.py:92
  422.0 36.4 %collective-permute-start.57 = (bf16[128,1024]{1,0:T(8,128)(2,1)}, bf16[128,1024]{1,0:T(8,128)(2,1)}, u32[]{:S(2)}, u32[]{:S(2)}) collective-permute-start(bf16[128,1024]{1,0:T(8,128)(2,1)} %get-tuple-element.377), channel_id=1, source_target_pairs={{0,2},{1,3},{2,0},{3,1},{4,6},{5,7},{6,4},{7,5},{8,10},{9,11},{10,... | collective-permute-start | bytes 786440 | tf_op jit(solution)/shard_map/ppermute | solution.py:92
  431.2 76.7 %all-to-all-start.4 = ((bf16[8,64,1024]{2,1,0:T(8,128)(2,1)}), bf16[8,64,1024]{2,1,0:T(8,128)(2,1)}, u32[]{:S(2)}, u32[]{:S(2)}) async-start(bf16[8,64,1024]{2,1,0:T(8,128)(2,1)} %bitcast.280), calls=%async_computation.4 | async-start | bytes 2097152 | tf_op jit(solution)/shard_map/all_to_all | solution.py:122
  435.6 137.9 %all-gather.6.cloned.1.call-start = ((), (), s32[]{:S(2)}) async-start(), calls=%async_computation.7 | async-start | bytes 2359296 | tf_op jit(solution)/shard_map/all_gather | solution.py:225
  439.6 26.7 %collective-permute-start.55 = (bf16[2,128,1024]{2,1,0:T(8,128)(2,1)S(1)}, bf16[2,128,1024]{2,1,0:T(8,128)(2,1)S(1)}, u32[]{:S(2)}, u32[]{:S(2)}) collective-permute-start(bf16[2,128,1024]{2,1,0:T(8,128)(2,1)S(1)} %slice_bitcast_fusion.4), channel_id=1, source_target_pairs={{0,8},{8,0},{1,9},{9,1},{2,10},{10,2},{3,11},{11,3},{4,12},{12,4},... | collective-permute-start | bytes 1572872 | tf_op jit(solution)/shard_map/ppermute | solution.py:92
  441.1 25.2 %collective-permute-start.54 = (bf16[2,128,1024]{2,1,0:T(8,128)(2,1)S(1)}, bf16[2,128,1024]{2,1,0:T(8,128)(2,1)S(1)}, u32[]{:S(2)}, u32[]{:S(2)}) collective-permute-start(bf16[2,128,1024]{2,1,0:T(8,128)(2,1)S(1)} %slice_bitcast_fusion.5), channel_id=1, source_target_pairs={{0,16},{16,0},{1,17},{17,1},{2,18},{18,2},{3,19},{19,3},{4,20},{20... | collective-permute-start | bytes 1572872 | tf_op jit(solution)/shard_map/ppermute | solution.py:92
  475.0 30.4 %collective-permute-start.59 = (bf16[512,1024]{1,0:T(8,128)(2,1)}, bf16[512,1024]{1,0:T(8,128)(2,1)}, u32[]{:S(2)}, u32[]{:S(2)}) collective-permute-start(bf16[512,1024]{1,0:T(8,128)(2,1)} %fusion.12), channel_id=1, source_target_pairs={{0,4},{4,0},{1,5},{5,1},{2,6},{6,2},{3,7},{7,3},{8,12},{12,8},{9,1... | collective-permute-start | bytes 3145736 | tf_op jit(solution)/shard_map/ppermute | solution.py:92
  481.7 25.1 %collective-permute-start.60 = (bf16[2,2,128,1024]{3,2,1,0:T(8,128)(2,1)}, bf16[2,2,128,1024]{3,2,1,0:T(8,128)(2,1)}, u32[]{:S(2)}, u32[]{:S(2)}) collective-permute-start(bf16[2,2,128,1024]{3,2,1,0:T(8,128)(2,1)} %pad_maximum_fusion.17), channel_id=1, source_target_pairs={{0,8},{8,0},{1,9},{9,1},{2,10},{10,2},{3,11},{11,3},{4,12},{12,4},... | collective-permute-start | bytes 3145736 | tf_op jit(solution)/shard_map/ppermute | solution.py:92
  520.3 69.1 %all-to-all-start.5 = ((bf16[8,64,1024]{2,1,0:T(8,128)(2,1)}), bf16[8,64,1024]{2,1,0:T(8,128)(2,1)S(1)}, u32[]{:S(2)}, u32[]{:S(2)}) async-start(bf16[8,64,1024]{2,1,0:T(8,128)(2,1)} %bitcast.261), calls=%async_computation.5 | async-start | bytes 2097152 | tf_op jit(solution)/shard_map/all_to_all | solution.py:122
  524.2 74.4 %all-gather.8.cloned.1.call-start = ((), (), s32[]{:S(2)}) async-start(), calls=%async_computation.8 | async-start | bytes 2359296 | tf_op jit(solution)/shard_map/all_gather | solution.py:225
  540.6 30.3 %collective-permute-start.68 = (bf16[128,1024]{1,0:T(8,128)(2,1)}, bf16[128,1024]{1,0:T(8,128)(2,1)}, u32[]{:S(2)}, u32[]{:S(2)}) collective-permute-start(bf16[128,1024]{1,0:T(8,128)(2,1)} %get-tuple-element.373), channel_id=1, source_target_pairs={{0,2},{1,3},{2,0},{3,1},{4,6},{5,7},{6,4},{7,5},{8,10},{9,11},{10,... | collective-permute-start | bytes 786440 | tf_op jit(solution)/shard_map/ppermute | solution.py:92
  (184 other events, 1744.8 us)
Sparse Core Ops, SparseCore 0:
  431.3 41.3 all-gather.3
  508.0 35.6 all-gather.5
  546.2 34.2 all-gather.7

commit v7 on v6

--- a/solution.py
+++ b/solution.py
@@ -708,13 +708,12 @@
     gqkv, g_self, cross_sum.got = lax.optimization_barrier((gqkv, g_self, cross_sum.got))
     self_sum = Sum([g_o, g_self])
     cross_sum.three()
-    first_back, grad_memory, up_total = meet(
-        (own_parts(gqkv, w_self), grad_memory, up_sum.result()), self_sum, cross_sum
-    )
+    first_back, grad_memory = lax.optimization_barrier((own_parts(gqkv, w_self), grad_memory))
+    _, grad_inputs, grad_gain_one = normalize_back(residual, gain_one, first_back, grad_after_self)
+    grad_inputs, up_total = meet((grad_inputs, up_sum.result()), self_sum, cross_sum)
+    grad_inputs = from_row(grad_inputs, rows).astype(F32)
     self_sum.two()
     up_all = gathered(up_total)
-    _, grad_inputs, grad_gain_one = normalize_back(residual, gain_one, first_back, grad_after_self)
-    grad_inputs = from_row(grad_inputs, rows).astype(F32)
     gains = jnp.stack([grad_gain_one, grad_gain_two, grad_gain_three])
     for axis in ("core", "yy", "batch"):
         gains = total_of(gains, axis)

time: 626 us -> 622 us (level)
    ppermute x73, starting transfers between devices: 98.9 us -> 112 us  [shift(): lax.ppermute(piece, axis, [(i, (i + step) % count) for i in range(count)])]
    ppermute x5, starting transfers between devices: 10.7 us -> 4.38 us  [total_of(): lax.ppermute(value, axis, [(i, i ^ step) for i in range(count)])]
    unnamed x276 -> x250, local copies, waits for them, and re-layouts: 26.6 us -> 28.4 us
  transfers between devices with their start and end apart: 87 -> 87, of which waited for: 31 -> 33; matrix products, arithmetic and copies ran while one was open for 29% -> 29% of each run, Pallas kernels for 13% -> 12%
where the time goes in v7:
time: 622 us; the launch traced here: 612 us
  starting transfers between devices  141 us (23%)
  waiting for transfers between devices  139 us (22%)
  matrix products  102 us (16%)
  Pallas kernels  79.7 us (13%)
  other arithmetic  69.8 us (11%)
  local copies, waits for them, and re-layouts  64.4 us (10%)
  between operations  16 us (3%)
    ppermute x73, waiting for transfers between devices, shift(): lax.ppermute(piece, axis, [(i, (i + step) % count) for i in range(count)])  112 us
    ppermute x73, starting transfers between devices, shift(): lax.ppermute(piece, axis, [(i, (i + step) % count) for i in range(count)])  112 us
    dot_general x28, matrix products, dot(): lax.dot_general(left, right, (((left_dim,), (right_dim,)), ((), ())), pre...  102 us
    pallas_call x4, Pallas kernels, call(): pl.pallas_call(functools.partial(kernel, self.index, layouts, self.chunk)...  57.2 us
    another operation x20, other arithmetic, three(): self.send(jnp.stack(first, 0), jnp.stack(second, 0), 'yy', 'batch')  30.3 us
    unnamed x250, local copies, waits for them, and re-layouts  28.4 us
    convert_element_type x20, other arithmetic, add(): return total.astype(BF)  27.7 us
    all_to_all x3, waiting for transfers between devices, to_row(): moved = lax.all_to_all(tokens, ('yy', 'head'), 0, 0, tiled=True)  20.4 us
  transfers between devices with their start and end apart: 87, of which 33 were waited for; matrix products, arithmetic and copies ran while one was open for 29% of the time, Pallas kernels for 12%

profile of v7, /device:TPU:1, one launch (start us, length us, event | category | flops | bytes accessed | tf_op | source)
XLA Modules:
  0.0 611.6 jit_solution(11090933368773588479)
XLA Ops:
  17.7 13.0 %collective-permute-done.1 = bf16[96,1024]{1,0:T(8,128)(2,1)S(1)} collective-permute-done((bf16[96,1024]{1,0:T(8,128)(2,1)S(1)}, bf16[96,1024]{1,0:T(8,128)(2,1)S(1)}, u32[]{:S(2)}, u32[]{:S(2)}) %collective-permute-start.1) | collective-permute-done | bytes 196640 | tf_op jit(solution)/shard_map/ppermute | solution.py:92
  31.5 4.7 all-to-all-start
  54.4 7.8 %collective-permute-done.4 = bf16[2,96,1024]{2,1,0:T(8,128)(2,1)} collective-permute-done((bf16[2,96,1024]{2,1,0:T(8,128)(2,1)}, bf16[2,96,1024]{2,1,0:T(8,128)(2,1)}, u32[]{:S(2)}, u32[]{:S(2)}) %collective-permute-start.4) | collective-permute-done | bytes 393248 | tf_op jit(solution)/shard_map/ppermute | solution.py:92
  77.9 13.8 %collective-permute-done.7 = bf16[2,2,96,1024]{3,2,1,0:T(8,128)(2,1)} collective-permute-done((bf16[2,2,96,1024]{3,2,1,0:T(8,128)(2,1)}, bf16[2,2,96,1024]{3,2,1,0:T(8,128)(2,1)}, u32[]{:S(2)}, u32[]{:S(2)}) %collective-permute-start.7) | collective-permute-done | bytes 786464 | tf_op jit(solution)/shard_map/ppermute | solution.py:92
  91.7 7.0 %convolution_convert_fusion.1.refs_0_ = bf16[1536,1024]{1,0:T(8,128)(2,1)} fusion(bf16[1024,1024]{1,0:T(8,128)(2,1)S(1)} %pad_maximum_fusion.3, bf16[384,1024]{1,0:T(8,128)(2,1)} %bitcast.24, bf16[384,1024]{1,0:T(8,128)(2,1)} %bitcast.23, bf16[384,1024]{1,0:T(8,128)(2,1)} %bitcast.22, bf16[384,1024]{1,0:T(8,128)(2,1)} %bitcast.18), kind=kOutput, calls=%fused_computation.8 | convolution fusion | flops 3235381248 | bytes 8388608 | tf_op jit(solution)/shard_map/dot_general | solution.py:25
  98.7 4.6 collective-permute-done.9
  112.9 4.3 all-to-all-start.1
  127.1 11.7 %shard_map.298 = (bf16[512,1024]{1,0:T(8,128)(2,1)S(1)}, f32[2,4,1,1024]{3,2,1,0:T(1,128)S(1)}) custom-call(s32[16]{0:T(128)S(1)} %select_n.214.need_ref, s32[4]{0:T(128)S(1)} %get-tuple-element.400.base_ref, s32[2,1024]{1,0:T(2,128)S(1)} %pad_add_fusion.1.span_ref, bf16[1536,1024]{1,0:T(8,128)(2,1)S(1)} %copy-done.39), custom_call_target="tpu_custom_call" | custom-call | flops 40000000000 | bytes 8388608 | tf_op jit(solution)/shard_map/pallas_call | solution.py:465
  143.2 14.4 %all-to-all-done.1 = bf16[8,64,1024]{2,1,0:T(8,128)(2,1)} async-done(((bf16[8,64,1024]{2,1,0:T(8,128)(2,1)}), bf16[8,64,1024]{2,1,0:T(8,128)(2,1)}, u32[]{:S(2)}, u32[]{:S(2)}) %all-to-all-start.1) | async-done | bytes 1048608 | tf_op jit(solution)/shard_map/all_to_all | solution.py:116
  164.7 6.6 %collective-permute-start.18 = (bf16[512,1024]{1,0:T(8,128)(2,1)S(1)}, bf16[512,1024]{1,0:T(8,128)(2,1)S(1)}, u32[]{:S(2)}, u32[]{:S(2)}) collective-permute-start(bf16[512,1024]{1,0:T(8,128)(2,1)S(1)} %convolution_convert_fusion.15), channel_id=1, source_target_pairs={{0,4},{4,0},{1,5},{5,1},{2,6},{6,2},{3,7},{7,3},{8,12},{12,8},{9,1... | collective-permute-start | bytes 3145736 | tf_op jit(solution)/shard_map/ppermute | solution.py:92
  191.9 5.1 collective-permute-start.24
  224.1 12.9 %shard_map.300 = (bf16[512,1024]{1,0:T(8,128)(2,1)S(1)}, f32[2,4,1,1024]{3,2,1,0:T(1,128)S(1)}) custom-call(s32[16]{0:T(128)S(1)} %select_n.206.need_ref, s32[4]{0:T(128)S(1)} %get-tuple-element.400.base_ref, s32[2,1024]{1,0:T(2,128)S(1)} %pad_add_fusion.span_ref, bf16[512,1024]{1,0:T(8,128)(2,1)S(1)} %copy-done.31, bf16[1024,1024]{1,0:T(8,128)(2,1)S(1)} %copy-done.37), custom_call_target="tpu_custom_call" | custom-call | flops 40000000000 | bytes 8388608 | tf_op jit(solution)/shard_map/pallas_call | solution.py:465
  241.0 6.0 all-to-all-done.2
  259.8 14.1 %add_convert_fusion = (bf16[2048,1024]{1,0:T(8,128)(2,1)}, bf16[2048,1024]{1,0:T(8,128)(2,1)}) fusion(bf16[1024,1024]{1,0:T(8,128)(2,1)S(1)} %constant_dynamic-update-slice_fusion.4, bf16[512,1024]{1,0:T(8,128)(2,1)} %bitcast.73, bf16[512,1024]{1,0:T(8,128)(2,1)} %bitcast.72, bf16[512,1024]{1,0:T(8,128)(2,1)} %bitcast.71, bf16[512,1024]{1,0:T(8,128)(2,1)} %bitcast.70), kind=kOutput, calls=%fused_computation.1 | convolution fusion | flops 4349493248 | bytes 14680064 | tf_op jit(solution)/shard_map/dot_general | solution.py:25
  273.9 6.9 %convolution_convert_fusion.3 = bf16[2048,1024]{1,0:T(8,128)(2,1)S(1)} fusion(bf16[2048,1024]{1,0:T(8,128)(2,1)} %get-tuple-element.233, bf16[1024,1024]{1,0:T(8,128)(2,1)S(1)} %constant_dynamic-update-slice_fusion.6), kind=kOutput, calls=%fused_computation.10 | convolution fusion | flops 4297064448 | bytes 10485760 | tf_op jit(solution)/shard_map/dot_general | solution.py:25
  288.2 12.0 %multiply_convert_fusion = bf16[2048,1024]{1,0:T(8,128)(2,1)} fusion(bf16[2048,1024]{1,0:T(8,128)(2,1)} %get-tuple-element.216, bf16[1024,1024]{1,0:T(8,128)(2,1)S(1)} %constant_dynamic-update-slice_fusion.6, bf16[512,1024]{1,0:T(8,128)(2,1)S(1)} %bitcast.380, bf16[512,1024]{1,0:T(8,128)(2,1)S(1)} %bitcast.285, bf16[512,1024]{1,0:T(8,128)(2,1)S(1)} %bitcast.383, ...), kind=kOutput, calls=%fused_computation | convolution fusion | flops 4318035968 | bytes 14680064 | tf_op jit(solution)/shard_map/dot_general | solution.py:25
  303.7 4.2 all-to-all-start.3
  317.5 4.5 fusion.15
  330.4 4.7 convolution_convert_fusion.2
  345.0 17.2 %shard_map.303 = (bf16[512,1024]{1,0:T(8,128)(2,1)S(1)}, bf16[1024,1024]{1,0:T(8,128)(2,1)S(1)}) custom-call(s32[16]{0:T(128)S(1)} %select_n.206.need_ref, s32[4]{0:T(128)S(1)} %get-tuple-element.400.base_ref, s32[2,1024]{1,0:T(2,128)S(1)} %pad_add_fusion.span_ref, bf16[512,1024]{1,0:T(8,128)(2,1)S(1)} %copy-done.32, bf16[1024,1024]{1,0:T(8,128)(2,1)S(1)} %copy-done.38, ...), custom_call_target="tpu_custom_call" | custom-call | flops 46000001024 | bytes 8388608 | tf_op jit(solution)/shard_map/pallas_call | solution.py:465
  384.1 11.4 %collective-permute-start.49 = (bf16[2,128,1024]{2,1,0:T(8,128)(2,1)}, bf16[2,128,1024]{2,1,0:T(8,128)(2,1)}, u32[]{:S(2)}, u32[]{:S(2)}) collective-permute-start(bf16[2,128,1024]{2,1,0:T(8,128)(2,1)} %slice_bitcast_fusion.8), channel_id=1, source_target_pairs={{0,8},{8,0},{1,9},{9,1},{2,10},{10,2},{3,11},{11,3},{4,12},{12,4},... | collective-permute-start | bytes 1572872 | tf_op jit(solution)/shard_map/ppermute | solution.py:92
  430.1 4.3 all-to-all-start.4
  441.0 15.3 %shard_map.305 = bf16[1536,1024]{1,0:T(8,128)(2,1)S(1)} custom-call(s32[16]{0:T(128)S(1)} %copy-done.25, s32[4]{0:T(128)S(1)} %get-tuple-element.400.base_ref, s32[2,1024]{1,0:T(2,128)S(1)} %copy-done.23, bf16[1536,1024]{1,0:T(8,128)(2,1)S(1)} %copy-done.40, bf16[512,1024]{1,0:T(8,128)(2,1)S(1)} %copy-done.28, bf16[512,1024]{1,0:T(8,128)(2,1)S(1)} %copy-done.33, ...), custom_call_target="tpu_custom_call" | custom-call | flops 46000001024 | bytes 8388608 | tf_op jit(solution)/shard_map/pallas_call | solution.py:465
  457.2 7.8 %collective-permute-done.55 = bf16[2,128,1024]{2,1,0:T(8,128)(2,1)S(1)} collective-permute-done((bf16[2,128,1024]{2,1,0:T(8,128)(2,1)S(1)}, bf16[2,128,1024]{2,1,0:T(8,128)(2,1)S(1)}, u32[]{:S(2)}, u32[]{:S(2)}) %collective-permute-start.55) | collective-permute-done | bytes 524320 | tf_op jit(solution)/shard_map/ppermute | solution.py:92
  473.3 4.5 collective-permute-start.59
  486.1 5.0 fusion.10.own_ref
  499.0 5.0 collective-permute-done.63
  520.4 9.7 %collective-permute-done.66 = bf16[2,128,1024]{2,1,0:T(8,128)(2,1)} collective-permute-done((bf16[2,128,1024]{2,1,0:T(8,128)(2,1)}, bf16[2,128,1024]{2,1,0:T(8,128)(2,1)}, u32[]{:S(2)}, u32[]{:S(2)}) %collective-permute-start.66) | collective-permute-done | bytes 524320 | tf_op jit(solution)/shard_map/ppermute | solution.py:92
  535.2 7.5 %collective-permute-start.67 = (bf16[128,1024]{1,0:T(8,128)(2,1)S(1)}, bf16[128,1024]{1,0:T(8,128)(2,1)S(1)}, u32[]{:S(2)}, u32[]{:S(2)}) collective-permute-start(bf16[128,1024]{1,0:T(8,128)(2,1)S(1)} %slice_bitcast_fusion.18), channel_id=1, source_target_pairs={{0,3},{1,0},{2,1},{3,2},{4,7},{5,4},{6,5},{7,6},{8,11},{9,8},{10,9... | collective-permute-start | bytes 786440 | tf_op jit(solution)/shard_map/ppermute | solution.py:92
  554.0 9.9 %collective-permute-done.68 = bf16[128,1024]{1,0:T(8,128)(2,1)S(1)} collective-permute-done((bf16[128,1024]{1,0:T(8,128)(2,1)S(1)}, bf16[128,1024]{1,0:T(8,128)(2,1)S(1)}, u32[]{:S(2)}, u32[]{:S(2)}) %collective-permute-start.68) | collective-permute-done | bytes 262176 | tf_op jit(solution)/shard_map/ppermute | solution.py:92
  569.4 12.0 %collective-permute-start.74 = (bf16[2,128,1024]{2,1,0:T(8,128)(2,1)S(1)}, bf16[2,128,1024]{2,1,0:T(8,128)(2,1)S(1)}, u32[]{:S(2)}, u32[]{:S(2)}) collective-permute-start(bf16[2,128,1024]{2,1,0:T(8,128)(2,1)S(1)} %pad_maximum_fusion.28), channel_id=1, source_target_pairs={{0,16},{16,0},{1,17},{17,1},{2,18},{18,2},{3,19},{19,3},{4,20},{20... | collective-permute-start | bytes 1572872 | tf_op jit(solution)/shard_map/ppermute | solution.py:92
  587.7 4.6 collective-permute-done.74
  (560 shorter events, 323.3 us)
Async XLA Ops:
  31.5 30.7 %all-to-all-start = ((bf16[8,64,1024]{2,1,0:T(8,128)(2,1)}), bf16[8,64,1024]{2,1,0:T(8,128)(2,1)S(1)}, u32[]{:S(2)}, u32[]{:S(2)}) async-start(bf16[8,64,1024]{2,1,0:T(8,128)(2,1)} %param.18), calls=%async_computation | async-start | bytes 2097152 | tf_op jit(solution)/shard_map/all_to_all | solution.py:116
  74.7 28.5 %collective-permute-start.9 = (bf16[160,1024]{1,0:T(8,128)(2,1)S(1)}, bf16[160,1024]{1,0:T(8,128)(2,1)S(1)}, u32[]{:S(2)}, u32[]{:S(2)}) collective-permute-start(bf16[160,1024]{1,0:T(8,128)(2,1)S(1)} %copy-done.84), channel_id=1, source_target_pairs={{0,2},{1,3},{2,0},{3,1},{4,6},{5,7},{6,4},{7,5},{8,10},{9,11},{10,... | collective-permute-start | bytes 983048 | tf_op jit(solution)/shard_map/ppermute | solution.py:92
  74.9 28.3 %collective-permute-start.8 = (bf16[160,1024]{1,0:T(8,128)(2,1)S(1)}, bf16[160,1024]{1,0:T(8,128)(2,1)S(1)}, u32[]{:S(2)}, u32[]{:S(2)}) collective-permute-start(bf16[160,1024]{1,0:T(8,128)(2,1)S(1)} %copy-done.84), channel_id=1, source_target_pairs={{0,1},{1,2},{2,3},{3,0},{4,5},{5,6},{6,7},{7,4},{8,9},{9,10},{10,1... | collective-permute-start | bytes 983048 | tf_op jit(solution)/shard_map/ppermute | solution.py:92
  108.5 34.7 %collective-permute-start.17 = (bf16[128,1024]{1,0:T(8,128)(2,1)S(1)}, bf16[128,1024]{1,0:T(8,128)(2,1)}, u32[]{:S(2)}, u32[]{:S(2)}) collective-permute-start(bf16[128,1024]{1,0:T(8,128)(2,1)S(1)} %bitcast.288), channel_id=1, source_target_pairs={{0,3},{1,0},{2,1},{3,2},{4,7},{5,4},{6,5},{7,6},{8,11},{9,8},{10,9... | collective-permute-start | bytes 786440 | tf_op jit(solution)/shard_map/ppermute | solution.py:92
  108.6 34.6 %collective-permute-start.16 = (bf16[128,1024]{1,0:T(8,128)(2,1)S(1)}, bf16[128,1024]{1,0:T(8,128)(2,1)}, u32[]{:S(2)}, u32[]{:S(2)}) collective-permute-start(bf16[128,1024]{1,0:T(8,128)(2,1)S(1)} %bitcast.289), channel_id=1, source_target_pairs={{0,2},{1,3},{2,0},{3,1},{4,6},{5,7},{6,4},{7,5},{8,10},{9,11},{10,... | collective-permute-start | bytes 786440 | tf_op jit(solution)/shard_map/ppermute | solution.py:92
  111.5 31.7 %collective-permute-start.15 = (bf16[128,1024]{1,0:T(8,128)(2,1)S(1)}, bf16[128,1024]{1,0:T(8,128)(2,1)}, u32[]{:S(2)}, u32[]{:S(2)}) collective-permute-start(bf16[128,1024]{1,0:T(8,128)(2,1)S(1)} %bitcast.290), channel_id=1, source_target_pairs={{0,1},{1,2},{2,3},{3,0},{4,5},{5,6},{6,7},{7,4},{8,9},{9,10},{10,1... | collective-permute-start | bytes 786440 | tf_op jit(solution)/shard_map/ppermute | solution.py:92
  112.9 44.8 %all-to-all-start.1 = ((bf16[8,64,1024]{2,1,0:T(8,128)(2,1)}), bf16[8,64,1024]{2,1,0:T(8,128)(2,1)}, u32[]{:S(2)}, u32[]{:S(2)}) async-start(bf16[8,64,1024]{2,1,0:T(8,128)(2,1)} %param.19), calls=%async_computation.1 | async-start | bytes 2097152 | tf_op jit(solution)/shard_map/all_to_all | solution.py:116
  123.4 34.3 %collective-permute-start.14 = (bf16[2,2,160,1024]{3,2,1,0:T(8,128)(2,1)}, bf16[2,2,160,1024]{3,2,1,0:T(8,128)(2,1)}, u32[]{:S(2)}, u32[]{:S(2)}) collective-permute-start(bf16[2,2,160,1024]{3,2,1,0:T(8,128)(2,1)} %pad_maximum_fusion.7), channel_id=1, source_target_pairs={{0,16},{16,0},{1,17},{17,1},{2,18},{18,2},{3,19},{19,3},{4,20},{20... | collective-permute-start | bytes 3932168 | tf_op jit(solution)/shard_map/ppermute | solution.py:92
  126.5 31.2 %collective-permute-start.13 = (bf16[2,2,160,1024]{3,2,1,0:T(8,128)(2,1)}, bf16[2,2,160,1024]{3,2,1,0:T(8,128)(2,1)}, u32[]{:S(2)}, u32[]{:S(2)}) collective-permute-start(bf16[2,2,160,1024]{3,2,1,0:T(8,128)(2,1)} %pad_maximum_fusion.6), channel_id=1, source_target_pairs={{0,8},{8,0},{1,9},{9,1},{2,10},{10,2},{3,11},{11,3},{4,12},{12,4},... | collective-permute-start | bytes 3932168 | tf_op jit(solution)/shard_map/ppermute | solution.py:92
  199.4 37.6 %collective-permute-start.27 = (bf16[2,2,128,1024]{3,2,1,0:T(8,128)(2,1)}, bf16[2,2,128,1024]{3,2,1,0:T(8,128)(2,1)}, u32[]{:S(2)}, u32[]{:S(2)}) collective-permute-start(bf16[2,2,128,1024]{3,2,1,0:T(8,128)(2,1)} %pad_maximum_fusion.11), channel_id=1, source_target_pairs={{0,16},{16,0},{1,17},{17,1},{2,18},{18,2},{3,19},{19,3},{4,20},{20... | collective-permute-start | bytes 3145736 | tf_op jit(solution)/shard_map/ppermute | solution.py:92
  201.8 35.2 %collective-permute-start.26 = (bf16[2,2,128,1024]{3,2,1,0:T(8,128)(2,1)}, bf16[2,2,128,1024]{3,2,1,0:T(8,128)(2,1)}, u32[]{:S(2)}, u32[]{:S(2)}) collective-permute-start(bf16[2,2,128,1024]{3,2,1,0:T(8,128)(2,1)} %pad_maximum_fusion.10), channel_id=1, source_target_pairs={{0,8},{8,0},{1,9},{9,1},{2,10},{10,2},{3,11},{11,3},{4,12},{12,4},... | collective-permute-start | bytes 3145736 | tf_op jit(solution)/shard_map/ppermute | solution.py:92
  217.7 29.3 %all-to-all-start.2 = ((bf16[8,64,1024]{2,1,0:T(8,128)(2,1)}), bf16[8,64,1024]{2,1,0:T(8,128)(2,1)S(1)}, u32[]{:S(2)}, u32[]{:S(2)}) async-start(bf16[8,64,1024]{2,1,0:T(8,128)(2,1)} %param.20), calls=%async_computation.2 | async-start | bytes 2097152 | tf_op jit(solution)/shard_map/all_to_all | solution.py:116
  257.5 25.1 %collective-permute-start.34 = (bf16[2,2,128,1024]{3,2,1,0:T(8,128)(2,1)S(1)}, bf16[2,2,128,1024]{3,2,1,0:T(8,128)(2,1)S(1)}, u32[]{:S(2)}, u32[]{:S(2)}) collective-permute-start(bf16[2,2,128,1024]{3,2,1,0:T(8,128)(2,1)S(1)} %pad_maximum_fusion.13), channel_id=1, source_target_pairs={{0,16},{16,0},{1,17},{17,1},{2,18},{18,2},{3,19},{19,3},{4,20},{20... | collective-permute-start | bytes 3145736 | tf_op jit(solution)/shard_map/ppermute | solution.py:92
  303.7 60.8 %all-to-all-start.3 = ((bf16[8,64,1024]{2,1,0:T(8,128)(2,1)}), bf16[8,64,1024]{2,1,0:T(8,128)(2,1)}, u32[]{:S(2)}, u32[]{:S(2)}) async-start(bf16[8,64,1024]{2,1,0:T(8,128)(2,1)} %bitcast.280), calls=%async_computation.3 | async-start | bytes 2097152 | tf_op jit(solution)/shard_map/all_to_all | solution.py:122
  307.9 241.8 %all-gather.4.cloned.1.call-start = ((), (), s32[]{:S(2)}) async-start(), calls=%async_computation.6 | async-start | bytes 2359296 | tf_op jit(solution)/shard_map/all_gather | solution.py:225
  336.6 27.9 %collective-permute-start.42 = (bf16[2,2,128,1024]{3,2,1,0:T(8,128)(2,1)S(1)}, bf16[2,2,128,1024]{3,2,1,0:T(8,128)(2,1)}, u32[]{:S(2)}, u32[]{:S(2)}) collective-permute-start(bf16[2,2,128,1024]{3,2,1,0:T(8,128)(2,1)S(1)} %bitcast.299), channel_id=1, source_target_pairs={{0,8},{8,0},{1,9},{9,1},{2,10},{10,2},{3,11},{11,3},{4,12},{12,4},... | collective-permute-start | bytes 3145736 | tf_op jit(solution)/shard_map/ppermute | solution.py:92
  337.3 27.2 %collective-permute-start.43 = (bf16[2,2,128,1024]{3,2,1,0:T(8,128)(2,1)S(1)}, bf16[2,2,128,1024]{3,2,1,0:T(8,128)(2,1)}, u32[]{:S(2)}, u32[]{:S(2)}) collective-permute-start(bf16[2,2,128,1024]{3,2,1,0:T(8,128)(2,1)S(1)} %bitcast.298), channel_id=1, source_target_pairs={{0,16},{16,0},{1,17},{17,1},{2,18},{18,2},{3,19},{19,3},{4,20},{20... | collective-permute-start | bytes 3145736 | tf_op jit(solution)/shard_map/ppermute | solution.py:92
  384.1 25.1 %collective-permute-start.49 = (bf16[2,128,1024]{2,1,0:T(8,128)(2,1)}, bf16[2,128,1024]{2,1,0:T(8,128)(2,1)}, u32[]{:S(2)}, u32[]{:S(2)}) collective-permute-start(bf16[2,128,1024]{2,1,0:T(8,128)(2,1)} %slice_bitcast_fusion.8), channel_id=1, source_target_pairs={{0,8},{8,0},{1,9},{9,1},{2,10},{10,2},{3,11},{11,3},{4,12},{12,4},... | collective-permute-start | bytes 1572872 | tf_op jit(solution)/shard_map/ppermute | solution.py:92
  398.9 30.3 %collective-permute-start.52 = (bf16[2,2,128,1024]{3,2,1,0:T(8,128)(2,1)}, bf16[2,2,128,1024]{3,2,1,0:T(8,128)(2,1)}, u32[]{:S(2)}, u32[]{:S(2)}) collective-permute-start(bf16[2,2,128,1024]{3,2,1,0:T(8,128)(2,1)} %pad_maximum_fusion.15), channel_id=1, source_target_pairs={{0,8},{8,0},{1,9},{9,1},{2,10},{10,2},{3,11},{11,3},{4,12},{12,4},... | collective-permute-start | bytes 3145736 | tf_op jit(solution)/shard_map/ppermute | solution.py:92
  404.1 26.0 %collective-permute-start.53 = (bf16[2,2,128,1024]{3,2,1,0:T(8,128)(2,1)S(1)}, bf16[2,2,128,1024]{3,2,1,0:T(8,128)(2,1)}, u32[]{:S(2)}, u32[]{:S(2)}) collective-permute-start(bf16[2,2,128,1024]{3,2,1,0:T(8,128)(2,1)S(1)} %pad_maximum_fusion.16), channel_id=1, source_target_pairs={{0,16},{16,0},{1,17},{17,1},{2,18},{18,2},{3,19},{19,3},{4,20},{20... | collective-permute-start | bytes 3145736 | tf_op jit(solution)/shard_map/ppermute | solution.py:92
  411.3 45.9 %collective-permute-start.56 = (bf16[128,1024]{1,0:T(8,128)(2,1)}, bf16[128,1024]{1,0:T(8,128)(2,1)}, u32[]{:S(2)}, u32[]{:S(2)}) collective-permute-start(bf16[128,1024]{1,0:T(8,128)(2,1)} %slice_bitcast_fusion.26), channel_id=1, source_target_pairs={{0,3},{1,0},{2,1},{3,2},{4,7},{5,4},{6,5},{7,6},{8,11},{9,8},{10,9... | collective-permute-start | bytes 786440 | tf_op jit(solution)/shard_map/ppermute | solution.py:92
  416.4 40.8 %collective-permute-start.58 = (bf16[128,1024]{1,0:T(8,128)(2,1)}, bf16[128,1024]{1,0:T(8,128)(2,1)}, u32[]{:S(2)}, u32[]{:S(2)}) collective-permute-start(bf16[128,1024]{1,0:T(8,128)(2,1)} %get-tuple-element.378), channel_id=1, source_target_pairs={{0,1},{1,2},{2,3},{3,0},{4,5},{5,6},{6,7},{7,4},{8,9},{9,10},{10,1... | collective-permute-start | bytes 786440 | tf_op jit(solution)/shard_map/ppermute | solution.py:92
  422.1 35.1 %collective-permute-start.57 = (bf16[128,1024]{1,0:T(8,128)(2,1)}, bf16[128,1024]{1,0:T(8,128)(2,1)}, u32[]{:S(2)}, u32[]{:S(2)}) collective-permute-start(bf16[128,1024]{1,0:T(8,128)(2,1)} %get-tuple-element.379), channel_id=1, source_target_pairs={{0,2},{1,3},{2,0},{3,1},{4,6},{5,7},{6,4},{7,5},{8,10},{9,11},{10,... | collective-permute-start | bytes 786440 | tf_op jit(solution)/shard_map/ppermute | solution.py:92
  430.1 63.0 %all-to-all-start.4 = ((bf16[8,64,1024]{2,1,0:T(8,128)(2,1)}), bf16[8,64,1024]{2,1,0:T(8,128)(2,1)}, u32[]{:S(2)}, u32[]{:S(2)}) async-start(bf16[8,64,1024]{2,1,0:T(8,128)(2,1)} %bitcast.279), calls=%async_computation.4 | async-start | bytes 2097152 | tf_op jit(solution)/shard_map/all_to_all | solution.py:122
  434.4 129.9 %all-gather.6.cloned.1.call-start = ((), (), s32[]{:S(2)}) async-start(), calls=%async_computation.7 | async-start | bytes 2359296 | tf_op jit(solution)/shard_map/all_gather | solution.py:225
  438.5 26.5 %collective-permute-start.55 = (bf16[2,128,1024]{2,1,0:T(8,128)(2,1)S(1)}, bf16[2,128,1024]{2,1,0:T(8,128)(2,1)S(1)}, u32[]{:S(2)}, u32[]{:S(2)}) collective-permute-start(bf16[2,128,1024]{2,1,0:T(8,128)(2,1)S(1)} %slice_bitcast_fusion.4), channel_id=1, source_target_pairs={{0,8},{8,0},{1,9},{9,1},{2,10},{10,2},{3,11},{11,3},{4,12},{12,4},... | collective-permute-start | bytes 1572872 | tf_op jit(solution)/shard_map/ppermute | solution.py:92
  439.9 25.1 %collective-permute-start.54 = (bf16[2,128,1024]{2,1,0:T(8,128)(2,1)S(1)}, bf16[2,128,1024]{2,1,0:T(8,128)(2,1)S(1)}, u32[]{:S(2)}, u32[]{:S(2)}) collective-permute-start(bf16[2,128,1024]{2,1,0:T(8,128)(2,1)S(1)} %slice_bitcast_fusion.5), channel_id=1, source_target_pairs={{0,16},{16,0},{1,17},{17,1},{2,18},{18,2},{3,19},{19,3},{4,20},{20... | collective-permute-start | bytes 1572872 | tf_op jit(solution)/shard_map/ppermute | solution.py:92
  469.6 29.4 %collective-permute-start.62 = (bf16[128,1024]{1,0:T(8,128)(2,1)}, bf16[128,1024]{1,0:T(8,128)(2,1)}, u32[]{:S(2)}, u32[]{:S(2)}) collective-permute-start(bf16[128,1024]{1,0:T(8,128)(2,1)} %slice_bitcast_fusion.23), channel_id=1, source_target_pairs={{0,3},{1,0},{2,1},{3,2},{4,7},{5,4},{6,5},{7,6},{8,11},{9,8},{10,9... | collective-permute-start | bytes 786440 | tf_op jit(solution)/shard_map/ppermute | solution.py:92
  480.4 25.1 %collective-permute-start.60 = (bf16[2,2,128,1024]{3,2,1,0:T(8,128)(2,1)}, bf16[2,2,128,1024]{3,2,1,0:T(8,128)(2,1)}, u32[]{:S(2)}, u32[]{:S(2)}) collective-permute-start(bf16[2,2,128,1024]{3,2,1,0:T(8,128)(2,1)} %pad_maximum_fusion.17), channel_id=1, source_target_pairs={{0,8},{8,0},{1,9},{9,1},{2,10},{10,2},{3,11},{11,3},{4,12},{12,4},... | collective-permute-start | bytes 3145736 | tf_op jit(solution)/shard_map/ppermute | solution.py:92
  513.0 30.0 %collective-permute-start.70 = (f32[3,1024]{1,0:T(4,128)S(1)}, f32[3,1024]{1,0:T(4,128)S(1)}, u32[]{:S(2)}, u32[]{:S(2)}) collective-permute-start(f32[3,1024]{1,0:T(4,128)S(1)} %pad_maximum_fusion.32), channel_id=1, source_target_pairs={{0,4},{4,0},{1,5},{5,1},{2,6},{6,2},{3,7},{7,3},{8,12},{12,8},{9,1... | collective-permute-start | bytes 36872 | tf_op jit(solution)/shard_map/ppermute | solution.py:276
  514.8 69.5 %all-to-all-start.5 = ((bf16[8,64,1024]{2,1,0:T(8,128)(2,1)}), bf16[8,64,1024]{2,1,0:T(8,128)(2,1)S(1)}, u32[]{:S(2)}, u32[]{:S(2)}) async-start(bf16[8,64,1024]{2,1,0:T(8,128)(2,1)} %bitcast.144), calls=%async_computation.5 | async-start | bytes 2097152 | tf_op jit(solution)/shard_map/all_to_all | solution.py:122
  518.3 76.1 %all-gather.8.cloned.1.call-start = ((), (), s32[]{:S(2)}) async-start(), calls=%async_computation.8 | async-start | bytes 2359296 | tf_op jit(solution)/shard_map/all_gather | solution.py:225
  (171 other events, 1639.0 us)
Sparse Core Ops, SparseCore 0:
  430.3 41.0 all-gather.3
  506.5 38.5 all-gather.5
  547.5 32.1 all-gather.7
